TPU v7x, 256 devices: a whole 4x4x8 slice. The times are simulated.
256 devices in a mesh: dp: 4 (over y), ctx: 64 (over z, x, core).
Axes of the slice: x: 4, y: 4, z: 8, core: 2. Of those that a mesh axis runs over, the one named last changes fastest.
Arguments:
- out_grad: float32 [4, 16, 131072], P('dp', None, 'ctx'), may hold values from -6 to 6
- conv_input: float32 [4, 16, 131072], P('dp', None, 'ctx'), may hold values from -0.001953125 to 0.001953125
- filter_taps: float32 [131072], P('ctx'), may hold values from -0.015625 to 0.015625
- skip_gain: float32 [16], replicated, may hold values from 0.5 to 2
Outputs:
- input_grad: float32 [4, 16, 131072], P('dp', None, 'ctx')
- filter_grad: float32 [131072], P('ctx')
All inputs are finite; a program needn't handle non-finite values.
Results may differ from a plain program's by a relative error of at most 0.00012.
Values sent between devices are 32-bit elements; how exact they have to be, the bound alone decides.
No kernel may reach another device: no remote copies, remote signals or barrier semaphores. Data moves between devices by JAX's collectives and lax.ppermute only.
A program may use at most 64 MiB of HBM per device.

v0:
```python
import functools

import jax
import jax.numpy as jnp
import ml_dtypes
import numpy as np
from jax import lax
from jax.experimental import pallas as pl
from jax.experimental.pallas import tpu as pltpu
from jax.sharding import Mesh, PartitionSpec as P

Y, Z, X, C = 4, 8, 4, 2
ROWS_IN, ROWS_OUT = 5, 3
SUB, LANES = 16, 128
POINTS = 128
SCALE = 1.0 / 131072.0


def class_of(x, c):
    return 2 * x + c


def z_tables():
    out = np.zeros((X * C, 2, X, 2, Z))
    z = np.arange(Z)
    for x in range(X):
        for c in range(C):
            for other in range(2):
                for shift in range(X):
                    k = class_of((x + shift) % X, c ^ other) + 0.5
                    angle = 2.0 * np.pi * z * k / 16.0
                    out[class_of(x, c), other, shift, 0] = np.cos(angle)
                    out[class_of(x, c), other, shift, 1] = -np.sin(angle)
    return out.reshape(X * C, -1).astype(np.float32)


def numpy_split(table):
    table = table.astype(np.float32)
    high = table.astype(ml_dtypes.bfloat16)
    low = (table - high.astype(np.float32)).astype(ml_dtypes.bfloat16)
    return high, low


def left_tables():
    out = np.zeros((X * C, 2, POINTS, X, C, 2, SUB))
    alpha = np.arange(POINTS)[:, None]
    for x in range(X):
        for c in range(C):
            k = class_of(x, c) + 0.5
            for shift in range(X):
                for other in range(C):
                    p = class_of((x - shift) % X, c ^ other)
                    a = p * SUB + np.arange(SUB)[None, :]
                    angle = -2.0 * np.pi * ((a * alpha % POINTS) / POINTS + a * k / 2048.0)
                    at = out[class_of(x, c), :, :, shift, other]
                    at[0, :, 0], at[0, :, 1] = np.cos(angle), -np.sin(angle)
                    at[1, :, 0], at[1, :, 1] = np.sin(angle), np.cos(angle)
    return out.reshape(X * C, 2 * POINTS, 2 * POINTS)


def twiddle_tables():
    out = np.zeros((X * C, 2, POINTS, LANES))
    alpha, b = np.arange(POINTS)[:, None], np.arange(LANES)[None, :]
    for p in range(X * C):
        angle = -2.0 * np.pi * b * (alpha + (p + 0.5) / 16.0) / 16384.0
        out[p, 0], out[p, 1] = np.cos(angle), np.sin(angle)
    return out.astype(np.float32)


def right_table():
    b = np.arange(LANES)
    angle = -2.0 * np.pi * (b[:, None] * b[None, :] % LANES) / LANES
    cosine, sine = np.cos(angle), np.sin(angle)
    return np.block([[cosine, sine], [-sine, cosine]])


def z_forward_kernel(coef_ref, in_ref, keep_ref, send_ref):
    for row in range(ROWS_IN):
        blocks = [in_ref[z, row] for z in range(Z)]
        for half, out_ref in enumerate((keep_ref, send_ref)):
            for shift in range(X):
                for part in range(2):
                    base = ((half * X + shift) * 2 + part) * Z
                    total = coef_ref[base] * blocks[0]
                    for z in range(1, Z):
                        total = total + coef_ref[base + z] * blocks[z]
                    out_ref[shift, row, part] = total


def z_inverse_kernel(coef_ref, own_ref, other_ref, out_ref):
    for row in range(ROWS_OUT):
        totals = [None] * Z
        for half, in_ref in enumerate((own_ref, other_ref)):
            for shift in range(X):
                for part in range(2):
                    base = ((half * X + shift) * 2 + part) * Z
                    value = in_ref[shift, row, part]
                    for z in range(Z):
                        term = coef_ref[base + z] * value
                        totals[z] = term if totals[z] is None else totals[z] + term
        for z in range(Z):
            out_ref[z, row] = totals[z] * SCALE


def split(value):
    high = value.astype(jnp.bfloat16)
    return high, (value - high.astype(jnp.float32)).astype(jnp.bfloat16)


def product(left, right):
    (left_high, left_low), (right_high, right_low) = left, right
    dot = functools.partial(jnp.dot, preferred_element_type=jnp.float32)
    return dot(left_high, right_high) + (dot(left_high, right_low) + dot(left_low, right_high))


def spectral_kernel(
    x0, x1, x2, x3, wh, wl, wth, wtl, tw, bh, bl, bth, btl, o0, o1, o2, o3
):
    chunks, outs = (x0, x1, x2, x3), (o0, o1, o2, o3)
    pieces = [(s, c, part) for s in range(X) for c in range(C) for part in range(2)]
    columns = [
        jnp.concatenate([chunks[s][c, row, part] for s, c, part in pieces], axis=0)
        for row in range(ROWS_IN)
    ]
    value = product((wh[...], wl[...]), split(jnp.concatenate(columns, axis=1)))
    cosine, sine = tw[0], tw[1]
    rows = []
    for row in range(ROWS_IN):
        lanes = slice(row * LANES, (row + 1) * LANES)
        real, imag = value[:POINTS, lanes], value[POINTS:, lanes]
        rows.append(
            jnp.concatenate([real * cosine - imag * sine, real * sine + imag * cosine], axis=1)
        )
    value = product(split(jnp.concatenate(rows, axis=0)), (bh[...], bl[...]))
    real = [value[row * POINTS : (row + 1) * POINTS, :LANES] for row in range(ROWS_IN)]
    imag = [value[row * POINTS : (row + 1) * POINTS, LANES:] for row in range(ROWS_IN)]
    rows = []
    for channel in range(2):
        gr, gi = real[channel], imag[channel]
        rows.append(
            jnp.concatenate([real[4] * gr + imag[4] * gi, real[4] * gi - imag[4] * gr], axis=1)
        )
    dh_real, dh_imag = 0.0, 0.0
    for channel in range(2):
        gr, gi, ur, ui = real[channel], imag[channel], real[2 + channel], imag[2 + channel]
        dh_real = dh_real + (gr * ur + gi * ui)
        dh_imag = dh_imag + (gi * ur - gr * ui)
    rows.append(jnp.concatenate([dh_real, dh_imag], axis=1))
    value = product(split(jnp.concatenate(rows, axis=0)), (bth[...], btl[...]))
    columns = []
    for row in range(ROWS_OUT):
        vr = value[row * POINTS : (row + 1) * POINTS, :LANES]
        vi = value[row * POINTS : (row + 1) * POINTS, LANES:]
        columns.append(
            jnp.concatenate([vr * cosine + vi * sine, vi * cosine - vr * sine], axis=0)
        )
    value = product((wth[...], wtl[...]), split(jnp.concatenate(columns, axis=1)))
    for index, (s, c, part) in enumerate(pieces):
        for row in range(ROWS_OUT):
            outs[s][c, row, part] = value[
                index * SUB : (index + 1) * SUB, row * LANES : (row + 1) * LANES
            ]


VMEM = pl.BlockSpec(memory_space=pltpu.VMEM)
SMEM = pl.BlockSpec(memory_space=pltpu.SMEM)
PARAMS = pltpu.CompilerParams(vmem_limit_bytes=32 * 1024 * 1024)


def f32(*shape):
    return jax.ShapeDtypeStruct(shape, jnp.float32)


def shift_x(value, shift):
    return lax.ppermute(value, "x", [(i, (i + shift) % X) for i in range(X)])


def swap_core(value):
    return lax.ppermute(value, "c", [(0, 1), (1, 0)])


def pair_y(value, partner):
    return lax.ppermute(value, "y", [(i, partner(i)) for i in range(Y)])


def per_device(out_grad, conv_input, filter_taps, skip_gain):
    place = class_of(lax.axis_index("x"), lax.axis_index("c"))

    def mine(table):
        return lax.dynamic_index_in_dim(jnp.asarray(table), place, 0, keepdims=False)

    coef = mine(z_tables())
    left = left_tables()
    wh, wl = (mine(t) for t in numpy_split(left))
    wth, wtl = (mine(t) for t in numpy_split(np.swapaxes(left, 1, 2)))
    twiddle = mine(twiddle_tables())
    right = right_table()
    bh, bl = (jnp.asarray(t) for t in numpy_split(right))
    bth, btl = (jnp.asarray(t) for t in numpy_split(right.T))

    blocks = jnp.concatenate(
        [
            out_grad.reshape(Z, 2, SUB, LANES),
            conv_input.reshape(Z, 2, SUB, LANES),
            jnp.broadcast_to(filter_taps.reshape(1, 1, SUB, LANES), (Z, 1, SUB, LANES)),
        ],
        axis=1,
    )
    blocks = lax.all_to_all(blocks, "z", 0, 0, tiled=True)
    tile = (SUB, LANES)
    kept, sent = pl.pallas_call(
        z_forward_kernel,
        out_shape=[f32(X, ROWS_IN, 2, *tile)] * 2,
        in_specs=[SMEM, VMEM],
        out_specs=[VMEM] * 2,
        compiler_params=PARAMS,
    )(coef, blocks)
    crossed = swap_core(sent)
    chunks = [jnp.stack([kept[s], crossed[s]]) for s in range(X)]
    chunks = [chunks[0]] + [shift_x(chunks[s], s) for s in range(1, X)]
    chunks = pl.pallas_call(
        spectral_kernel,
        out_shape=[f32(C, ROWS_OUT, 2, *tile)] * X,
        in_specs=[VMEM] * 13,
        out_specs=[VMEM] * X,
        compiler_params=PARAMS,
    )(*chunks, wh, wl, wth, wtl, twiddle, bh, bl, bth, btl)
    chunks = [chunks[0]] + [shift_x(chunks[s], -s) for s in range(1, X)]
    own = jnp.stack([chunk[0] for chunk in chunks])
    other = swap_core(jnp.stack([chunk[1] for chunk in chunks]))
    blocks = pl.pallas_call(
        z_inverse_kernel,
        out_shape=f32(Z, ROWS_OUT, *tile),
        in_specs=[SMEM, VMEM, VMEM],
        out_specs=VMEM,
        compiler_params=PARAMS,
    )(coef, own, other)
    blocks = lax.all_to_all(blocks, "z", 0, 0, tiled=True)
    filter_grad = jnp.sum(blocks[:, 2], axis=0)
    near = pair_y(filter_grad, lambda i: i ^ 1)
    far = pair_y(filter_grad, lambda i: Y - 1 - i)
    across = pair_y(filter_grad, lambda i: i ^ 2)
    filter_grad = (filter_grad + near) + (far + across)
    input_grad = blocks[:, :2].reshape(out_grad.shape) + skip_gain[None, :, None] * out_grad
    return (input_grad, filter_grad.reshape(filter_taps.shape))


def solution(mesh):
    fine = Mesh(mesh.devices.reshape(Y, Z, X, C), ("y", "z", "x", "c"))
    return jax.shard_map(
        per_device,
        mesh=fine,
        in_specs=(P("y", None, ("z", "x", "c")), P("y", None, ("z", "x", "c")), P(("z", "x", "c")), P()),
        out_specs=(P("y", None, ("z", "x", "c")), P(("z", "x", "c"))),
        check_vma=False,
    )
```

profile of v0, /device:TPU:1, one launch (start us, length us, event | category | flops | bytes accessed | tf_op | source)
XLA Modules:
  0.0 74.9 jit_solution(689356479615326008)
XLA Ops:
  0.6 0.0 copy-start.4
  0.6 1.0 %copy.17 = f32[2,8,16,128]{3,2,1,0:T(8,128)S(1)} copy(f32[2,8,16,128]{3,1,2,0:T(8,128)} %bitcast.28) | data formatting | bytes 262144
  1.6 0.0 copy-done.4
  1.6 0.0 copy-start.5
  1.7 0.7 copy-done.5
  2.3 0.8 %pad_maximum_fusion = f32[8,5,16,128]{3,2,1,0:T(8,128)} fusion(f32[8,1,16,128]{3,2,1,0:T(8,128)S(1)} %broadcast_in_dim.9, f32[8,2,16,128]{3,2,1,0:T(8,128)S(1)} %bitcast.25, f32[8,2,16,128]{3,2,1,0:T(8,128)S(1)} %bitcast.26), kind=kLoop, calls=%fused_computation | loop fusion | flops 163840 | bytes 655360 | tf_op jit(solution)/shard_map/concatenate | solution.py:201
  3.1 9.0 %all-to-all-start = ((f32[8,5,16,128]{3,2,1,0:T(8,128)}), f32[8,5,16,128]{3,2,1,0:T(8,128)S(1)}, u32[]{:S(2)}, u32[]{:S(2)}) async-start(f32[8,5,16,128]{3,2,1,0:T(8,128)} %pad_maximum_fusion), calls=%async_computation | async-start | bytes 655360 | tf_op jit(solution)/shard_map/all_to_all | solution.py:209
  12.1 0.7 fusion.coef_ref
  12.8 1.0 %dynamic-slice_bitcast_fusion.3 = (bf16[256,256]{1,0:T(8,128)(2,1)S(1)}, bf16[256,256]{1,0:T(8,128)(2,1)S(1)}) fusion(bf16[8,256,256]{2,1,0:T(8,128)(2,1)} %constant.54.clone, s32[]{:T(128)S(6)} %select_n.11, bf16[8,256,256]{2,1,0:T(8,128)(2,1)} %constant.53.clone), kind=kLoop, calls=%fused_computation.11 | loop fusion | bytes 524292 | tf_op jit(solution)/shard_map/jit(dynamic_index_in_dim)/squeeze | solution.py:190
  13.8 10.2 %all-to-all-done.in_ref = f32[8,5,16,128]{3,2,1,0:T(8,128)S(1)} async-done(((f32[8,5,16,128]{3,2,1,0:T(8,128)}), f32[8,5,16,128]{3,2,1,0:T(8,128)S(1)}, u32[]{:S(2)}, u32[]{:S(2)}) %all-to-all-start) | async-done | bytes 327712 | tf_op jit(solution)/shard_map/all_to_all | solution.py:209
  24.0 0.9 %shard_map.149 = (f32[4,5,2,16,128]{4,3,2,1,0:T(8,128)S(1)}, f32[4,5,2,16,128]{4,3,2,1,0:T(8,128)S(1)}) custom-call(f32[128]{0:T(128)S(1)} %fusion.coef_ref, f32[8,5,16,128]{3,2,1,0:T(8,128)S(1)} %all-to-all-done.in_ref), custom_call_target="tpu_custom_call" | custom-call | tf_op jit(solution)/shard_map/pallas_call | solution.py:211
  25.0 2.4 %collective-permute-start = (f32[4,5,2,16,128]{4,3,2,1,0:T(8,128)S(1)}, f32[4,5,2,16,128]{4,3,2,1,0:T(8,128)S(1)}, u32[]{:S(2)}, u32[]{:S(2)}) collective-permute-start(f32[4,5,2,16,128]{4,3,2,1,0:T(8,128)S(1)} %get-tuple-element.9), channel_id=1, source_target_pairs={{0,1},{1,0},{2,3},{3,2},{4,5},{5,4},{6,7},{7,6},{8,9},{9,8},{10,11... | collective-permute-start | bytes 983048 | tf_op jit(solution)/shard_map/ppermute | solution.py:179
  27.4 1.0 %dynamic-slice_bitcast_fusion.1 = (bf16[256,256]{1,0:T(8,128)(2,1)S(1)}, bf16[256,256]{1,0:T(8,128)(2,1)S(1)}) fusion(bf16[8,256,256]{2,1,0:T(8,128)(2,1)} %constant.56.clone, s32[]{:T(128)S(6)} %select_n.11, bf16[8,256,256]{2,1,0:T(8,128)(2,1)} %constant.55.clone), kind=kLoop, calls=%fused_computation.9 | loop fusion | bytes 524292 | tf_op jit(solution)/shard_map/jit(dynamic_index_in_dim)/squeeze | solution.py:190
  28.4 0.2 collective-permute-done
  28.7 1.3 %collective-permute-start.1 = (f32[2,5,2,16,128]{4,3,2,1,0:T(8,128)S(1)}, f32[2,5,2,16,128]{4,3,2,1,0:T(8,128)S(1)}, u32[]{:S(2)}, u32[]{:S(2)}) collective-permute-start(f32[2,5,2,16,128]{4,3,2,1,0:T(8,128)S(1)} %pad_maximum_fusion.4), channel_id=1, source_target_pairs={{0,2},{2,4},{4,6},{6,0},{1,3},{3,5},{5,7},{7,1},{8,10},{10,12},{12... | collective-permute-start | bytes 491528 | tf_op jit(solution)/shard_map/ppermute | solution.py:175
  30.0 2.5 %collective-permute-start.2 = (f32[2,5,2,16,128]{4,3,2,1,0:T(8,128)S(1)}, f32[2,5,2,16,128]{4,3,2,1,0:T(8,128)S(1)}, u32[]{:S(2)}, u32[]{:S(2)}) collective-permute-start(f32[2,5,2,16,128]{4,3,2,1,0:T(8,128)S(1)} %pad_maximum_fusion.5), channel_id=1, source_target_pairs={{0,4},{2,6},{4,0},{6,2},{1,5},{3,7},{5,1},{7,3},{8,12},{10,14},{12... | collective-permute-start | bytes 491528 | tf_op jit(solution)/shard_map/ppermute | solution.py:175
  32.5 1.2 %collective-permute-start.3 = (f32[2,5,2,16,128]{4,3,2,1,0:T(8,128)S(1)}, f32[2,5,2,16,128]{4,3,2,1,0:T(8,128)S(1)}, u32[]{:S(2)}, u32[]{:S(2)}) collective-permute-start(f32[2,5,2,16,128]{4,3,2,1,0:T(8,128)S(1)} %pad_maximum_fusion.6), channel_id=1, source_target_pairs={{0,6},{2,0},{4,2},{6,4},{1,7},{3,1},{5,3},{7,5},{8,14},{10,8},{12,... | collective-permute-start | bytes 491528 | tf_op jit(solution)/shard_map/ppermute | solution.py:175
  33.8 0.0 copy-start.2
  33.8 0.0 copy-start.3
  33.8 1.0 %dynamic-slice_bitcast_fusion.tw = f32[2,128,128]{2,1,0:T(8,128)S(1)} fusion(f32[8,2,128,128]{3,2,1,0:T(8,128)} %constant.57.clone, s32[]{:T(128)S(6)} %select_n.11), kind=kLoop, calls=%fused_computation.8 | loop fusion | bytes 262148 | tf_op jit(solution)/shard_map/jit(dynamic_index_in_dim)/squeeze | solution.py:190
  34.7 0.0 copy-start
  34.7 0.0 copy-start.1
  34.8 0.6 collective-permute-done.1.x1
  35.4 4.5 %collective-permute-done.2.x2 = f32[2,5,2,16,128]{4,3,2,1,0:T(8,128)S(1)} collective-permute-done((f32[2,5,2,16,128]{4,3,2,1,0:T(8,128)S(1)}, f32[2,5,2,16,128]{4,3,2,1,0:T(8,128)S(1)}, u32[]{:S(2)}, u32[]{:S(2)}) %collective-permute-start.2) | collective-permute-done | bytes 163872 | tf_op jit(solution)/shard_map/ppermute | solution.py:175
  39.9 0.0 collective-permute-done.3.x3
  39.9 0.0 copy-done.2
  39.9 0.0 copy-done.3
  39.9 0.0 copy-done
  39.9 0.0 copy-done.1
  39.9 1.9 %shard_map.150 = (f32[2,3,2,16,128]{4,3,2,1,0:T(8,128)S(1)}, f32[2,3,2,16,128]{4,3,2,1,0:T(8,128)S(1)}, f32[2,3,2,16,128]{4,3,2,1,0:T(8,128)S(1)}, f32[2,3,2,16,128]{4,3,2,1,0:T(8,128)S(1)}) custom-call(f32[2,5,2,16,128]{4,3,2,1,0:T(8,128)S(1)} %pad_maximum_fusion.3.x0, f32[2,5,2,16,128]{4,3,2,1,0:T(8,128)S(1)} %collective-permute-done.1.x1, ...), custom_call_target="tpu_custom_call" | custom-call | tf_op jit(solution)/shard_map/pallas_call | solution.py:221
  41.8 2.4 %collective-permute-start.4 = (f32[2,3,2,16,128]{4,3,2,1,0:T(8,128)S(1)}, f32[2,3,2,16,128]{4,3,2,1,0:T(8,128)S(1)}, u32[]{:S(2)}, u32[]{:S(2)}) collective-permute-start(f32[2,3,2,16,128]{4,3,2,1,0:T(8,128)S(1)} %get-tuple-element.11), channel_id=1, source_target_pairs={{0,6},{2,0},{4,2},{6,4},{1,7},{3,1},{5,3},{7,5},{8,14},{10,8},{12,... | collective-permute-start | bytes 294920 | tf_op jit(solution)/shard_map/ppermute | solution.py:175
  44.2 0.8 %collective-permute-start.5 = (f32[2,3,2,16,128]{4,3,2,1,0:T(8,128)S(1)}, f32[2,3,2,16,128]{4,3,2,1,0:T(8,128)S(1)}, u32[]{:S(2)}, u32[]{:S(2)}) collective-permute-start(f32[2,3,2,16,128]{4,3,2,1,0:T(8,128)S(1)} %get-tuple-element.12), channel_id=1, source_target_pairs={{0,4},{2,6},{4,0},{6,2},{1,5},{3,7},{5,1},{7,3},{8,12},{10,14},{12... | collective-permute-start | bytes 294920 | tf_op jit(solution)/shard_map/ppermute | solution.py:175
  45.0 0.0 collective-permute-start.6
  45.0 1.1 %collective-permute-done.4 = f32[2,3,2,16,128]{4,3,2,1,0:T(8,128)S(1)} collective-permute-done((f32[2,3,2,16,128]{4,3,2,1,0:T(8,128)S(1)}, f32[2,3,2,16,128]{4,3,2,1,0:T(8,128)S(1)}, u32[]{:S(2)}, u32[]{:S(2)}) %collective-permute-start.4) | collective-permute-done | bytes 98336 | tf_op jit(solution)/shard_map/ppermute | solution.py:175
  46.2 3.2 %collective-permute-done.5 = f32[2,3,2,16,128]{4,3,2,1,0:T(8,128)S(1)} collective-permute-done((f32[2,3,2,16,128]{4,3,2,1,0:T(8,128)S(1)}, f32[2,3,2,16,128]{4,3,2,1,0:T(8,128)S(1)}, u32[]{:S(2)}, u32[]{:S(2)}) %collective-permute-start.5) | collective-permute-done | bytes 98336 | tf_op jit(solution)/shard_map/ppermute | solution.py:175
  49.3 1.6 %collective-permute-done.6 = f32[2,3,2,16,128]{4,3,2,1,0:T(8,128)S(1)} collective-permute-done((f32[2,3,2,16,128]{4,3,2,1,0:T(8,128)S(1)}, f32[2,3,2,16,128]{4,3,2,1,0:T(8,128)S(1)}, u32[]{:S(2)}, u32[]{:S(2)}) %collective-permute-start.6) | collective-permute-done | bytes 98336 | tf_op jit(solution)/shard_map/ppermute | solution.py:175
  51.0 2.2 %collective-permute-start.7 = (f32[4,3,2,16,128]{4,3,2,1,0:T(8,128)S(1)}, f32[4,3,2,16,128]{4,3,2,1,0:T(8,128)S(1)}, u32[]{:S(2)}, u32[]{:S(2)}) collective-permute-start(f32[4,3,2,16,128]{4,3,2,1,0:T(8,128)S(1)} %pad_maximum_fusion.2), channel_id=1, source_target_pairs={{0,1},{1,0},{2,3},{3,2},{4,5},{5,4},{6,7},{7,6},{8,9},{9,8},{10,11... | collective-permute-start | bytes 589832 | tf_op jit(solution)/shard_map/ppermute | solution.py:179
  53.2 1.1 %collective-permute-done.7.other_ref = f32[4,3,2,16,128]{4,3,2,1,0:T(8,128)S(1)} collective-permute-done((f32[4,3,2,16,128]{4,3,2,1,0:T(8,128)S(1)}, f32[4,3,2,16,128]{4,3,2,1,0:T(8,128)S(1)}, u32[]{:S(2)}, u32[]{:S(2)}) %collective-permute-start.7) | collective-permute-done | bytes 196640 | tf_op jit(solution)/shard_map/ppermute | solution.py:179
  54.3 0.8 %shard_map.151 = f32[8,3,16,128]{3,2,1,0:T(8,128)S(1)} custom-call(f32[128]{0:T(128)S(1)} %fusion.coef_ref, f32[4,3,2,16,128]{4,3,2,1,0:T(8,128)S(1)} %pad_maximum_fusion.1.own_ref, f32[4,3,2,16,128]{4,3,2,1,0:T(8,128)S(1)} %collective-permute-done.7.other_ref), custom_call_target="tpu_custom_call" | custom-call | tf_op jit(solution)/shard_map/pallas_call | solution.py:231
  55.1 12.5 %all_to_all.10 = f32[8,3,16,128]{3,2,1,0:T(8,128)S(1)} all-to-all(f32[8,3,16,128]{3,2,1,0:T(8,128)S(1)} %shard_map.151), channel_id=1, replica_groups=mesh['y'=4,'z'=8,'x'=4,'c'=2] {'z'}, dimensions={0} | all-to-all | bytes 393216 | tf_op jit(solution)/shard_map/all_to_all | solution.py:238
  67.6 3.0 %collective-permute-start.10 = (f32[16,128]{1,0:T(8,128)S(1)}, f32[16,128]{1,0:T(8,128)S(1)}, u32[]{:S(2)}, u32[]{:S(2)}) collective-permute-start(f32[16,128]{1,0:T(8,128)S(1)} %slice_reduce_fusion), channel_id=1, source_target_pairs={{0,128},{64,192},{128,0},{192,64},{1,129},{65,193},{129,1},{193,65... | collective-permute-start | bytes 24584 | tf_op jit(solution)/shard_map/ppermute | solution.py:183
  70.6 0.8 %collective-permute-start.9 = (f32[16,128]{1,0:T(8,128)S(1)}, f32[16,128]{1,0:T(8,128)S(1)}, u32[]{:S(2)}, u32[]{:S(2)}) collective-permute-start(f32[16,128]{1,0:T(8,128)S(1)} %slice_reduce_fusion), channel_id=1, source_target_pairs={{0,192},{64,128},{128,64},{192,0},{1,193},{65,129},{129,65},{193,1... | collective-permute-start | bytes 24584 | tf_op jit(solution)/shard_map/ppermute | solution.py:183
  71.4 0.0 collective-permute-start.8
  71.4 0.0 copy-start.6
  71.4 0.6 copy-done.6
  72.0 0.7 multiply_add_fusion
  72.8 0.0 collective-permute-done.10
  72.8 1.5 %collective-permute-done.9 = f32[16,128]{1,0:T(8,128)S(1)} collective-permute-done((f32[16,128]{1,0:T(8,128)S(1)}, f32[16,128]{1,0:T(8,128)S(1)}, u32[]{:S(2)}, u32[]{:S(2)}) %collective-permute-start.9) | collective-permute-done | bytes 8224 | tf_op jit(solution)/shard_map/ppermute | solution.py:183
  74.3 0.0 collective-permute-done.8
  74.3 0.6 add_bitcast_fusion
  (17 shorter events, 0.2 us)
Async XLA Ops:
  0.6 1.0 %copy-start.4 = (f32[1,16,2048]{2,1,0:T(8,128)S(1)}, f32[1,16,2048]{2,1,0:T(8,128)}, u32[]{:S(2)}) copy-start(f32[1,16,2048]{2,1,0:T(8,128)} %param.14) | copy-start | bytes 393220
  1.6 0.7 copy-start.5
  3.1 20.9 %all-to-all-start = ((f32[8,5,16,128]{3,2,1,0:T(8,128)}), f32[8,5,16,128]{3,2,1,0:T(8,128)S(1)}, u32[]{:S(2)}, u32[]{:S(2)}) async-start(f32[8,5,16,128]{3,2,1,0:T(8,128)} %pad_maximum_fusion), calls=%async_computation | async-start | bytes 655360 | tf_op jit(solution)/shard_map/all_to_all | solution.py:209
  25.0 3.7 %collective-permute-start = (f32[4,5,2,16,128]{4,3,2,1,0:T(8,128)S(1)}, f32[4,5,2,16,128]{4,3,2,1,0:T(8,128)S(1)}, u32[]{:S(2)}, u32[]{:S(2)}) collective-permute-start(f32[4,5,2,16,128]{4,3,2,1,0:T(8,128)S(1)} %get-tuple-element.9), channel_id=1, source_target_pairs={{0,1},{1,0},{2,3},{3,2},{4,5},{5,4},{6,7},{7,6},{8,9},{9,8},{10,11... | collective-permute-start | bytes 983048 | tf_op jit(solution)/shard_map/ppermute | solution.py:179
  28.7 6.7 %collective-permute-start.1 = (f32[2,5,2,16,128]{4,3,2,1,0:T(8,128)S(1)}, f32[2,5,2,16,128]{4,3,2,1,0:T(8,128)S(1)}, u32[]{:S(2)}, u32[]{:S(2)}) collective-permute-start(f32[2,5,2,16,128]{4,3,2,1,0:T(8,128)S(1)} %pad_maximum_fusion.4), channel_id=1, source_target_pairs={{0,2},{2,4},{4,6},{6,0},{1,3},{3,5},{5,7},{7,1},{8,10},{10,12},{12... | collective-permute-start | bytes 491528 | tf_op jit(solution)/shard_map/ppermute | solution.py:175
  30.0 9.9 %collective-permute-start.2 = (f32[2,5,2,16,128]{4,3,2,1,0:T(8,128)S(1)}, f32[2,5,2,16,128]{4,3,2,1,0:T(8,128)S(1)}, u32[]{:S(2)}, u32[]{:S(2)}) collective-permute-start(f32[2,5,2,16,128]{4,3,2,1,0:T(8,128)S(1)} %pad_maximum_fusion.5), channel_id=1, source_target_pairs={{0,4},{2,6},{4,0},{6,2},{1,5},{3,7},{5,1},{7,3},{8,12},{10,14},{12... | collective-permute-start | bytes 491528 | tf_op jit(solution)/shard_map/ppermute | solution.py:175
  32.5 7.3 %collective-permute-start.3 = (f32[2,5,2,16,128]{4,3,2,1,0:T(8,128)S(1)}, f32[2,5,2,16,128]{4,3,2,1,0:T(8,128)S(1)}, u32[]{:S(2)}, u32[]{:S(2)}) collective-permute-start(f32[2,5,2,16,128]{4,3,2,1,0:T(8,128)S(1)} %pad_maximum_fusion.6), channel_id=1, source_target_pairs={{0,6},{2,0},{4,2},{6,4},{1,7},{3,1},{5,3},{7,5},{8,14},{10,8},{12,... | collective-permute-start | bytes 491528 | tf_op jit(solution)/shard_map/ppermute | solution.py:175
  33.8 6.1 %copy-start.2 = (bf16[256,256]{1,0:T(8,128)(2,1)S(1)}, bf16[256,256]{1,0:T(8,128)(2,1)}, u32[]{:S(2)}) copy-start(bf16[256,256]{1,0:T(8,128)(2,1)} %constant.59.clone.bl) | copy-start | bytes 393220
  33.8 6.1 %copy-start.3 = (bf16[256,256]{1,0:T(8,128)(2,1)S(1)}, bf16[256,256]{1,0:T(8,128)(2,1)}, u32[]{:S(2)}) copy-start(bf16[256,256]{1,0:T(8,128)(2,1)} %constant.58.clone.bh) | copy-start | bytes 393220
  34.7 5.2 %copy-start = (bf16[256,256]{1,0:T(8,128)(2,1)S(1)}, bf16[256,256]{1,0:T(8,128)(2,1)}, u32[]{:S(2)}) copy-start(bf16[256,256]{1,0:T(8,128)(2,1)} %constant.61.clone.btl) | copy-start | bytes 393220
  34.7 5.2 %copy-start.1 = (bf16[256,256]{1,0:T(8,128)(2,1)S(1)}, bf16[256,256]{1,0:T(8,128)(2,1)}, u32[]{:S(2)}) copy-start(bf16[256,256]{1,0:T(8,128)(2,1)} %constant.60.clone.bth) | copy-start | bytes 393220
  41.8 4.4 %collective-permute-start.4 = (f32[2,3,2,16,128]{4,3,2,1,0:T(8,128)S(1)}, f32[2,3,2,16,128]{4,3,2,1,0:T(8,128)S(1)}, u32[]{:S(2)}, u32[]{:S(2)}) collective-permute-start(f32[2,3,2,16,128]{4,3,2,1,0:T(8,128)S(1)} %get-tuple-element.11), channel_id=1, source_target_pairs={{0,6},{2,0},{4,2},{6,4},{1,7},{3,1},{5,3},{7,5},{8,14},{10,8},{12,... | collective-permute-start | bytes 294920 | tf_op jit(solution)/shard_map/ppermute | solution.py:175
  44.2 5.1 %collective-permute-start.5 = (f32[2,3,2,16,128]{4,3,2,1,0:T(8,128)S(1)}, f32[2,3,2,16,128]{4,3,2,1,0:T(8,128)S(1)}, u32[]{:S(2)}, u32[]{:S(2)}) collective-permute-start(f32[2,3,2,16,128]{4,3,2,1,0:T(8,128)S(1)} %get-tuple-element.12), channel_id=1, source_target_pairs={{0,4},{2,6},{4,0},{6,2},{1,5},{3,7},{5,1},{7,3},{8,12},{10,14},{12... | collective-permute-start | bytes 294920 | tf_op jit(solution)/shard_map/ppermute | solution.py:175
  45.0 5.9 %collective-permute-start.6 = (f32[2,3,2,16,128]{4,3,2,1,0:T(8,128)S(1)}, f32[2,3,2,16,128]{4,3,2,1,0:T(8,128)S(1)}, u32[]{:S(2)}, u32[]{:S(2)}) collective-permute-start(f32[2,3,2,16,128]{4,3,2,1,0:T(8,128)S(1)} %get-tuple-element.13), channel_id=1, source_target_pairs={{0,2},{2,4},{4,6},{6,0},{1,3},{3,5},{5,7},{7,1},{8,10},{10,12},{12... | collective-permute-start | bytes 294920 | tf_op jit(solution)/shard_map/ppermute | solution.py:175
  51.0 3.3 %collective-permute-start.7 = (f32[4,3,2,16,128]{4,3,2,1,0:T(8,128)S(1)}, f32[4,3,2,16,128]{4,3,2,1,0:T(8,128)S(1)}, u32[]{:S(2)}, u32[]{:S(2)}) collective-permute-start(f32[4,3,2,16,128]{4,3,2,1,0:T(8,128)S(1)} %pad_maximum_fusion.2), channel_id=1, source_target_pairs={{0,1},{1,0},{2,3},{3,2},{4,5},{5,4},{6,7},{7,6},{8,9},{9,8},{10,11... | collective-permute-start | bytes 589832 | tf_op jit(solution)/shard_map/ppermute | solution.py:179
  67.6 5.2 %collective-permute-start.10 = (f32[16,128]{1,0:T(8,128)S(1)}, f32[16,128]{1,0:T(8,128)S(1)}, u32[]{:S(2)}, u32[]{:S(2)}) collective-permute-start(f32[16,128]{1,0:T(8,128)S(1)} %slice_reduce_fusion), channel_id=1, source_target_pairs={{0,128},{64,192},{128,0},{192,64},{1,129},{65,193},{129,1},{193,65... | collective-permute-start | bytes 24584 | tf_op jit(solution)/shard_map/ppermute | solution.py:183
  70.6 3.7 %collective-permute-start.9 = (f32[16,128]{1,0:T(8,128)S(1)}, f32[16,128]{1,0:T(8,128)S(1)}, u32[]{:S(2)}, u32[]{:S(2)}) collective-permute-start(f32[16,128]{1,0:T(8,128)S(1)} %slice_reduce_fusion), channel_id=1, source_target_pairs={{0,192},{64,128},{128,64},{192,0},{1,193},{65,129},{129,65},{193,1... | collective-permute-start | bytes 24584 | tf_op jit(solution)/shard_map/ppermute | solution.py:183
  71.4 2.9 %collective-permute-start.8 = (f32[16,128]{1,0:T(8,128)S(1)}, f32[16,128]{1,0:T(8,128)S(1)}, u32[]{:S(2)}, u32[]{:S(2)}) collective-permute-start(f32[16,128]{1,0:T(8,128)S(1)} %slice_reduce_fusion), channel_id=1, source_target_pairs={{0,64},{64,0},{128,192},{192,128},{1,65},{65,1},{129,193},{193,129... | collective-permute-start | bytes 24584 | tf_op jit(solution)/shard_map/ppermute | solution.py:183
  71.4 0.7 copy-start.6
where the time goes:
time: 75.6 us; the launch traced here: 74.9 us
  starting transfers between devices  25.7 us (34%)
  waiting for transfers between devices  24.1 us (32%)
  blocking collectives  12.5 us (17%)
  local copies, waits for them, and re-layouts  6.03 us (8%)
  Pallas kernels  3.63 us (5%)
  other arithmetic  2.18 us (3%)
  between operations  0.81 us (1%)
    all_to_all x1, blocking collectives, per_device(): blocks = lax.all_to_all(blocks, 'z', 0, 0, tiled=True)  12.5 us
    ppermute x6, waiting for transfers between devices, shift_x(): return lax.ppermute(value, 'x', [(i, (i + shift) % X) for i in range(X)])  11 us
    all_to_all x1, waiting for transfers between devices, per_device(): blocks = lax.all_to_all(blocks, 'z', 0, 0, tiled=True)  10.2 us
    all_to_all x1, starting transfers between devices, per_device(): blocks = lax.all_to_all(blocks, 'z', 0, 0, tiled=True)  9.01 us
    ppermute x6, starting transfers between devices, shift_x(): return lax.ppermute(value, 'x', [(i, (i + shift) % X) for i in range(X)])  8.31 us
    ppermute x2, starting transfers between devices, swap_core(): return lax.ppermute(value, 'c', [(0, 1), (1, 0)])  4.63 us
    ppermute x3, starting transfers between devices, pair_y(): return lax.ppermute(value, 'y', [(i, partner(i)) for i in range(Y)])  3.78 us
    squeeze x4, local copies, waits for them, and re-layouts, mine(): lax.dynamic_index_in_dim(jnp.asarray(table), place, 0, keepdims=False)  3.62 us
  transfers between devices with their start and end apart: 12, of which 9 were waited for; matrix products, arithmetic and copies ran while one was open for 6% of the time, Pallas kernels for 0%

commit v1 on v0

v1 whole, which is shorter than its diff:
```python
import functools
import math

import jax
import jax.numpy as jnp
import ml_dtypes
import numpy as np
from jax import lax
from jax.experimental import pallas as pl
from jax.experimental.pallas import tpu as pltpu
from jax.sharding import Mesh, PartitionSpec as P

Y, Z, X, C = 4, 8, 4, 2
ROWS_IN, ROWS_OUT = 5, 3
ORDER_IN, ORDER_OUT = (2, 0, 1, 3), (0, 2, 1, 3)
SUB, LANES = 16, 128
POINTS = 128
SCALE = 1.0 / 131072.0


def class_of(x, c):
    return 2 * x + c


def z_weight(x, parity, part, z):
    def weight(k):
        angle = math.pi * (2 * k + 1) * z / 16.0
        return math.cos(angle) if part == 0 else -math.sin(angle)

    return jnp.where(parity == 0, jnp.float32(weight(2 * x)), jnp.float32(weight(2 * x + 1)))


def slot_of(x, place, order):
    shift = (x - place // 2) & (X - 1)
    slot = jnp.int32(order.index(0))
    for other in range(1, X):
        slot = jnp.where(shift == other, order.index(other), slot)
    return slot


def numpy_split(table):
    table = table.astype(np.float32)
    high = table.astype(ml_dtypes.bfloat16)
    low = (table - high.astype(np.float32)).astype(ml_dtypes.bfloat16)
    return high, low


def left_tables(order):
    out = np.zeros((X * C, 2, POINTS, X, C, 2, SUB))
    alpha = np.arange(POINTS)[:, None]
    for x in range(X):
        for c in range(C):
            k = class_of(x, c) + 0.5
            for slot, shift in enumerate(order):
                for other in range(C):
                    p = class_of((x - shift) % X, c ^ other)
                    a = p * SUB + np.arange(SUB)[None, :]
                    angle = -2.0 * np.pi * ((a * alpha % POINTS) / POINTS + a * k / 2048.0)
                    at = out[class_of(x, c), :, :, slot, other]
                    at[0, :, 0], at[0, :, 1] = np.cos(angle), -np.sin(angle)
                    at[1, :, 0], at[1, :, 1] = np.sin(angle), np.cos(angle)
    return out.reshape(X * C, 2 * POINTS, 2 * POINTS)


def twiddle_tables():
    out = np.zeros((X * C, 2, POINTS, LANES))
    alpha, b = np.arange(POINTS)[:, None], np.arange(LANES)[None, :]
    for p in range(X * C):
        angle = -2.0 * np.pi * b * (alpha + (p + 0.5) / 16.0) / 16384.0
        out[p, 0], out[p, 1] = np.cos(angle), np.sin(angle)
    return out.astype(np.float32)


def right_table():
    b = np.arange(LANES)
    angle = -2.0 * np.pi * (b[:, None] * b[None, :] % LANES) / LANES
    cosine, sine = np.cos(angle), np.sin(angle)
    return np.block([[cosine, sine], [-sine, cosine]])


def pack_kernel(place_ref, grad_hbm, input_hbm, filter_hbm, out_ref, grad_ref, input_ref, filter_ref, sems):
    pairs = ((grad_hbm.at[0], grad_ref), (input_hbm.at[0], input_ref), (filter_hbm, filter_ref))
    copies = [pltpu.make_async_copy(*pair, sems.at[i]) for i, pair in enumerate(pairs)]
    for copy in copies:
        copy.start()
    for first, ref in ((0, grad_ref), (2, input_ref)):
        copies[first // 2].wait()
        values = ref[...].reshape(Z * 2, SUB, LANES)
        for z in range(Z):
            for row in range(2):
                out_ref[z, first + row] = values[2 * z + row]
    copies[2].wait()
    for z in range(Z):
        out_ref[z, 4] = filter_ref[...]


def z_forward_kernel(half, place_ref, in_ref, *out_refs):
    place = place_ref[0]
    parity = (place & 1) ^ half
    for x in range(X):
        slot = slot_of(x, place, ORDER_IN)
        for part in range(2):
            total = None
            for z in range(Z):
                term = z_weight(x, parity, part, z) * in_ref[z]
                total = term if total is None else total + term
            out_refs[0][slot, :, part] = total


def z_inverse_sums(half, place_ref, in_ref):
    place = place_ref[0]
    parity = (place & 1) ^ half
    slots = [slot_of(x, place, ORDER_OUT) for x in range(X)]
    values = [[in_ref[slots[x], :, part] for part in range(2)] for x in range(X)]
    for z in range(Z):
        total = None
        for x in range(X):
            for part in range(2):
                term = (z_weight(x, parity, part, z) * SCALE) * values[x][part]
                total = term if total is None else total + term
        yield z, total


def z_inverse_own_kernel(place_ref, skip_ref, in_ref, packed_ref, out_ref, skipped_ref):
    for z, total in z_inverse_sums(0, place_ref, in_ref):
        out_ref[z] = total
    for channel in range(Z * 2):
        z, row = divmod(channel, 2)
        skipped_ref[z, row] = skip_ref[channel] * packed_ref[z, row]


def z_inverse_other_kernel(place_ref, in_ref, own_ref, out_ref):
    for z, total in z_inverse_sums(1, place_ref, in_ref):
        out_ref[z] = own_ref[z] + total


def split(value):
    high = value.astype(jnp.bfloat16)
    return high, (value - high.astype(jnp.float32)).astype(jnp.bfloat16)


def product(left, right):
    (left_high, left_low), (right_high, right_low) = left, right
    dot = functools.partial(jnp.dot, preferred_element_type=jnp.float32)
    return dot(left_high, right_high) + (dot(left_high, right_low) + dot(left_low, right_high))


def spectral_kernel(
    x0, x1, x2, x3, left, tw, right, o0, o1, o2, o3
):
    chunks, outs = (x0, x1, x2, x3), (o0, o1, o2, o3)
    wh, wl, wth, wtl = (left[i] for i in range(4))
    bh, bl, bth, btl = (right[i] for i in range(4))
    pieces = [(s, c, part) for s in range(X) for c in range(C) for part in range(2)]
    columns = [
        jnp.concatenate([chunks[s][c, row, part] for s, c, part in pieces], axis=0)
        for row in range(ROWS_IN)
    ]
    value = product((wh, wl), split(jnp.concatenate(columns, axis=1)))
    cosine, sine = tw[0], tw[1]
    rows = []
    for row in range(ROWS_IN):
        lanes = slice(row * LANES, (row + 1) * LANES)
        real, imag = value[:POINTS, lanes], value[POINTS:, lanes]
        rows.append(
            jnp.concatenate([real * cosine - imag * sine, real * sine + imag * cosine], axis=1)
        )
    value = product(split(jnp.concatenate(rows, axis=0)), (bh, bl))
    real = [value[row * POINTS : (row + 1) * POINTS, :LANES] for row in range(ROWS_IN)]
    imag = [value[row * POINTS : (row + 1) * POINTS, LANES:] for row in range(ROWS_IN)]
    rows = []
    for channel in range(2):
        gr, gi = real[channel], imag[channel]
        rows.append(
            jnp.concatenate([real[4] * gr + imag[4] * gi, real[4] * gi - imag[4] * gr], axis=1)
        )
    dh_real, dh_imag = 0.0, 0.0
    for channel in range(2):
        gr, gi, ur, ui = real[channel], imag[channel], real[2 + channel], imag[2 + channel]
        dh_real = dh_real + (gr * ur + gi * ui)
        dh_imag = dh_imag + (gi * ur - gr * ui)
    rows.append(jnp.concatenate([dh_real, dh_imag], axis=1))
    value = product(split(jnp.concatenate(rows, axis=0)), (bth, btl))
    columns = []
    for row in range(ROWS_OUT):
        vr = value[row * POINTS : (row + 1) * POINTS, :LANES]
        vi = value[row * POINTS : (row + 1) * POINTS, LANES:]
        columns.append(
            jnp.concatenate([vr * cosine + vi * sine, vi * cosine - vr * sine], axis=0)
        )
    value = product((wth, wtl), split(jnp.concatenate(columns, axis=1)))
    for index, (s, c, part) in enumerate(pieces):
        for row in range(ROWS_OUT):
            outs[s][c, row, part] = value[
                index * SUB : (index + 1) * SUB, row * LANES : (row + 1) * LANES
            ]


VMEM = pl.BlockSpec(memory_space=pltpu.VMEM)
HBM = pl.BlockSpec(memory_space=pltpu.HBM)
SMEM = pl.BlockSpec(memory_space=pltpu.SMEM)
PARAMS = pltpu.CompilerParams(vmem_limit_bytes=32 * 1024 * 1024)


def f32(*shape):
    return jax.ShapeDtypeStruct(shape, jnp.float32)


def shift_x(value, shift):
    return lax.ppermute(value, "x", [(i, (i + shift) % X) for i in range(X)])


def swap_core(value):
    return lax.ppermute(value, "c", [(0, 1), (1, 0)])


def pair_y(value, partner):
    return lax.ppermute(value, "y", [(i, partner(i)) for i in range(Y)])


def per_device(out_grad, conv_input, filter_taps, skip_gain):
    place = class_of(lax.axis_index("x"), lax.axis_index("c"))

    def mine(table):
        return lax.dynamic_index_in_dim(jnp.asarray(table), place, 0, keepdims=False)

    tile = (SUB, LANES)
    scalar = place.reshape(1)
    matrix = right_table()
    right = jnp.asarray(np.stack(numpy_split(matrix) + numpy_split(matrix.T)))

    packed = pl.pallas_call(
        pack_kernel,
        out_shape=f32(Z, ROWS_IN, *tile),
        in_specs=[SMEM] + [HBM] * 3,
        out_specs=VMEM,
        scratch_shapes=[
            pltpu.VMEM((Z * 2, SUB * LANES), jnp.float32),
            pltpu.VMEM((Z * 2, SUB * LANES), jnp.float32),
            pltpu.VMEM(tile, jnp.float32),
            pltpu.SemaphoreType.DMA((3,)),
        ],
        compiler_params=pltpu.CompilerParams(vmem_limit_bytes=60 * 1024 * 1024),
    )(scalar, out_grad, conv_input, filter_taps.reshape(tile))
    blocks = lax.all_to_all(packed, "z", 0, 0, tiled=True)

    def z_forward(half):
        return pl.pallas_call(
            functools.partial(z_forward_kernel, half),
            out_shape=f32(X, ROWS_IN, 2, *tile),
            in_specs=[SMEM, VMEM],
            out_specs=VMEM,
            compiler_params=PARAMS,
        )(scalar, blocks)

    sent = z_forward(1)
    first = swap_core(sent[0])
    crossed = swap_core(sent[1:])
    kept = z_forward(0)
    chunks = [jnp.stack([kept[0], first])] + [jnp.stack([kept[i], crossed[i - 1]]) for i in range(1, X)]
    place, chunks[0] = lax.optimization_barrier((place, chunks[0]))
    matrix, back = left_tables(ORDER_IN), np.swapaxes(left_tables(ORDER_OUT), 1, 2)
    left = mine(np.stack(numpy_split(matrix) + numpy_split(back), axis=1))
    twiddle = mine(twiddle_tables())
    chunks = [shift_x(chunk, s) if s else chunk for chunk, s in zip(chunks, ORDER_IN)]
    chunks = pl.pallas_call(
        spectral_kernel,
        out_shape=[f32(C, ROWS_OUT, 2, *tile)] * X,
        in_specs=[VMEM] * 7,
        out_specs=[VMEM] * X,
        compiler_params=PARAMS,
    )(*chunks, left, twiddle, right)
    chunks = [shift_x(chunk, -s) if s else chunk for chunk, s in zip(chunks, ORDER_OUT)]
    own = jnp.stack([chunk[0] for chunk in chunks])
    other = swap_core(jnp.stack([chunk[1] for chunk in chunks]))

    partial, skipped = pl.pallas_call(
        z_inverse_own_kernel,
        out_shape=[f32(Z, ROWS_OUT, *tile), f32(Z, 2, *tile)],
        in_specs=[SMEM, SMEM, VMEM, VMEM],
        out_specs=[VMEM] * 2,
        compiler_params=PARAMS,
    )(scalar, skip_gain, own, packed)
    blocks = pl.pallas_call(
        z_inverse_other_kernel,
        out_shape=f32(Z, ROWS_OUT, *tile),
        in_specs=[SMEM, VMEM, VMEM],
        out_specs=VMEM,
        compiler_params=PARAMS,
    )(scalar, other, partial)
    blocks = lax.all_to_all(blocks, "z", 0, 0, tiled=True)
    filter_grad = jnp.sum(blocks[:, 2], axis=0)
    across = pair_y(filter_grad, lambda i: i ^ 2)
    far = pair_y(filter_grad, lambda i: Y - 1 - i)
    near = pair_y(filter_grad, lambda i: i ^ 1)
    filter_grad = (filter_grad + near) + (far + across)
    input_grad = blocks[:, :2] + skipped
    return (input_grad.reshape(out_grad.shape), filter_grad.reshape(filter_taps.shape))


def solution(mesh):
    fine = Mesh(mesh.devices.reshape(Y, Z, X, C), ("y", "z", "x", "c"))
    return jax.shard_map(
        per_device,
        mesh=fine,
        in_specs=(P("y", None, ("z", "x", "c")), P("y", None, ("z", "x", "c")), P(("z", "x", "c")), P()),
        out_specs=(P("y", None, ("z", "x", "c")), P(("z", "x", "c"))),
        check_vma=False,
    )
```

time: 75.6 us -> 72.5 us (0.959)
  blocking collectives: 12.5 us -> 33.2 us
  waiting for transfers between devices: 24.1 us -> 10.2 us
  starting transfers between devices: 25.7 us -> 19.4 us
  local copies, waits for them, and re-layouts: 6.03 us -> 2.79 us
  other arithmetic: 2.18 us -> 0.71 us
  Pallas kernels: 3.63 us -> 4.83 us
    all_to_all x0 -> x1, blocking collectives: none -> 20.7 us  [per_device(): blocks = lax.all_to_all(packed, 'z', 0, 0, tiled=True)]
    all_to_all x1 -> x0, waiting for transfers between devices: 10.2 us -> none  [per_device(): blocks = lax.all_to_all(blocks, 'z', 0, 0, tiled=True)]
    all_to_all x1 -> x0, starting transfers between devices: 9.01 us -> none  [per_device(): blocks = lax.all_to_all(blocks, 'z', 0, 0, tiled=True)]
    ppermute x6, waiting for transfers between devices: 11 us -> 6.99 us  [shift_x(): return lax.ppermute(value, 'x', [(i, (i + shift) % X) for i in range(X)])]
    unnamed x16 -> x6, local copies, waits for them, and re-layouts: 2.29 us -> 0.02 us
    ppermute x6, starting transfers between devices: 8.31 us -> 10.5 us  [shift_x(): return lax.ppermute(value, 'x', [(i, (i + shift) % X) for i in range(X)])]
    squeeze x4 -> x2, local copies, waits for them, and re-layouts: 3.62 us -> 1.99 us  [mine(): lax.dynamic_index_in_dim(jnp.asarray(table), place, 0, keepdims=False)]
    pallas_call x2 -> x5, Pallas kernels: 1.76 us -> 2.95 us  [the longest x1 1.81 us: per_device(): pl.pallas_call(pack_kernel, out_shape=f32(Z, ROWS_IN, *tile), in_specs=[S...]
  transfers between devices with their start and end apart: 12 -> 12, of which waited for: 9 -> 8; matrix products, arithmetic and copies ran while one was open for 6% -> 4% of each run, Pallas kernels for 0% -> 1%
where the time goes in v1:
time: 72.5 us; the launch traced here: 71.9 us
  blocking collectives  33.2 us (46%)
  starting transfers between devices  19.4 us (27%)
  waiting for transfers between devices  10.2 us (14%)
  Pallas kernels  4.83 us (7%)
  local copies, waits for them, and re-layouts  2.79 us (4%)
  between operations  0.82 us (1%)
    all_to_all x1, blocking collectives, per_device(): blocks = lax.all_to_all(packed, 'z', 0, 0, tiled=True)  20.7 us
    all_to_all x1, blocking collectives, per_device(): blocks = lax.all_to_all(blocks, 'z', 0, 0, tiled=True)  12.5 us
    ppermute x6, starting transfers between devices, shift_x(): return lax.ppermute(value, 'x', [(i, (i + shift) % X) for i in range(X)])  10.5 us
    ppermute x6, waiting for transfers between devices, shift_x(): return lax.ppermute(value, 'x', [(i, (i + shift) % X) for i in range(X)])  6.99 us
    ppermute x3, starting transfers between devices, swap_core(): return lax.ppermute(value, 'c', [(0, 1), (1, 0)])  5.12 us
    ppermute x3, starting transfers between devices, pair_y(): return lax.ppermute(value, 'y', [(i, partner(i)) for i in range(Y)])  3.78 us
    ppermute x3, waiting for transfers between devices, pair_y(): return lax.ppermute(value, 'y', [(i, partner(i)) for i in range(Y)])  2.22 us
    squeeze x2, local copies, waits for them, and re-layouts, mine(): lax.dynamic_index_in_dim(jnp.asarray(table), place, 0, keepdims=False)  1.99 us
  transfers between devices with their start and end apart: 12, of which 8 were waited for; matrix products, arithmetic and copies ran while one was open for 4% of the time, Pallas kernels for 1%

profile of v1, /device:TPU:1, one launch (start us, length us, event | category | flops | bytes accessed | tf_op | source)
XLA Modules:
  0.0 71.9 jit_solution(7630568298246391382)
XLA Ops:
  0.6 0.0 copy-start.1
  0.6 1.8 %shard_map.86.packed_ref = f32[8,5,16,128]{3,2,1,0:T(8,128)} custom-call(s32[1]{0:T(128)} %bitcast.place_ref, f32[1,16,2048]{2,1,0:T(8,128)} %grad_hbm.1, f32[1,16,2048]{2,1,0:T(8,128)} %input_hbm.1, f32[16,128]{1,0:T(8,128)} %bitcast.14), custom_call_target="tpu_custom_call" | custom-call | tf_op jit(solution)/shard_map/pallas_call | solution.py:232
  2.5 20.7 %all_to_all.10.in_ref = f32[8,5,16,128]{3,2,1,0:T(8,128)S(1)} all-to-all(f32[8,5,16,128]{3,2,1,0:T(8,128)} %shard_map.86.packed_ref), channel_id=1, replica_groups=mesh['y'=4,'z'=8,'x'=4,'c'=2] {'z'}, dimensions={0} | all-to-all | bytes 655360 | tf_op jit(solution)/shard_map/all_to_all | solution.py:245
  23.2 0.2 shard_map.88
  23.4 0.0 copy-start
  23.4 0.0 copy-start.2
  23.4 2.7 %collective-permute-start = (f32[5,2,16,128]{3,2,1,0:T(8,128)S(1)}, f32[5,2,16,128]{3,2,1,0:T(8,128)S(1)}, u32[]{:S(2)}, u32[]{:S(2)}) collective-permute-start(f32[5,2,16,128]{3,2,1,0:T(8,128)S(1)} %slice_bitcast_fusion), channel_id=1, source_target_pairs={{0,1},{1,0},{2,3},{3,2},{4,5},{5,4},{6,7},{7,6},{8,9},{9,8},{10,11... | collective-permute-start | bytes 245768 | tf_op jit(solution)/shard_map/ppermute | solution.py:214
  26.1 0.1 collective-permute-start.2
  26.2 0.2 shard_map.87
  26.4 0.6 collective-permute-done
  27.0 2.8 %collective-permute-start.1 = (f32[2,5,2,16,128]{4,3,2,1,0:T(8,128)S(1)}, f32[2,5,2,16,128]{4,3,2,1,0:T(8,128)S(1)}, u32[]{:S(2)}, u32[]{:S(2)}) collective-permute-start(f32[2,5,2,16,128]{4,3,2,1,0:T(8,128)S(1)} %pad_maximum_fusion.2), channel_id=1, source_target_pairs={{0,4},{2,6},{4,0},{6,2},{1,5},{3,7},{5,1},{7,3},{8,12},{10,14},{12... | collective-permute-start | bytes 491528 | tf_op jit(solution)/shard_map/ppermute | solution.py:210
  29.8 1.1 %dynamic-slice_bitcast_fusion.left = bf16[4,256,256]{2,1,0:T(8,128)(2,1)S(1)} fusion(bf16[8,4,256,256]{3,2,1,0:T(8,128)(2,1)} %constant.29.clone, s32[]{:T(128)S(6)} %select_n.6), kind=kLoop, calls=%fused_computation | loop fusion | bytes 1048580 | tf_op jit(solution)/shard_map/jit(dynamic_index_in_dim)/squeeze | solution.py:225
  30.9 0.0 collective-permute-done.2
  31.0 0.4 collective-permute-start.3
  31.4 2.4 %collective-permute-start.4 = (f32[2,5,2,16,128]{4,3,2,1,0:T(8,128)S(1)}, f32[2,5,2,16,128]{4,3,2,1,0:T(8,128)S(1)}, u32[]{:S(2)}, u32[]{:S(2)}) collective-permute-start(f32[2,5,2,16,128]{4,3,2,1,0:T(8,128)S(1)} %pad_maximum_fusion.5), channel_id=1, source_target_pairs={{0,6},{2,0},{4,2},{6,4},{1,7},{3,1},{5,3},{7,5},{8,14},{10,8},{12,... | collective-permute-start | bytes 491528 | tf_op jit(solution)/shard_map/ppermute | solution.py:210
  33.8 0.9 %dynamic-slice_bitcast_fusion.1.tw = f32[2,128,128]{2,1,0:T(8,128)S(1)} fusion(f32[8,2,128,128]{3,2,1,0:T(8,128)} %constant.30.clone, s32[]{:T(128)S(6)} %select_n.6), kind=kLoop, calls=%fused_computation.8 | loop fusion | bytes 262148 | tf_op jit(solution)/shard_map/jit(dynamic_index_in_dim)/squeeze | solution.py:225
  34.7 0.0 collective-permute-done.1.x0
  34.8 2.9 %collective-permute-done.3.x2 = f32[2,5,2,16,128]{4,3,2,1,0:T(8,128)S(1)} collective-permute-done((f32[2,5,2,16,128]{4,3,2,1,0:T(8,128)S(1)}, f32[2,5,2,16,128]{4,3,2,1,0:T(8,128)S(1)}, u32[]{:S(2)}, u32[]{:S(2)}) %collective-permute-start.3) | collective-permute-done | bytes 163872 | tf_op jit(solution)/shard_map/ppermute | solution.py:210
  37.6 0.1 collective-permute-done.4.x3
  37.7 0.0 copy-done.1
  37.7 1.9 %shard_map.89 = (f32[2,3,2,16,128]{4,3,2,1,0:T(8,128)S(1)}, f32[2,3,2,16,128]{4,3,2,1,0:T(8,128)S(1)}, f32[2,3,2,16,128]{4,3,2,1,0:T(8,128)S(1)}, f32[2,3,2,16,128]{4,3,2,1,0:T(8,128)S(1)}) custom-call(f32[2,5,2,16,128]{4,3,2,1,0:T(8,128)S(1)} %collective-permute-done.1.x0, f32[2,5,2,16,128]{4,3,2,1,0:T(8,128)S(1)} %pad_maximum_fusion.3.x1, ...), custom_call_target="tpu_custom_call" | custom-call | tf_op jit(solution)/shard_map/pallas_call | solution.py:266
  39.6 3.3 %collective-permute-start.5 = (f32[2,3,2,16,128]{4,3,2,1,0:T(8,128)S(1)}, f32[2,3,2,16,128]{4,3,2,1,0:T(8,128)S(1)}, u32[]{:S(2)}, u32[]{:S(2)}) collective-permute-start(f32[2,3,2,16,128]{4,3,2,1,0:T(8,128)S(1)} %get-tuple-element.13), channel_id=1, source_target_pairs={{0,4},{2,6},{4,0},{6,2},{1,5},{3,7},{5,1},{7,3},{8,12},{10,14},{12... | collective-permute-start | bytes 294920 | tf_op jit(solution)/shard_map/ppermute | solution.py:210
  43.0 0.9 %collective-permute-start.6 = (f32[2,3,2,16,128]{4,3,2,1,0:T(8,128)S(1)}, f32[2,3,2,16,128]{4,3,2,1,0:T(8,128)S(1)}, u32[]{:S(2)}, u32[]{:S(2)}) collective-permute-start(f32[2,3,2,16,128]{4,3,2,1,0:T(8,128)S(1)} %get-tuple-element.14), channel_id=1, source_target_pairs={{0,6},{2,0},{4,2},{6,4},{1,7},{3,1},{5,3},{7,5},{8,14},{10,8},{12,... | collective-permute-start | bytes 294920 | tf_op jit(solution)/shard_map/ppermute | solution.py:210
  43.9 0.6 collective-permute-start.7
  44.5 0.5 collective-permute-done.5
  45.0 2.3 %collective-permute-done.6 = f32[2,3,2,16,128]{4,3,2,1,0:T(8,128)S(1)} collective-permute-done((f32[2,3,2,16,128]{4,3,2,1,0:T(8,128)S(1)}, f32[2,3,2,16,128]{4,3,2,1,0:T(8,128)S(1)}, u32[]{:S(2)}, u32[]{:S(2)}) %collective-permute-start.6) | collective-permute-done | bytes 98336 | tf_op jit(solution)/shard_map/ppermute | solution.py:210
  47.3 1.2 %collective-permute-done.7 = f32[2,3,2,16,128]{4,3,2,1,0:T(8,128)S(1)} collective-permute-done((f32[2,3,2,16,128]{4,3,2,1,0:T(8,128)S(1)}, f32[2,3,2,16,128]{4,3,2,1,0:T(8,128)S(1)}, u32[]{:S(2)}, u32[]{:S(2)}) %collective-permute-start.7) | collective-permute-done | bytes 98336 | tf_op jit(solution)/shard_map/ppermute | solution.py:210
  48.6 2.4 %collective-permute-start.8 = (f32[4,3,2,16,128]{4,3,2,1,0:T(8,128)S(1)}, f32[4,3,2,16,128]{4,3,2,1,0:T(8,128)S(1)}, u32[]{:S(2)}, u32[]{:S(2)}) collective-permute-start(f32[4,3,2,16,128]{4,3,2,1,0:T(8,128)S(1)} %pad_maximum_fusion), channel_id=1, source_target_pairs={{0,1},{1,0},{2,3},{3,2},{4,5},{5,4},{6,7},{7,6},{8,9},{9,8},{10,11... | collective-permute-start | bytes 589832 | tf_op jit(solution)/shard_map/ppermute | solution.py:214
  51.0 0.0 copy-done
  51.0 0.0 copy-done.2
  51.0 0.7 shard_map.90
  51.7 0.4 collective-permute-done.8.in_ref
  52.0 0.1 shard_map.91
  52.1 12.5 %all_to_all.11 = f32[8,3,16,128]{3,2,1,0:T(8,128)S(1)} all-to-all(f32[8,3,16,128]{3,2,1,0:T(8,128)S(1)} %shard_map.91), channel_id=1, replica_groups=mesh['y'=4,'z'=8,'x'=4,'c'=2] {'z'}, dimensions={0} | all-to-all | bytes 393216 | tf_op jit(solution)/shard_map/all_to_all | solution.py:291
  64.6 3.0 %collective-permute-start.11 = (f32[16,128]{1,0:T(8,128)S(1)}, f32[16,128]{1,0:T(8,128)S(1)}, u32[]{:S(2)}, u32[]{:S(2)}) collective-permute-start(f32[16,128]{1,0:T(8,128)S(1)} %slice_reduce_fusion), channel_id=1, source_target_pairs={{0,128},{64,192},{128,0},{192,64},{1,129},{65,193},{129,1},{193,65... | collective-permute-start | bytes 24584 | tf_op jit(solution)/shard_map/ppermute | solution.py:218
  67.6 0.8 %collective-permute-start.10 = (f32[16,128]{1,0:T(8,128)S(1)}, f32[16,128]{1,0:T(8,128)S(1)}, u32[]{:S(2)}, u32[]{:S(2)}) collective-permute-start(f32[16,128]{1,0:T(8,128)S(1)} %slice_reduce_fusion), channel_id=1, source_target_pairs={{0,192},{64,128},{128,64},{192,0},{1,193},{65,129},{129,65},{193,1... | collective-permute-start | bytes 24584 | tf_op jit(solution)/shard_map/ppermute | solution.py:218
  68.4 0.0 collective-permute-start.9
  68.4 0.7 reshape.18
  69.1 0.0 collective-permute-done.11
  69.1 2.2 %collective-permute-done.10 = f32[16,128]{1,0:T(8,128)S(1)} collective-permute-done((f32[16,128]{1,0:T(8,128)S(1)}, f32[16,128]{1,0:T(8,128)S(1)}, u32[]{:S(2)}, u32[]{:S(2)}) %collective-permute-start.10) | collective-permute-done | bytes 8224 | tf_op jit(solution)/shard_map/ppermute | solution.py:218
  71.3 0.0 collective-permute-done.9
  71.3 0.6 add_bitcast_fusion
  (16 shorter events, 0.2 us)
Async XLA Ops:
  0.6 37.1 %copy-start.1 = (bf16[4,256,256]{2,1,0:T(8,128)(2,1)S(1)}, bf16[4,256,256]{2,1,0:T(8,128)(2,1)}, u32[]{:S(2)}) copy-start(bf16[4,256,256]{2,1,0:T(8,128)(2,1)} %constant.28.clone.right) | copy-start | bytes 1572868
  23.4 27.6 %copy-start = (f32[8,5,16,128]{3,2,1,0:T(8,128)S(1)}, f32[8,5,16,128]{3,2,1,0:T(8,128)}, u32[]{:S(2)}) copy-start(f32[8,5,16,128]{3,2,1,0:T(8,128)} %shard_map.86.packed_ref) | copy-start | bytes 983044
  23.4 27.6 %copy-start.2 = (f32[16]{0:T(128)S(1)}, f32[16]{0:T(128)}, u32[]{:S(2)}) copy-start(f32[16]{0:T(128)} %skip_ref.1) | copy-start | bytes 196
  23.4 3.6 %collective-permute-start = (f32[5,2,16,128]{3,2,1,0:T(8,128)S(1)}, f32[5,2,16,128]{3,2,1,0:T(8,128)S(1)}, u32[]{:S(2)}, u32[]{:S(2)}) collective-permute-start(f32[5,2,16,128]{3,2,1,0:T(8,128)S(1)} %slice_bitcast_fusion), channel_id=1, source_target_pairs={{0,1},{1,0},{2,3},{3,2},{4,5},{5,4},{6,7},{7,6},{8,9},{9,8},{10,11... | collective-permute-start | bytes 245768 | tf_op jit(solution)/shard_map/ppermute | solution.py:214
  26.1 4.9 %collective-permute-start.2 = (f32[3,5,2,16,128]{4,3,2,1,0:T(8,128)S(1)}, f32[3,5,2,16,128]{4,3,2,1,0:T(8,128)S(1)}, u32[]{:S(2)}, u32[]{:S(2)}) collective-permute-start(f32[3,5,2,16,128]{4,3,2,1,0:T(8,128)S(1)} %slice.79), channel_id=1, source_target_pairs={{0,1},{1,0},{2,3},{3,2},{4,5},{5,4},{6,7},{7,6},{8,9},{9,8},{10,11... | collective-permute-start | bytes 737288 | tf_op jit(solution)/shard_map/ppermute | solution.py:214
  27.0 7.8 %collective-permute-start.1 = (f32[2,5,2,16,128]{4,3,2,1,0:T(8,128)S(1)}, f32[2,5,2,16,128]{4,3,2,1,0:T(8,128)S(1)}, u32[]{:S(2)}, u32[]{:S(2)}) collective-permute-start(f32[2,5,2,16,128]{4,3,2,1,0:T(8,128)S(1)} %pad_maximum_fusion.2), channel_id=1, source_target_pairs={{0,4},{2,6},{4,0},{6,2},{1,5},{3,7},{5,1},{7,3},{8,12},{10,14},{12... | collective-permute-start | bytes 491528 | tf_op jit(solution)/shard_map/ppermute | solution.py:210
  31.0 6.7 %collective-permute-start.3 = (f32[2,5,2,16,128]{4,3,2,1,0:T(8,128)S(1)}, f32[2,5,2,16,128]{4,3,2,1,0:T(8,128)S(1)}, u32[]{:S(2)}, u32[]{:S(2)}) collective-permute-start(f32[2,5,2,16,128]{4,3,2,1,0:T(8,128)S(1)} %pad_maximum_fusion.4), channel_id=1, source_target_pairs={{0,2},{2,4},{4,6},{6,0},{1,3},{3,5},{5,7},{7,1},{8,10},{10,12},{12... | collective-permute-start | bytes 491528 | tf_op jit(solution)/shard_map/ppermute | solution.py:210
  31.4 6.4 %collective-permute-start.4 = (f32[2,5,2,16,128]{4,3,2,1,0:T(8,128)S(1)}, f32[2,5,2,16,128]{4,3,2,1,0:T(8,128)S(1)}, u32[]{:S(2)}, u32[]{:S(2)}) collective-permute-start(f32[2,5,2,16,128]{4,3,2,1,0:T(8,128)S(1)} %pad_maximum_fusion.5), channel_id=1, source_target_pairs={{0,6},{2,0},{4,2},{6,4},{1,7},{3,1},{5,3},{7,5},{8,14},{10,8},{12,... | collective-permute-start | bytes 491528 | tf_op jit(solution)/shard_map/ppermute | solution.py:210
  39.6 5.4 %collective-permute-start.5 = (f32[2,3,2,16,128]{4,3,2,1,0:T(8,128)S(1)}, f32[2,3,2,16,128]{4,3,2,1,0:T(8,128)S(1)}, u32[]{:S(2)}, u32[]{:S(2)}) collective-permute-start(f32[2,3,2,16,128]{4,3,2,1,0:T(8,128)S(1)} %get-tuple-element.13), channel_id=1, source_target_pairs={{0,4},{2,6},{4,0},{6,2},{1,5},{3,7},{5,1},{7,3},{8,12},{10,14},{12... | collective-permute-start | bytes 294920 | tf_op jit(solution)/shard_map/ppermute | solution.py:210
  43.0 4.3 %collective-permute-start.6 = (f32[2,3,2,16,128]{4,3,2,1,0:T(8,128)S(1)}, f32[2,3,2,16,128]{4,3,2,1,0:T(8,128)S(1)}, u32[]{:S(2)}, u32[]{:S(2)}) collective-permute-start(f32[2,3,2,16,128]{4,3,2,1,0:T(8,128)S(1)} %get-tuple-element.14), channel_id=1, source_target_pairs={{0,6},{2,0},{4,2},{6,4},{1,7},{3,1},{5,3},{7,5},{8,14},{10,8},{12,... | collective-permute-start | bytes 294920 | tf_op jit(solution)/shard_map/ppermute | solution.py:210
  43.9 4.7 %collective-permute-start.7 = (f32[2,3,2,16,128]{4,3,2,1,0:T(8,128)S(1)}, f32[2,3,2,16,128]{4,3,2,1,0:T(8,128)S(1)}, u32[]{:S(2)}, u32[]{:S(2)}) collective-permute-start(f32[2,3,2,16,128]{4,3,2,1,0:T(8,128)S(1)} %get-tuple-element.15), channel_id=1, source_target_pairs={{0,2},{2,4},{4,6},{6,0},{1,3},{3,5},{5,7},{7,1},{8,10},{10,12},{12... | collective-permute-start | bytes 294920 | tf_op jit(solution)/shard_map/ppermute | solution.py:210
  48.6 3.4 %collective-permute-start.8 = (f32[4,3,2,16,128]{4,3,2,1,0:T(8,128)S(1)}, f32[4,3,2,16,128]{4,3,2,1,0:T(8,128)S(1)}, u32[]{:S(2)}, u32[]{:S(2)}) collective-permute-start(f32[4,3,2,16,128]{4,3,2,1,0:T(8,128)S(1)} %pad_maximum_fusion), channel_id=1, source_target_pairs={{0,1},{1,0},{2,3},{3,2},{4,5},{5,4},{6,7},{7,6},{8,9},{9,8},{10,11... | collective-permute-start | bytes 589832 | tf_op jit(solution)/shard_map/ppermute | solution.py:214
  64.6 4.5 %collective-permute-start.11 = (f32[16,128]{1,0:T(8,128)S(1)}, f32[16,128]{1,0:T(8,128)S(1)}, u32[]{:S(2)}, u32[]{:S(2)}) collective-permute-start(f32[16,128]{1,0:T(8,128)S(1)} %slice_reduce_fusion), channel_id=1, source_target_pairs={{0,128},{64,192},{128,0},{192,64},{1,129},{65,193},{129,1},{193,65... | collective-permute-start | bytes 24584 | tf_op jit(solution)/shard_map/ppermute | solution.py:218
  67.6 3.7 %collective-permute-start.10 = (f32[16,128]{1,0:T(8,128)S(1)}, f32[16,128]{1,0:T(8,128)S(1)}, u32[]{:S(2)}, u32[]{:S(2)}) collective-permute-start(f32[16,128]{1,0:T(8,128)S(1)} %slice_reduce_fusion), channel_id=1, source_target_pairs={{0,192},{64,128},{128,64},{192,0},{1,193},{65,129},{129,65},{193,1... | collective-permute-start | bytes 24584 | tf_op jit(solution)/shard_map/ppermute | solution.py:218
  68.4 2.9 %collective-permute-start.9 = (f32[16,128]{1,0:T(8,128)S(1)}, f32[16,128]{1,0:T(8,128)S(1)}, u32[]{:S(2)}, u32[]{:S(2)}) collective-permute-start(f32[16,128]{1,0:T(8,128)S(1)} %slice_reduce_fusion), channel_id=1, source_target_pairs={{0,64},{64,0},{128,192},{192,128},{1,65},{65,1},{129,193},{193,129... | collective-permute-start | bytes 24584 | tf_op jit(solution)/shard_map/ppermute | solution.py:218

commit v2 on v1

--- a/solution.py
+++ b/solution.py
@@ -152,48 +152,50 @@
     wh, wl, wth, wtl = (left[i] for i in range(4))
     bh, bl, bth, btl = (right[i] for i in range(4))
     pieces = [(s, c, part) for s in range(X) for c in range(C) for part in range(2)]
-    columns = [
-        jnp.concatenate([chunks[s][c, row, part] for s, c, part in pieces], axis=0)
-        for row in range(ROWS_IN)
-    ]
-    value = product((wh, wl), split(jnp.concatenate(columns, axis=1)))
     cosine, sine = tw[0], tw[1]
-    rows = []
-    for row in range(ROWS_IN):
-        lanes = slice(row * LANES, (row + 1) * LANES)
-        real, imag = value[:POINTS, lanes], value[POINTS:, lanes]
-        rows.append(
-            jnp.concatenate([real * cosine - imag * sine, real * sine + imag * cosine], axis=1)
-        )
-    value = product(split(jnp.concatenate(rows, axis=0)), (bh, bl))
-    real = [value[row * POINTS : (row + 1) * POINTS, :LANES] for row in range(ROWS_IN)]
-    imag = [value[row * POINTS : (row + 1) * POINTS, LANES:] for row in range(ROWS_IN)]
-    rows = []
-    for channel in range(2):
-        gr, gi = real[channel], imag[channel]
-        rows.append(
-            jnp.concatenate([real[4] * gr + imag[4] * gi, real[4] * gi - imag[4] * gr], axis=1)
-        )
+
+    def forward(*picked):
+        columns = [
+            jnp.concatenate([chunks[s][c, row, part] for s, c, part in pieces], axis=0)
+            for row in picked
+        ]
+        value = product((wh, wl), split(jnp.concatenate(columns, axis=1)))
+        rows = []
+        for i in range(len(picked)):
+            lanes = slice(i * LANES, (i + 1) * LANES)
+            real, imag = value[:POINTS, lanes], value[POINTS:, lanes]
+            rows.append(
+                jnp.concatenate([real * cosine - imag * sine, real * sine + imag * cosine], axis=1)
+            )
+        value = product(split(jnp.concatenate(rows, axis=0)), (bh, bl))
+        spans = [slice(i * POINTS, (i + 1) * POINTS) for i in range(len(picked))]
+        return [(value[span, :LANES], value[span, LANES:]) for span in spans]
+
+    def inverse(spectra, picked):
+        rows = jnp.concatenate([jnp.concatenate(pair, axis=1) for pair in spectra], axis=0)
+        value = product(split(rows), (bth, btl))
+        columns = []
+        for i in range(len(picked)):
+            span = slice(i * POINTS, (i + 1) * POINTS)
+            vr, vi = value[span, :LANES], value[span, LANES:]
+            columns.append(
+                jnp.concatenate([vr * cosine + vi * sine, vi * cosine - vr * sine], axis=0)
+            )
+        value = product((wth, wtl), split(jnp.concatenate(columns, axis=1)))
+        for index, (s, c, part) in enumerate(pieces):
+            for i, row in enumerate(picked):
+                outs[s][c, row, part] = value[
+                    index * SUB : (index + 1) * SUB, i * LANES : (i + 1) * LANES
+                ]
+
+    ((fr, fi),) = forward(4)
+    pairs = [forward(channel, 2 + channel) for channel in range(2)]
+    inverse([(fr * gr + fi * gi, fr * gi - fi * gr) for (gr, gi), _ in pairs], (0, 1))
     dh_real, dh_imag = 0.0, 0.0
-    for channel in range(2):
-        gr, gi, ur, ui = real[channel], imag[channel], real[2 + channel], imag[2 + channel]
+    for (gr, gi), (ur, ui) in pairs:
         dh_real = dh_real + (gr * ur + gi * ui)
         dh_imag = dh_imag + (gi * ur - gr * ui)
-    rows.append(jnp.concatenate([dh_real, dh_imag], axis=1))
-    value = product(split(jnp.concatenate(rows, axis=0)), (bth, btl))
-    columns = []
-    for row in range(ROWS_OUT):
-        vr = value[row * POINTS : (row + 1) * POINTS, :LANES]
-        vi = value[row * POINTS : (row + 1) * POINTS, LANES:]
-        columns.append(
-            jnp.concatenate([vr * cosine + vi * sine, vi * cosine - vr * sine], axis=0)
-        )
-    value = product((wth, wtl), split(jnp.concatenate(columns, axis=1)))
-    for index, (s, c, part) in enumerate(pieces):
-        for row in range(ROWS_OUT):
-            outs[s][c, row, part] = value[
-                index * SUB : (index + 1) * SUB, row * LANES : (row + 1) * LANES
-            ]
+    inverse([(dh_real, dh_imag)], (2,))
 
 
 VMEM = pl.BlockSpec(memory_space=pltpu.VMEM)
@@ -231,7 +233,7 @@
 
     packed = pl.pallas_call(
         pack_kernel,
-        out_shape=f32(Z, ROWS_IN, *tile),
+        out_shape=pltpu.VMEM((Z, ROWS_IN, *tile), jnp.float32),
         in_specs=[SMEM] + [HBM] * 3,
         out_specs=VMEM,
         scratch_shapes=[
@@ -258,7 +260,7 @@
     crossed = swap_core(sent[1:])
     kept = z_forward(0)
     chunks = [jnp.stack([kept[0], first])] + [jnp.stack([kept[i], crossed[i - 1]]) for i in range(1, X)]
-    place, chunks[0] = lax.optimization_barrier((place, chunks[0]))
+    place, chunks[X - 1] = lax.optimization_barrier((place, chunks[X - 1]))
     matrix, back = left_tables(ORDER_IN), np.swapaxes(left_tables(ORDER_OUT), 1, 2)
     left = mine(np.stack(numpy_split(matrix) + numpy_split(back), axis=1))
     twiddle = mine(twiddle_tables())

time: 72.5 us -> 71.4 us (0.985)
  Pallas kernels: 4.83 us -> 3.96 us
  waiting for transfers between devices: 10.2 us -> 11 us
  starting transfers between devices: 19.4 us -> 18.6 us
    ppermute x6, starting transfers between devices: 10.5 us -> 9.74 us  [shift_x(): return lax.ppermute(value, 'x', [(i, (i + shift) % X) for i in range(X)])]
    ppermute x6, waiting for transfers between devices: 6.99 us -> 7.8 us  [shift_x(): return lax.ppermute(value, 'x', [(i, (i + shift) % X) for i in range(X)])]
    pallas_call x1, Pallas kernels: 1.81 us -> 1.08 us  [per_device(): pl.pallas_call(pack_kernel, out_shape=pltpu.VMEM((Z, ROWS_IN, *tile), jnp...]
  transfers between devices with their start and end apart: 12 -> 12, of which waited for: 8 -> 7; matrix products, arithmetic and copies ran while one was open for 4% -> 4% of each run, Pallas kernels for 1% -> 1%
where the time goes in v2:
time: 71.4 us; the launch traced here: 70.9 us
  blocking collectives  32.9 us (46%)
  starting transfers between devices  18.6 us (26%)
  waiting for transfers between devices  11 us (15%)
  Pallas kernels  3.96 us (6%)
  local copies, waits for them, and re-layouts  2.8 us (4%)
  between operations  0.79 us (1%)
    all_to_all x1, blocking collectives, per_device(): blocks = lax.all_to_all(packed, 'z', 0, 0, tiled=True)  20.5 us
    all_to_all x1, blocking collectives, per_device(): blocks = lax.all_to_all(blocks, 'z', 0, 0, tiled=True)  12.5 us
    ppermute x6, starting transfers between devices, shift_x(): return lax.ppermute(value, 'x', [(i, (i + shift) % X) for i in range(X)])  9.74 us
    ppermute x6, waiting for transfers between devices, shift_x(): return lax.ppermute(value, 'x', [(i, (i + shift) % X) for i in range(X)])  7.8 us
    ppermute x3, starting transfers between devices, swap_core(): return lax.ppermute(value, 'c', [(0, 1), (1, 0)])  5.12 us
    ppermute x3, starting transfers between devices, pair_y(): return lax.ppermute(value, 'y', [(i, partner(i)) for i in range(Y)])  3.78 us
    ppermute x3, waiting for transfers between devices, pair_y(): return lax.ppermute(value, 'y', [(i, partner(i)) for i in range(Y)])  2.23 us
    squeeze x2, local copies, waits for them, and re-layouts, mine(): lax.dynamic_index_in_dim(jnp.asarray(table), place, 0, keepdims=False)  2 us
  transfers between devices with their start and end apart: 12, of which 7 were waited for; matrix products, arithmetic and copies ran while one was open for 4% of the time, Pallas kernels for 1%

profile of v2, /device:TPU:1, one launch (start us, length us, event | category | flops | bytes accessed | tf_op | source)
XLA Modules:
  0.0 70.9 jit_solution(9951131551417630814)
XLA Ops:
  0.6 0.0 copy-start
  0.6 1.1 %shard_map.86.packed_ref = f32[8,5,16,128]{3,2,1,0:T(8,128)S(1)} custom-call(s32[1]{0:T(128)} %bitcast.place_ref, f32[1,16,2048]{2,1,0:T(8,128)} %grad_hbm.1, f32[1,16,2048]{2,1,0:T(8,128)} %input_hbm.1, f32[16,128]{1,0:T(8,128)} %bitcast.14), custom_call_target="tpu_custom_call" | custom-call | tf_op jit(solution)/shard_map/pallas_call | solution.py:234
  1.7 20.5 %all_to_all.10.in_ref = f32[8,5,16,128]{3,2,1,0:T(8,128)S(1)} all-to-all(f32[8,5,16,128]{3,2,1,0:T(8,128)S(1)} %shard_map.86.packed_ref), channel_id=1, replica_groups=mesh['y'=4,'z'=8,'x'=4,'c'=2] {'z'}, dimensions={0} | all-to-all | bytes 655360 | tf_op jit(solution)/shard_map/all_to_all | solution.py:247
  22.2 0.2 shard_map.88
  22.4 0.0 copy-start.1
  22.4 2.7 %collective-permute-start = (f32[5,2,16,128]{3,2,1,0:T(8,128)S(1)}, f32[5,2,16,128]{3,2,1,0:T(8,128)S(1)}, u32[]{:S(2)}, u32[]{:S(2)}) collective-permute-start(f32[5,2,16,128]{3,2,1,0:T(8,128)S(1)} %slice_bitcast_fusion), channel_id=1, source_target_pairs={{0,1},{1,0},{2,3},{3,2},{4,5},{5,4},{6,7},{7,6},{8,9},{9,8},{10,11... | collective-permute-start | bytes 245768 | tf_op jit(solution)/shard_map/ppermute | solution.py:216
  25.1 0.1 collective-permute-start.2
  25.2 0.2 shard_map.87
  25.4 0.6 collective-permute-done
  26.0 2.8 %collective-permute-start.1 = (f32[2,5,2,16,128]{4,3,2,1,0:T(8,128)S(1)}, f32[2,5,2,16,128]{4,3,2,1,0:T(8,128)S(1)}, u32[]{:S(2)}, u32[]{:S(2)}) collective-permute-start(f32[2,5,2,16,128]{4,3,2,1,0:T(8,128)S(1)} %pad_maximum_fusion.2), channel_id=1, source_target_pairs={{0,4},{2,6},{4,0},{6,2},{1,5},{3,7},{5,1},{7,3},{8,12},{10,14},{12... | collective-permute-start | bytes 491528 | tf_op jit(solution)/shard_map/ppermute | solution.py:212
  28.9 0.0 collective-permute-done.2
  28.9 0.4 collective-permute-start.3
  29.3 2.4 %collective-permute-start.4 = (f32[2,5,2,16,128]{4,3,2,1,0:T(8,128)S(1)}, f32[2,5,2,16,128]{4,3,2,1,0:T(8,128)S(1)}, u32[]{:S(2)}, u32[]{:S(2)}) collective-permute-start(f32[2,5,2,16,128]{4,3,2,1,0:T(8,128)S(1)} %pad_maximum_fusion.5), channel_id=1, source_target_pairs={{0,6},{2,0},{4,2},{6,4},{1,7},{3,1},{5,3},{7,5},{8,14},{10,8},{12,... | collective-permute-start | bytes 491528 | tf_op jit(solution)/shard_map/ppermute | solution.py:212
  31.7 0.9 %dynamic-slice_bitcast_fusion.1.tw = f32[2,128,128]{2,1,0:T(8,128)S(1)} fusion(f32[8,2,128,128]{3,2,1,0:T(8,128)} %constant.30.clone, s32[]{:T(128)S(6)} %select_n.6), kind=kLoop, calls=%fused_computation.8 | loop fusion | bytes 262148 | tf_op jit(solution)/shard_map/jit(dynamic_index_in_dim)/squeeze | solution.py:227
  32.6 1.1 %dynamic-slice_bitcast_fusion.left = bf16[4,256,256]{2,1,0:T(8,128)(2,1)S(1)} fusion(bf16[8,4,256,256]{3,2,1,0:T(8,128)(2,1)} %constant.29.clone, s32[]{:T(128)S(6)} %select_n.6), kind=kLoop, calls=%fused_computation | loop fusion | bytes 1048580 | tf_op jit(solution)/shard_map/jit(dynamic_index_in_dim)/squeeze | solution.py:227
  33.7 0.0 collective-permute-done.1.x0
  33.7 3.1 %collective-permute-done.3.x2 = f32[2,5,2,16,128]{4,3,2,1,0:T(8,128)S(1)} collective-permute-done((f32[2,5,2,16,128]{4,3,2,1,0:T(8,128)S(1)}, f32[2,5,2,16,128]{4,3,2,1,0:T(8,128)S(1)}, u32[]{:S(2)}, u32[]{:S(2)}) %collective-permute-start.3) | collective-permute-done | bytes 163872 | tf_op jit(solution)/shard_map/ppermute | solution.py:212
  36.9 0.0 collective-permute-done.4.x3
  36.9 0.0 copy-done
  36.9 1.8 %shard_map.89 = (f32[2,3,2,16,128]{4,3,2,1,0:T(8,128)S(1)}, f32[2,3,2,16,128]{4,3,2,1,0:T(8,128)S(1)}, f32[2,3,2,16,128]{4,3,2,1,0:T(8,128)S(1)}, f32[2,3,2,16,128]{4,3,2,1,0:T(8,128)S(1)}) custom-call(f32[2,5,2,16,128]{4,3,2,1,0:T(8,128)S(1)} %collective-permute-done.1.x0, f32[2,5,2,16,128]{4,3,2,1,0:T(8,128)S(1)} %pad_maximum_fusion.3.x1, ...), custom_call_target="tpu_custom_call" | custom-call | tf_op jit(solution)/shard_map/pallas_call | solution.py:268
  38.6 1.8 %collective-permute-start.5 = (f32[2,3,2,16,128]{4,3,2,1,0:T(8,128)S(1)}, f32[2,3,2,16,128]{4,3,2,1,0:T(8,128)S(1)}, u32[]{:S(2)}, u32[]{:S(2)}) collective-permute-start(f32[2,3,2,16,128]{4,3,2,1,0:T(8,128)S(1)} %get-tuple-element.13), channel_id=1, source_target_pairs={{0,4},{2,6},{4,0},{6,2},{1,5},{3,7},{5,1},{7,3},{8,12},{10,14},{12... | collective-permute-start | bytes 294920 | tf_op jit(solution)/shard_map/ppermute | solution.py:212
  40.5 2.3 %collective-permute-start.6 = (f32[2,3,2,16,128]{4,3,2,1,0:T(8,128)S(1)}, f32[2,3,2,16,128]{4,3,2,1,0:T(8,128)S(1)}, u32[]{:S(2)}, u32[]{:S(2)}) collective-permute-start(f32[2,3,2,16,128]{4,3,2,1,0:T(8,128)S(1)} %get-tuple-element.14), channel_id=1, source_target_pairs={{0,6},{2,0},{4,2},{6,4},{1,7},{3,1},{5,3},{7,5},{8,14},{10,8},{12,... | collective-permute-start | bytes 294920 | tf_op jit(solution)/shard_map/ppermute | solution.py:212
  42.8 0.0 collective-permute-start.7
  42.8 0.9 %collective-permute-done.5 = f32[2,3,2,16,128]{4,3,2,1,0:T(8,128)S(1)} collective-permute-done((f32[2,3,2,16,128]{4,3,2,1,0:T(8,128)S(1)}, f32[2,3,2,16,128]{4,3,2,1,0:T(8,128)S(1)}, u32[]{:S(2)}, u32[]{:S(2)}) %collective-permute-start.5) | collective-permute-done | bytes 98336 | tf_op jit(solution)/shard_map/ppermute | solution.py:212
  43.7 1.9 %collective-permute-done.6 = f32[2,3,2,16,128]{4,3,2,1,0:T(8,128)S(1)} collective-permute-done((f32[2,3,2,16,128]{4,3,2,1,0:T(8,128)S(1)}, f32[2,3,2,16,128]{4,3,2,1,0:T(8,128)S(1)}, u32[]{:S(2)}, u32[]{:S(2)}) %collective-permute-start.6) | collective-permute-done | bytes 98336 | tf_op jit(solution)/shard_map/ppermute | solution.py:212
  45.6 1.9 %collective-permute-done.7 = f32[2,3,2,16,128]{4,3,2,1,0:T(8,128)S(1)} collective-permute-done((f32[2,3,2,16,128]{4,3,2,1,0:T(8,128)S(1)}, f32[2,3,2,16,128]{4,3,2,1,0:T(8,128)S(1)}, u32[]{:S(2)}, u32[]{:S(2)}) %collective-permute-start.7) | collective-permute-done | bytes 98336 | tf_op jit(solution)/shard_map/ppermute | solution.py:212
  47.5 2.4 %collective-permute-start.8 = (f32[4,3,2,16,128]{4,3,2,1,0:T(8,128)S(1)}, f32[4,3,2,16,128]{4,3,2,1,0:T(8,128)S(1)}, u32[]{:S(2)}, u32[]{:S(2)}) collective-permute-start(f32[4,3,2,16,128]{4,3,2,1,0:T(8,128)S(1)} %pad_maximum_fusion), channel_id=1, source_target_pairs={{0,1},{1,0},{2,3},{3,2},{4,5},{5,4},{6,7},{7,6},{8,9},{9,8},{10,11... | collective-permute-start | bytes 589832 | tf_op jit(solution)/shard_map/ppermute | solution.py:216
  49.9 0.0 copy-done.1
  49.9 0.7 shard_map.90
  50.6 0.4 collective-permute-done.8.in_ref
  50.9 0.1 shard_map.91
  51.1 12.5 %all_to_all.11 = f32[8,3,16,128]{3,2,1,0:T(8,128)S(1)} all-to-all(f32[8,3,16,128]{3,2,1,0:T(8,128)S(1)} %shard_map.91), channel_id=1, replica_groups=mesh['y'=4,'z'=8,'x'=4,'c'=2] {'z'}, dimensions={0} | all-to-all | bytes 393216 | tf_op jit(solution)/shard_map/all_to_all | solution.py:293
  63.5 3.0 %collective-permute-start.11 = (f32[16,128]{1,0:T(8,128)S(1)}, f32[16,128]{1,0:T(8,128)S(1)}, u32[]{:S(2)}, u32[]{:S(2)}) collective-permute-start(f32[16,128]{1,0:T(8,128)S(1)} %slice_reduce_fusion), channel_id=1, source_target_pairs={{0,128},{64,192},{128,0},{192,64},{1,129},{65,193},{129,1},{193,65... | collective-permute-start | bytes 24584 | tf_op jit(solution)/shard_map/ppermute | solution.py:220
  66.5 0.8 %collective-permute-start.10 = (f32[16,128]{1,0:T(8,128)S(1)}, f32[16,128]{1,0:T(8,128)S(1)}, u32[]{:S(2)}, u32[]{:S(2)}) collective-permute-start(f32[16,128]{1,0:T(8,128)S(1)} %slice_reduce_fusion), channel_id=1, source_target_pairs={{0,192},{64,128},{128,64},{192,0},{1,193},{65,129},{129,65},{193,1... | collective-permute-start | bytes 24584 | tf_op jit(solution)/shard_map/ppermute | solution.py:220
  67.3 0.0 collective-permute-start.9
  67.3 0.7 reshape.18
  68.0 0.0 collective-permute-done.11
  68.0 2.2 %collective-permute-done.10 = f32[16,128]{1,0:T(8,128)S(1)} collective-permute-done((f32[16,128]{1,0:T(8,128)S(1)}, f32[16,128]{1,0:T(8,128)S(1)}, u32[]{:S(2)}, u32[]{:S(2)}) %collective-permute-start.10) | collective-permute-done | bytes 8224 | tf_op jit(solution)/shard_map/ppermute | solution.py:220
  70.2 0.0 collective-permute-done.9
  70.3 0.6 add_bitcast_fusion
  (16 shorter events, 0.2 us)
Async XLA Ops:
  0.6 36.2 %copy-start = (bf16[4,256,256]{2,1,0:T(8,128)(2,1)S(1)}, bf16[4,256,256]{2,1,0:T(8,128)(2,1)}, u32[]{:S(2)}) copy-start(bf16[4,256,256]{2,1,0:T(8,128)(2,1)} %constant.28.clone.right) | copy-start | bytes 1572868
  22.4 27.5 %copy-start.1 = (f32[16]{0:T(128)S(1)}, f32[16]{0:T(128)}, u32[]{:S(2)}) copy-start(f32[16]{0:T(128)} %skip_ref.1) | copy-start | bytes 196
  22.4 3.6 %collective-permute-start = (f32[5,2,16,128]{3,2,1,0:T(8,128)S(1)}, f32[5,2,16,128]{3,2,1,0:T(8,128)S(1)}, u32[]{:S(2)}, u32[]{:S(2)}) collective-permute-start(f32[5,2,16,128]{3,2,1,0:T(8,128)S(1)} %slice_bitcast_fusion), channel_id=1, source_target_pairs={{0,1},{1,0},{2,3},{3,2},{4,5},{5,4},{6,7},{7,6},{8,9},{9,8},{10,11... | collective-permute-start | bytes 245768 | tf_op jit(solution)/shard_map/ppermute | solution.py:216
  25.1 3.8 %collective-permute-start.2 = (f32[3,5,2,16,128]{4,3,2,1,0:T(8,128)S(1)}, f32[3,5,2,16,128]{4,3,2,1,0:T(8,128)S(1)}, u32[]{:S(2)}, u32[]{:S(2)}) collective-permute-start(f32[3,5,2,16,128]{4,3,2,1,0:T(8,128)S(1)} %slice.79), channel_id=1, source_target_pairs={{0,1},{1,0},{2,3},{3,2},{4,5},{5,4},{6,7},{7,6},{8,9},{9,8},{10,11... | collective-permute-start | bytes 737288 | tf_op jit(solution)/shard_map/ppermute | solution.py:216
  26.0 7.7 %collective-permute-start.1 = (f32[2,5,2,16,128]{4,3,2,1,0:T(8,128)S(1)}, f32[2,5,2,16,128]{4,3,2,1,0:T(8,128)S(1)}, u32[]{:S(2)}, u32[]{:S(2)}) collective-permute-start(f32[2,5,2,16,128]{4,3,2,1,0:T(8,128)S(1)} %pad_maximum_fusion.2), channel_id=1, source_target_pairs={{0,4},{2,6},{4,0},{6,2},{1,5},{3,7},{5,1},{7,3},{8,12},{10,14},{12... | collective-permute-start | bytes 491528 | tf_op jit(solution)/shard_map/ppermute | solution.py:212
  28.9 7.9 %collective-permute-start.3 = (f32[2,5,2,16,128]{4,3,2,1,0:T(8,128)S(1)}, f32[2,5,2,16,128]{4,3,2,1,0:T(8,128)S(1)}, u32[]{:S(2)}, u32[]{:S(2)}) collective-permute-start(f32[2,5,2,16,128]{4,3,2,1,0:T(8,128)S(1)} %pad_maximum_fusion.4), channel_id=1, source_target_pairs={{0,2},{2,4},{4,6},{6,0},{1,3},{3,5},{5,7},{7,1},{8,10},{10,12},{12... | collective-permute-start | bytes 491528 | tf_op jit(solution)/shard_map/ppermute | solution.py:212
  29.3 7.5 %collective-permute-start.4 = (f32[2,5,2,16,128]{4,3,2,1,0:T(8,128)S(1)}, f32[2,5,2,16,128]{4,3,2,1,0:T(8,128)S(1)}, u32[]{:S(2)}, u32[]{:S(2)}) collective-permute-start(f32[2,5,2,16,128]{4,3,2,1,0:T(8,128)S(1)} %pad_maximum_fusion.5), channel_id=1, source_target_pairs={{0,6},{2,0},{4,2},{6,4},{1,7},{3,1},{5,3},{7,5},{8,14},{10,8},{12,... | collective-permute-start | bytes 491528 | tf_op jit(solution)/shard_map/ppermute | solution.py:212
  38.6 5.1 %collective-permute-start.5 = (f32[2,3,2,16,128]{4,3,2,1,0:T(8,128)S(1)}, f32[2,3,2,16,128]{4,3,2,1,0:T(8,128)S(1)}, u32[]{:S(2)}, u32[]{:S(2)}) collective-permute-start(f32[2,3,2,16,128]{4,3,2,1,0:T(8,128)S(1)} %get-tuple-element.13), channel_id=1, source_target_pairs={{0,4},{2,6},{4,0},{6,2},{1,5},{3,7},{5,1},{7,3},{8,12},{10,14},{12... | collective-permute-start | bytes 294920 | tf_op jit(solution)/shard_map/ppermute | solution.py:212
  40.5 5.1 %collective-permute-start.6 = (f32[2,3,2,16,128]{4,3,2,1,0:T(8,128)S(1)}, f32[2,3,2,16,128]{4,3,2,1,0:T(8,128)S(1)}, u32[]{:S(2)}, u32[]{:S(2)}) collective-permute-start(f32[2,3,2,16,128]{4,3,2,1,0:T(8,128)S(1)} %get-tuple-element.14), channel_id=1, source_target_pairs={{0,6},{2,0},{4,2},{6,4},{1,7},{3,1},{5,3},{7,5},{8,14},{10,8},{12,... | collective-permute-start | bytes 294920 | tf_op jit(solution)/shard_map/ppermute | solution.py:212
  42.8 4.7 %collective-permute-start.7 = (f32[2,3,2,16,128]{4,3,2,1,0:T(8,128)S(1)}, f32[2,3,2,16,128]{4,3,2,1,0:T(8,128)S(1)}, u32[]{:S(2)}, u32[]{:S(2)}) collective-permute-start(f32[2,3,2,16,128]{4,3,2,1,0:T(8,128)S(1)} %get-tuple-element.15), channel_id=1, source_target_pairs={{0,2},{2,4},{4,6},{6,0},{1,3},{3,5},{5,7},{7,1},{8,10},{10,12},{12... | collective-permute-start | bytes 294920 | tf_op jit(solution)/shard_map/ppermute | solution.py:212
  47.5 3.4 %collective-permute-start.8 = (f32[4,3,2,16,128]{4,3,2,1,0:T(8,128)S(1)}, f32[4,3,2,16,128]{4,3,2,1,0:T(8,128)S(1)}, u32[]{:S(2)}, u32[]{:S(2)}) collective-permute-start(f32[4,3,2,16,128]{4,3,2,1,0:T(8,128)S(1)} %pad_maximum_fusion), channel_id=1, source_target_pairs={{0,1},{1,0},{2,3},{3,2},{4,5},{5,4},{6,7},{7,6},{8,9},{9,8},{10,11... | collective-permute-start | bytes 589832 | tf_op jit(solution)/shard_map/ppermute | solution.py:216
  63.5 4.5 %collective-permute-start.11 = (f32[16,128]{1,0:T(8,128)S(1)}, f32[16,128]{1,0:T(8,128)S(1)}, u32[]{:S(2)}, u32[]{:S(2)}) collective-permute-start(f32[16,128]{1,0:T(8,128)S(1)} %slice_reduce_fusion), channel_id=1, source_target_pairs={{0,128},{64,192},{128,0},{192,64},{1,129},{65,193},{129,1},{193,65... | collective-permute-start | bytes 24584 | tf_op jit(solution)/shard_map/ppermute | solution.py:220
  66.5 3.7 %collective-permute-start.10 = (f32[16,128]{1,0:T(8,128)S(1)}, f32[16,128]{1,0:T(8,128)S(1)}, u32[]{:S(2)}, u32[]{:S(2)}) collective-permute-start(f32[16,128]{1,0:T(8,128)S(1)} %slice_reduce_fusion), channel_id=1, source_target_pairs={{0,192},{64,128},{128,64},{192,0},{1,193},{65,129},{129,65},{193,1... | collective-permute-start | bytes 24584 | tf_op jit(solution)/shard_map/ppermute | solution.py:220
  67.3 2.9 %collective-permute-start.9 = (f32[16,128]{1,0:T(8,128)S(1)}, f32[16,128]{1,0:T(8,128)S(1)}, u32[]{:S(2)}, u32[]{:S(2)}) collective-permute-start(f32[16,128]{1,0:T(8,128)S(1)} %slice_reduce_fusion), channel_id=1, source_target_pairs={{0,64},{64,0},{128,192},{192,128},{1,65},{65,1},{129,193},{193,129... | collective-permute-start | bytes 24584 | tf_op jit(solution)/shard_map/ppermute | solution.py:220

commit v3 on v2

--- a/solution.py
+++ b/solution.py
@@ -12,6 +12,8 @@
 
 Y, Z, X, C = 4, 8, 4, 2
 ROWS_IN, ROWS_OUT = 5, 3
+SHIFTS, SHIFTS_BACK = ((3, 6, 1, 0), (4, 5, 2, 7)), ((1, 6, 3, 0), (2, 5, 4, 7))
+KEPT, UNUSED = 3, 7
 ORDER_IN, ORDER_OUT = (2, 0, 1, 3), (0, 2, 1, 3)
 SUB, LANES = 16, 128
 POINTS = 128
@@ -22,12 +24,18 @@
     return 2 * x + c
 
 
-def z_weight(x, parity, part, z):
-    def weight(k):
-        angle = math.pi * (2 * k + 1) * z / 16.0
-        return math.cos(angle) if part == 0 else -math.sin(angle)
-
-    return jnp.where(parity == 0, jnp.float32(weight(2 * x)), jnp.float32(weight(2 * x + 1)))
+def came_from(zone, core, shifts):
+    shift = jnp.where(core == 0, *shifts)
+    return (zone - shift) & (Z - 1)
+
+
+def turn(source, multiple):
+    real, imag = jnp.float32(1.0), jnp.float32(0.0)
+    for z in range(1, Z):
+        angle = math.pi * multiple * z / 16.0
+        real = jnp.where(source == z, jnp.float32(math.cos(angle)), real)
+        imag = jnp.where(source == z, jnp.float32(-math.sin(angle)), imag)
+    return real, imag
 
 
 def slot_of(x, place, order):
@@ -94,44 +102,71 @@
         out_ref[z, 4] = filter_ref[...]
 
 
-def z_forward_kernel(half, place_ref, in_ref, *out_refs):
-    place = place_ref[0]
-    parity = (place & 1) ^ half
+def z_forward_kernel(half, place_ref, zone_ref, m0, m1, m2, m3, out_ref):
+    place, steps = place_ref[0], (m0, m1, m2, m3)
+    core = place & 1
+    parity = core ^ half
+    weights, turns = [], []
+    for i in range(len(steps)):
+        source = came_from(zone_ref[0], core, (SHIFTS[0][i], SHIFTS[1][i]))
+        starts = [turn(source, multiple) for multiple in (1, 3)]
+        weights.append([
+            jnp.full((SUB, LANES), jnp.where(parity == 0, low, high)) for low, high in zip(*starts)
+        ])
+        turns.append([jnp.full((SUB, LANES), part) for part in turn(source, 4)])
     for x in range(X):
         slot = slot_of(x, place, ORDER_IN)
         for part in range(2):
-            total = None
-            for z in range(Z):
-                term = z_weight(x, parity, part, z) * in_ref[z]
-                total = term if total is None else total + term
-            out_refs[0][slot, :, part] = total
-
-
-def z_inverse_sums(half, place_ref, in_ref):
+            for source in range(C):
+                total = weights[0][part] * m0[source]
+                for weight, ref in zip(weights[1:], steps[1:]):
+                    total = total + weight[part] * ref[source]
+                out_ref[slot, source ^ half, :, part] = total
+        weights = [
+            [real * re - imag * im, real * im + imag * re]
+            for (real, imag), (re, im) in zip(weights, turns)
+        ]
+
+
+def z_return_kernel(half, place_ref, zone_ref, near_ref, far_ref, out_ref):
     place = place_ref[0]
-    parity = (place & 1) ^ half
+    core = place & 1
     slots = [slot_of(x, place, ORDER_OUT) for x in range(X)]
-    values = [[in_ref[slots[x], :, part] for part in range(2)] for x in range(X)]
-    for z in range(Z):
-        total = None
+    for i in range(Z // 2):
+        shift = jnp.where(core == half, SHIFTS_BACK[0][i], SHIFTS_BACK[1][i])
+        target = (zone_ref[0] + shift) & (Z - 1)
+        starts = [turn(target, multiple) for multiple in (1, 3)]
+        weight = [
+            jnp.full((SUB, LANES), jnp.where(core == 0, low, high) * SCALE)
+            for low, high in zip(*starts)
+        ]
+        re, im = [jnp.full((SUB, LANES), part) for part in turn(target, 4)]
+        totals = [None, None]
         for x in range(X):
             for part in range(2):
-                term = (z_weight(x, parity, part, z) * SCALE) * values[x][part]
-                total = term if total is None else total + term
-        yield z, total
-
-
-def z_inverse_own_kernel(place_ref, skip_ref, in_ref, packed_ref, out_ref, skipped_ref):
-    for z, total in z_inverse_sums(0, place_ref, in_ref):
-        out_ref[z] = total
-    for channel in range(Z * 2):
-        z, row = divmod(channel, 2)
-        skipped_ref[z, row] = skip_ref[channel] * packed_ref[z, row]
-
-
-def z_inverse_other_kernel(place_ref, in_ref, own_ref, out_ref):
-    for z, total in z_inverse_sums(1, place_ref, in_ref):
-        out_ref[z] = own_ref[z] + total
+                for block, ref in enumerate((near_ref, far_ref)):
+                    term = weight[part] * ref[slots[x], :, part]
+                    totals[block] = term if totals[block] is None else totals[block] + term
+            real, imag = weight
+            weight = [real * re - imag * im, real * im + imag * re]
+        for block in range(2):
+            out_ref[i, block ^ half] = totals[block]
+
+
+def filter_sum_kernel(r0, r1, r2, r3, other_ref, out_ref):
+    pairs = [ref[0, 2] + other_ref[i, 2] for i, ref in enumerate((r0, r1, r2, r3))]
+    out_ref[...] = (pairs[0] + pairs[1]) + (pairs[2] + pairs[3])
+
+
+def finish_kernel(place_ref, zone_ref, skip_ref, packed_ref, r0, r1, r2, r3, other_ref, out_ref):
+    core = place_ref[0] & 1
+    for half in range(2):
+        for i, ref in enumerate((r0, r1, r2, r3)):
+            shifts = (SHIFTS_BACK[0][i], SHIFTS_BACK[1][i])
+            source = came_from(zone_ref[0], core ^ half, shifts)
+            for row in range(2):
+                value = other_ref[i, row] if half else ref[0, row]
+                out_ref[source, row] = value + skip_ref[2 * source + row] * packed_ref[source, row]
 
 
 def split(value):
@@ -212,6 +247,11 @@
     return lax.ppermute(value, "x", [(i, (i + shift) % X) for i in range(X)])
 
 
+def shift_z(value, even, odd):
+    pairs = [(C * z + c, C * ((z + by) % Z) + c) for c, by in enumerate((even, odd)) for z in range(Z)]
+    return lax.ppermute(value, ("z", "c"), pairs)
+
+
 def swap_core(value):
     return lax.ppermute(value, "c", [(0, 1), (1, 0)])
 
@@ -244,22 +284,36 @@
         ],
         compiler_params=pltpu.CompilerParams(vmem_limit_bytes=60 * 1024 * 1024),
     )(scalar, out_grad, conv_input, filter_taps.reshape(tile))
-    blocks = lax.all_to_all(packed, "z", 0, 0, tiled=True)
+    zone, core = lax.axis_index("z"), lax.axis_index("c")
+
+    def toward(i, crossed):
+        shift = jnp.where(core == crossed, SHIFTS[0][i], SHIFTS[1][i])
+        return lax.dynamic_index_in_dim(packed, (zone + shift) & (Z - 1), 0, keepdims=False)
+
+    given = swap_core(jnp.stack([toward(i, 1) for i in range(Z // 2)]))
+
+    def exchange_z(messages, shifts):
+        even = shifts[0][:KEPT] + (UNUSED,)
+        moved = [shift_z(m, *by) for m, *by in zip(messages, even, shifts[1])]
+        moved[KEPT] = jnp.where(core == 0, messages[KEPT], moved[KEPT])
+        return moved
+
+    steps = exchange_z([jnp.stack([toward(i, 0), given[i]]) for i in range(Z // 2)], SHIFTS)
 
     def z_forward(half):
         return pl.pallas_call(
             functools.partial(z_forward_kernel, half),
-            out_shape=f32(X, ROWS_IN, 2, *tile),
-            in_specs=[SMEM, VMEM],
+            out_shape=f32(X, C, ROWS_IN, 2, *tile),
+            in_specs=[SMEM, SMEM] + [VMEM] * 4,
             out_specs=VMEM,
             compiler_params=PARAMS,
-        )(scalar, blocks)
+        )(scalar, zone.reshape(1), *steps)
 
     sent = z_forward(1)
     first = swap_core(sent[0])
     crossed = swap_core(sent[1:])
     kept = z_forward(0)
-    chunks = [jnp.stack([kept[0], first])] + [jnp.stack([kept[i], crossed[i - 1]]) for i in range(1, X)]
+    chunks = [kept[0] + first] + [kept[i] + crossed[i - 1] for i in range(1, X)]
     place, chunks[X - 1] = lax.optimization_barrier((place, chunks[X - 1]))
     matrix, back = left_tables(ORDER_IN), np.swapaxes(left_tables(ORDER_OUT), 1, 2)
     left = mine(np.stack(numpy_split(matrix) + numpy_split(back), axis=1))
@@ -273,30 +327,40 @@
         compiler_params=PARAMS,
     )(*chunks, left, twiddle, right)
     chunks = [shift_x(chunk, -s) if s else chunk for chunk, s in zip(chunks, ORDER_OUT)]
-    own = jnp.stack([chunk[0] for chunk in chunks])
-    other = swap_core(jnp.stack([chunk[1] for chunk in chunks]))
-
-    partial, skipped = pl.pallas_call(
-        z_inverse_own_kernel,
-        out_shape=[f32(Z, ROWS_OUT, *tile), f32(Z, 2, *tile)],
-        in_specs=[SMEM, SMEM, VMEM, VMEM],
-        out_specs=[VMEM] * 2,
-        compiler_params=PARAMS,
-    )(scalar, skip_gain, own, packed)
-    blocks = pl.pallas_call(
-        z_inverse_other_kernel,
-        out_shape=f32(Z, ROWS_OUT, *tile),
-        in_specs=[SMEM, VMEM, VMEM],
+    near = jnp.stack([chunk[0] for chunk in chunks])
+    far = jnp.stack([chunk[1] for chunk in chunks])
+
+    def z_return(half):
+        return pl.pallas_call(
+            functools.partial(z_return_kernel, half),
+            out_shape=f32(Z // 2, C, ROWS_OUT, *tile),
+            in_specs=[SMEM] * 2 + [VMEM] * 2,
+            out_specs=VMEM,
+            compiler_params=PARAMS,
+        )(scalar, zone.reshape(1), near, far)
+
+    crossed = swap_core(z_return(1))
+    kept = z_return(0)
+    steps = exchange_z([kept[i] + crossed[i] for i in range(Z // 2)], SHIFTS_BACK)
+    others = swap_core(jnp.stack([step[1] for step in steps]))
+    filter_grad = pl.pallas_call(
+        filter_sum_kernel,
+        out_shape=f32(*tile),
+        in_specs=[VMEM] * 5,
         out_specs=VMEM,
         compiler_params=PARAMS,
-    )(scalar, other, partial)
-    blocks = lax.all_to_all(blocks, "z", 0, 0, tiled=True)
-    filter_grad = jnp.sum(blocks[:, 2], axis=0)
+    )(*steps, others)
+    input_grad = pl.pallas_call(
+        finish_kernel,
+        out_shape=f32(Z, 2, *tile),
+        in_specs=[SMEM] * 3 + [VMEM] * 6,
+        out_specs=VMEM,
+        compiler_params=PARAMS,
+    )(scalar, zone.reshape(1), skip_gain, packed, *steps, others)
     across = pair_y(filter_grad, lambda i: i ^ 2)
     far = pair_y(filter_grad, lambda i: Y - 1 - i)
     near = pair_y(filter_grad, lambda i: i ^ 1)
     filter_grad = (filter_grad + near) + (far + across)
-    input_grad = blocks[:, :2] + skipped
     return (input_grad.reshape(out_grad.shape), filter_grad.reshape(filter_taps.shape))
 
 

time: 71.4 us -> 69.5 us (0.973)
  blocking collectives: 32.9 us -> 0 us
  starting transfers between devices: 18.6 us -> 36.2 us
  waiting for transfers between devices: 11 us -> 24.5 us
    all_to_all x2 -> x0, blocking collectives: 32.9 us -> none  [the longest x1 20.5 us: per_device(): blocks = lax.all_to_all(packed, 'z', 0, 0, tiled=True)]
    ppermute x0 -> x8, starting transfers between devices: none -> 14.1 us  [shift_z(): return lax.ppermute(value, ('z', 'c'), pairs)]
    ppermute x0 -> x8, waiting for transfers between devices: none -> 10.3 us  [shift_z(): return lax.ppermute(value, ('z', 'c'), pairs)]
    ppermute x3 -> x5, starting transfers between devices: 5.12 us -> 9.08 us  [swap_core(): return lax.ppermute(value, 'c', [(0, 1), (1, 0)])]
    ppermute x3 -> x5, waiting for transfers between devices: 0.98 us -> 4.28 us  [swap_core(): return lax.ppermute(value, 'c', [(0, 1), (1, 0)])]
  transfers between devices with their start and end apart: 12 -> 22, of which waited for: 7 -> 15; matrix products, arithmetic and copies ran while one was open for 4% -> 4% of each run, Pallas kernels for 1% -> 1%
where the time goes in v3:
time: 69.5 us; the launch traced here: 69.3 us
  starting transfers between devices  36.2 us (52%)
  waiting for transfers between devices  24.5 us (35%)
  Pallas kernels  4.08 us (6%)
  local copies, waits for them, and re-layouts  2.84 us (4%)
  other arithmetic  0.83 us (1%)
  between operations  0.83 us (1%)
    ppermute x8, starting transfers between devices, shift_z(): return lax.ppermute(value, ('z', 'c'), pairs)  14.1 us
    ppermute x8, waiting for transfers between devices, shift_z(): return lax.ppermute(value, ('z', 'c'), pairs)  10.3 us
    ppermute x6, starting transfers between devices, shift_x(): return lax.ppermute(value, 'x', [(i, (i + shift) % X) for i in range(X)])  9.29 us
    ppermute x5, starting transfers between devices, swap_core(): return lax.ppermute(value, 'c', [(0, 1), (1, 0)])  9.08 us
    ppermute x6, waiting for transfers between devices, shift_x(): return lax.ppermute(value, 'x', [(i, (i + shift) % X) for i in range(X)])  8.27 us
    ppermute x5, waiting for transfers between devices, swap_core(): return lax.ppermute(value, 'c', [(0, 1), (1, 0)])  4.28 us
    ppermute x3, starting transfers between devices, pair_y(): return lax.ppermute(value, 'y', [(i, partner(i)) for i in range(Y)])  3.69 us
    squeeze x2, local copies, waits for them, and re-layouts, mine(): lax.dynamic_index_in_dim(jnp.asarray(table), place, 0, keepdims=False)  2 us
  transfers between devices with their start and end apart: 22, of which 15 were waited for; matrix products, arithmetic and copies ran while one was open for 4% of the time, Pallas kernels for 1%

profile of v3, /device:TPU:1, one launch (start us, length us, event | category | flops | bytes accessed | tf_op | source)
XLA Modules:
  0.0 69.3 jit_solution(6082061474166453362)
XLA Ops:
  0.7 1.0 %shard_map.86.packed_ref = f32[8,5,16,128]{3,2,1,0:T(8,128)S(1)} custom-call(s32[1]{0:T(128)} %bitcast.place_ref, f32[1,16,2048]{2,1,0:T(8,128)} %grad_hbm.1, f32[1,16,2048]{2,1,0:T(8,128)} %input_hbm.1, f32[16,128]{1,0:T(8,128)} %bitcast.31), custom_call_target="tpu_custom_call" | custom-call | tf_op jit(solution)/shard_map/pallas_call | solution.py:274
  1.7 0.0 copy-start
  1.8 3.3 %collective-permute-start = (f32[4,5,16,128]{3,2,1,0:T(8,128)S(1)}, f32[4,5,16,128]{3,2,1,0:T(8,128)S(1)}, u32[]{:S(2)}, u32[]{:S(2)}) collective-permute-start(f32[4,5,16,128]{3,2,1,0:T(8,128)S(1)} %pad_maximum_fusion.2), channel_id=1, source_target_pairs={{0,1},{1,0},{2,3},{3,2},{4,5},{5,4},{6,7},{7,6},{8,9},{9,8},{10,11... | collective-permute-start | bytes 491528 | tf_op jit(solution)/shard_map/ppermute | solution.py:256
  5.1 1.0 %collective-permute-done = f32[4,5,16,128]{3,2,1,0:T(8,128)S(1)} collective-permute-done((f32[4,5,16,128]{3,2,1,0:T(8,128)S(1)}, f32[4,5,16,128]{3,2,1,0:T(8,128)S(1)}, u32[]{:S(2)}, u32[]{:S(2)}) %collective-permute-start) | collective-permute-done | bytes 163872 | tf_op jit(solution)/shard_map/ppermute | solution.py:256
  6.2 3.9 %collective-permute-start.4 = (f32[2,5,16,128]{3,2,1,0:T(8,128)S(1)}, f32[2,5,16,128]{3,2,1,0:T(8,128)S(1)}, u32[]{:S(2)}, u32[]{:S(2)}) collective-permute-start(f32[2,5,16,128]{3,2,1,0:T(8,128)S(1)} %pad_maximum_fusion.7), channel_id=1, source_target_pairs={{0,56},{8,0},{16,8},{24,16},{32,24},{40,32},{48,40},{56,48},{1,57}... | collective-permute-start | bytes 245768 | tf_op jit(solution)/shard_map/ppermute | solution.py:252
  10.1 1.4 %collective-permute-start.1 = (f32[2,5,16,128]{3,2,1,0:T(8,128)S(1)}, f32[2,5,16,128]{3,2,1,0:T(8,128)S(1)}, u32[]{:S(2)}, u32[]{:S(2)}) collective-permute-start(f32[2,5,16,128]{3,2,1,0:T(8,128)S(1)} %pad_maximum_fusion.4), channel_id=1, source_target_pairs={{0,24},{8,32},{16,40},{24,48},{32,56},{40,0},{48,8},{56,16},{1,33}... | collective-permute-start | bytes 245768 | tf_op jit(solution)/shard_map/ppermute | solution.py:252
  11.5 0.4 collective-permute-start.2
  11.9 1.6 %collective-permute-start.3 = (f32[2,5,16,128]{3,2,1,0:T(8,128)S(1)}, f32[2,5,16,128]{3,2,1,0:T(8,128)S(1)}, u32[]{:S(2)}, u32[]{:S(2)}) collective-permute-start(f32[2,5,16,128]{3,2,1,0:T(8,128)S(1)} %pad_maximum_fusion.6), channel_id=1, source_target_pairs={{0,8},{8,16},{16,24},{24,32},{32,40},{40,48},{48,56},{56,0},{1,17}... | collective-permute-start | bytes 245768 | tf_op jit(solution)/shard_map/ppermute | solution.py:252
  13.5 0.0 collective-permute-done.4
  13.5 5.1 %collective-permute-done.1.m0 = f32[2,5,16,128]{3,2,1,0:T(8,128)S(1)} collective-permute-done((f32[2,5,16,128]{3,2,1,0:T(8,128)S(1)}, f32[2,5,16,128]{3,2,1,0:T(8,128)S(1)}, u32[]{:S(2)}, u32[]{:S(2)}) %collective-permute-start.1) | collective-permute-done | bytes 81952 | tf_op jit(solution)/shard_map/ppermute | solution.py:252
  18.6 0.9 %collective-permute-done.2.m1 = f32[2,5,16,128]{3,2,1,0:T(8,128)S(1)} collective-permute-done((f32[2,5,16,128]{3,2,1,0:T(8,128)S(1)}, f32[2,5,16,128]{3,2,1,0:T(8,128)S(1)}, u32[]{:S(2)}, u32[]{:S(2)}) %collective-permute-start.2) | collective-permute-done | bytes 81952 | tf_op jit(solution)/shard_map/ppermute | solution.py:252
  19.5 0.0 collective-permute-done.3.m2
  19.5 0.2 shard_map.88
  19.8 2.2 %collective-permute-start.7 = (f32[3,2,5,2,16,128]{5,4,3,2,1,0:T(8,128)S(1)}, f32[3,2,5,2,16,128]{5,4,3,2,1,0:T(8,128)S(1)}, u32[]{:S(2)}, u32[]{:S(2)}) collective-permute-start(f32[3,2,5,2,16,128]{5,4,3,2,1,0:T(8,128)S(1)} %slice.139), channel_id=1, source_target_pairs={{0,1},{1,0},{2,3},{3,2},{4,5},{5,4},{6,7},{7,6},{8,9},{9,8},{10,11... | collective-permute-start | bytes 1474568 | tf_op jit(solution)/shard_map/ppermute | solution.py:256
  22.0 0.1 collective-permute-start.5
  22.1 0.2 shard_map.87
  22.3 1.4 %collective-permute-done.5 = f32[2,5,2,16,128]{4,3,2,1,0:T(8,128)S(1)} collective-permute-done((f32[2,5,2,16,128]{4,3,2,1,0:T(8,128)S(1)}, f32[2,5,2,16,128]{4,3,2,1,0:T(8,128)S(1)}, u32[]{:S(2)}, u32[]{:S(2)}) %collective-permute-start.5) | collective-permute-done | bytes 163872 | tf_op jit(solution)/shard_map/ppermute | solution.py:256
  23.7 0.0 copy-start.1
  23.7 2.8 %collective-permute-start.6 = (f32[2,5,2,16,128]{4,3,2,1,0:T(8,128)S(1)}, f32[2,5,2,16,128]{4,3,2,1,0:T(8,128)S(1)}, u32[]{:S(2)}, u32[]{:S(2)}) collective-permute-start(f32[2,5,2,16,128]{4,3,2,1,0:T(8,128)S(1)} %fusion.3), channel_id=1, source_target_pairs={{0,4},{2,6},{4,0},{6,2},{1,5},{3,7},{5,1},{7,3},{8,12},{10,14},{12... | collective-permute-start | bytes 491528 | tf_op jit(solution)/shard_map/ppermute | solution.py:247
  26.6 0.0 collective-permute-done.7
  26.6 0.1 fusion
  26.6 0.9 %collective-permute-start.9 = (f32[2,5,2,16,128]{4,3,2,1,0:T(8,128)S(1)}, f32[2,5,2,16,128]{4,3,2,1,0:T(8,128)S(1)}, u32[]{:S(2)}, u32[]{:S(2)}) collective-permute-start(f32[2,5,2,16,128]{4,3,2,1,0:T(8,128)S(1)} %get-tuple-element.8), channel_id=1, source_target_pairs={{0,6},{2,0},{4,2},{6,4},{1,7},{3,1},{5,3},{7,5},{8,14},{10,8},{12,... | collective-permute-start | bytes 491528 | tf_op jit(solution)/shard_map/ppermute | solution.py:247
  27.6 0.6 collective-permute-start.8
  28.2 0.9 %dynamic-slice_bitcast_fusion.1.tw = f32[2,128,128]{2,1,0:T(8,128)S(1)} fusion(f32[8,2,128,128]{3,2,1,0:T(8,128)} %constant.63.clone, s32[]{:T(128)S(6)} %select_n.90), kind=kLoop, calls=%fused_computation.13 | loop fusion | bytes 262148 | tf_op jit(solution)/shard_map/jit(dynamic_index_in_dim)/squeeze | solution.py:267
  29.1 1.1 %dynamic-slice_bitcast_fusion.left = bf16[4,256,256]{2,1,0:T(8,128)(2,1)S(1)} fusion(bf16[8,4,256,256]{3,2,1,0:T(8,128)(2,1)} %constant.62.clone, s32[]{:T(128)S(6)} %select_n.90), kind=kLoop, calls=%fused_computation | loop fusion | bytes 1048580 | tf_op jit(solution)/shard_map/jit(dynamic_index_in_dim)/squeeze | solution.py:267
  30.2 0.6 collective-permute-done.6.x0
  30.7 3.6 %collective-permute-done.9.x3 = f32[2,5,2,16,128]{4,3,2,1,0:T(8,128)S(1)} collective-permute-done((f32[2,5,2,16,128]{4,3,2,1,0:T(8,128)S(1)}, f32[2,5,2,16,128]{4,3,2,1,0:T(8,128)S(1)}, u32[]{:S(2)}, u32[]{:S(2)}) %collective-permute-start.9) | collective-permute-done | bytes 163872 | tf_op jit(solution)/shard_map/ppermute | solution.py:247
  34.4 0.0 collective-permute-done.8.x2
  34.4 0.0 copy-done
  34.4 1.7 %shard_map.89 = (f32[2,3,2,16,128]{4,3,2,1,0:T(8,128)S(1)}, f32[2,3,2,16,128]{4,3,2,1,0:T(8,128)S(1)}, f32[2,3,2,16,128]{4,3,2,1,0:T(8,128)S(1)}, f32[2,3,2,16,128]{4,3,2,1,0:T(8,128)S(1)}) custom-call(f32[2,5,2,16,128]{4,3,2,1,0:T(8,128)S(1)} %collective-permute-done.6.x0, f32[2,5,2,16,128]{4,3,2,1,0:T(8,128)S(1)} %get-tuple-element.16.x1, ...), custom_call_target="tpu_custom_call" | custom-call | tf_op jit(solution)/shard_map/pallas_call | solution.py:322
  36.2 3.4 %collective-permute-start.10 = (f32[2,3,2,16,128]{4,3,2,1,0:T(8,128)S(1)}, f32[2,3,2,16,128]{4,3,2,1,0:T(8,128)S(1)}, u32[]{:S(2)}, u32[]{:S(2)}) collective-permute-start(f32[2,3,2,16,128]{4,3,2,1,0:T(8,128)S(1)} %get-tuple-element.11), channel_id=1, source_target_pairs={{0,4},{2,6},{4,0},{6,2},{1,5},{3,7},{5,1},{7,3},{8,12},{10,14},{12... | collective-permute-start | bytes 294920 | tf_op jit(solution)/shard_map/ppermute | solution.py:247
  39.6 0.9 %collective-permute-start.11 = (f32[2,3,2,16,128]{4,3,2,1,0:T(8,128)S(1)}, f32[2,3,2,16,128]{4,3,2,1,0:T(8,128)S(1)}, u32[]{:S(2)}, u32[]{:S(2)}) collective-permute-start(f32[2,3,2,16,128]{4,3,2,1,0:T(8,128)S(1)} %get-tuple-element.12), channel_id=1, source_target_pairs={{0,6},{2,0},{4,2},{6,4},{1,7},{3,1},{5,3},{7,5},{8,14},{10,8},{12,... | collective-permute-start | bytes 294920 | tf_op jit(solution)/shard_map/ppermute | solution.py:247
  40.5 0.6 collective-permute-start.12
  41.1 0.5 collective-permute-done.10
  41.6 2.9 %collective-permute-done.11 = f32[2,3,2,16,128]{4,3,2,1,0:T(8,128)S(1)} collective-permute-done((f32[2,3,2,16,128]{4,3,2,1,0:T(8,128)S(1)}, f32[2,3,2,16,128]{4,3,2,1,0:T(8,128)S(1)}, u32[]{:S(2)}, u32[]{:S(2)}) %collective-permute-start.11) | collective-permute-done | bytes 98336 | tf_op jit(solution)/shard_map/ppermute | solution.py:247
  44.5 0.7 %collective-permute-done.12 = f32[2,3,2,16,128]{4,3,2,1,0:T(8,128)S(1)} collective-permute-done((f32[2,3,2,16,128]{4,3,2,1,0:T(8,128)S(1)}, f32[2,3,2,16,128]{4,3,2,1,0:T(8,128)S(1)}, u32[]{:S(2)}, u32[]{:S(2)}) %collective-permute-start.12) | collective-permute-done | bytes 98336 | tf_op jit(solution)/shard_map/ppermute | solution.py:247
  45.2 0.2 shard_map.91
  45.4 2.5 %collective-permute-start.13 = (f32[4,2,3,16,128]{4,3,2,1,0:T(8,128)S(1)}, f32[4,2,3,16,128]{4,3,2,1,0:T(8,128)S(1)}, u32[]{:S(2)}, u32[]{:S(2)}) collective-permute-start(f32[4,2,3,16,128]{4,3,2,1,0:T(8,128)S(1)} %shard_map.91), channel_id=1, source_target_pairs={{0,1},{1,0},{2,3},{3,2},{4,5},{5,4},{6,7},{7,6},{8,9},{9,8},{10,11... | collective-permute-start | bytes 589832 | tf_op jit(solution)/shard_map/ppermute | solution.py:256
  47.9 0.1 shard_map.90
  48.0 0.9 %collective-permute-done.13 = f32[4,2,3,16,128]{4,3,2,1,0:T(8,128)S(1)} collective-permute-done((f32[4,2,3,16,128]{4,3,2,1,0:T(8,128)S(1)}, f32[4,2,3,16,128]{4,3,2,1,0:T(8,128)S(1)}, u32[]{:S(2)}, u32[]{:S(2)}) %collective-permute-start.13) | collective-permute-done | bytes 196640 | tf_op jit(solution)/shard_map/ppermute | solution.py:256
  49.0 1.3 %collective-permute-start.17 = (f32[2,3,16,128]{3,2,1,0:T(8,128)S(1)}, f32[2,3,16,128]{3,2,1,0:T(8,128)S(1)}, u32[]{:S(2)}, u32[]{:S(2)}) collective-permute-start(f32[2,3,16,128]{3,2,1,0:T(8,128)S(1)} %get-tuple-element.17), channel_id=1, source_target_pairs={{0,56},{8,0},{16,8},{24,16},{32,24},{40,32},{48,40},{56,48},{1,57}... | collective-permute-start | bytes 147464 | tf_op jit(solution)/shard_map/ppermute | solution.py:252
  50.3 3.3 %collective-permute-start.16 = (f32[2,3,16,128]{3,2,1,0:T(8,128)S(1)}, f32[2,3,16,128]{3,2,1,0:T(8,128)S(1)}, u32[]{:S(2)}, u32[]{:S(2)}) collective-permute-start(f32[2,3,16,128]{3,2,1,0:T(8,128)S(1)} %get-tuple-element.18), channel_id=1, source_target_pairs={{0,24},{8,32},{16,40},{24,48},{32,56},{40,0},{48,8},{56,16},{1,33}... | collective-permute-start | bytes 147464 | tf_op jit(solution)/shard_map/ppermute | solution.py:252
  53.7 1.1 %collective-permute-start.15 = (f32[2,3,16,128]{3,2,1,0:T(8,128)S(1)}, f32[2,3,16,128]{3,2,1,0:T(8,128)S(1)}, u32[]{:S(2)}, u32[]{:S(2)}) collective-permute-start(f32[2,3,16,128]{3,2,1,0:T(8,128)S(1)} %get-tuple-element.19), channel_id=1, source_target_pairs={{0,48},{8,56},{16,0},{24,8},{32,16},{40,24},{48,32},{56,40},{1,41}... | collective-permute-start | bytes 147464 | tf_op jit(solution)/shard_map/ppermute | solution.py:252
  54.8 1.1 %collective-permute-start.14 = (f32[2,3,16,128]{3,2,1,0:T(8,128)S(1)}, f32[2,3,16,128]{3,2,1,0:T(8,128)S(1)}, u32[]{:S(2)}, u32[]{:S(2)}) collective-permute-start(f32[2,3,16,128]{3,2,1,0:T(8,128)S(1)} %get-tuple-element.20), channel_id=1, source_target_pairs={{0,8},{8,16},{16,24},{24,32},{32,40},{40,48},{48,56},{56,0},{1,17}... | collective-permute-start | bytes 147464 | tf_op jit(solution)/shard_map/ppermute | solution.py:252
  55.9 0.0 collective-permute-done.17
  55.9 1.8 %collective-permute-done.16.r2 = f32[2,3,16,128]{3,2,1,0:T(8,128)S(1)} collective-permute-done((f32[2,3,16,128]{3,2,1,0:T(8,128)S(1)}, f32[2,3,16,128]{3,2,1,0:T(8,128)S(1)}, u32[]{:S(2)}, u32[]{:S(2)}) %collective-permute-start.16) | collective-permute-done | bytes 49184 | tf_op jit(solution)/shard_map/ppermute | solution.py:252
  57.7 0.9 %collective-permute-done.15.r1 = f32[2,3,16,128]{3,2,1,0:T(8,128)S(1)} collective-permute-done((f32[2,3,16,128]{3,2,1,0:T(8,128)S(1)}, f32[2,3,16,128]{3,2,1,0:T(8,128)S(1)}, u32[]{:S(2)}, u32[]{:S(2)}) %collective-permute-start.15) | collective-permute-done | bytes 49184 | tf_op jit(solution)/shard_map/ppermute | solution.py:252
  58.6 1.6 %collective-permute-done.14.r0 = f32[2,3,16,128]{3,2,1,0:T(8,128)S(1)} collective-permute-done((f32[2,3,16,128]{3,2,1,0:T(8,128)S(1)}, f32[2,3,16,128]{3,2,1,0:T(8,128)S(1)}, u32[]{:S(2)}, u32[]{:S(2)}) %collective-permute-start.14) | collective-permute-done | bytes 49184 | tf_op jit(solution)/shard_map/ppermute | solution.py:252
  60.2 0.9 %collective-permute-start.18 = (f32[4,3,16,128]{3,2,1,0:T(8,128)S(1)}, f32[4,3,16,128]{3,2,1,0:T(8,128)S(1)}, u32[]{:S(2)}, u32[]{:S(2)}) collective-permute-start(f32[4,3,16,128]{3,2,1,0:T(8,128)S(1)} %pad_maximum_fusion.3), channel_id=1, source_target_pairs={{0,1},{1,0},{2,3},{3,2},{4,5},{5,4},{6,7},{7,6},{8,9},{9,8},{10,11... | collective-permute-start | bytes 294920 | tf_op jit(solution)/shard_map/ppermute | solution.py:256
  61.1 0.9 %collective-permute-done.18.other_ref = f32[4,3,16,128]{3,2,1,0:T(8,128)S(1)} collective-permute-done((f32[4,3,16,128]{3,2,1,0:T(8,128)S(1)}, f32[4,3,16,128]{3,2,1,0:T(8,128)S(1)}, u32[]{:S(2)}, u32[]{:S(2)}) %collective-permute-start.18) | collective-permute-done | bytes 98336 | tf_op jit(solution)/shard_map/ppermute | solution.py:256
  62.1 2.9 %collective-permute-start.21 = (f32[16,128]{1,0:T(8,128)S(1)}, f32[16,128]{1,0:T(8,128)S(1)}, u32[]{:S(2)}, u32[]{:S(2)}) collective-permute-start(f32[16,128]{1,0:T(8,128)S(1)} %shard_map.93), channel_id=1, source_target_pairs={{0,128},{64,192},{128,0},{192,64},{1,129},{65,193},{129,1},{193,65... | collective-permute-start | bytes 24584 | tf_op jit(solution)/shard_map/ppermute | solution.py:260
  65.0 0.8 %collective-permute-start.20 = (f32[16,128]{1,0:T(8,128)S(1)}, f32[16,128]{1,0:T(8,128)S(1)}, u32[]{:S(2)}, u32[]{:S(2)}) collective-permute-start(f32[16,128]{1,0:T(8,128)S(1)} %shard_map.93), channel_id=1, source_target_pairs={{0,192},{64,128},{128,64},{192,0},{1,193},{65,129},{129,65},{193,1... | collective-permute-start | bytes 24584 | tf_op jit(solution)/shard_map/ppermute | solution.py:260
  65.8 0.0 collective-permute-start.19
  65.8 0.0 copy-done.1
  65.8 0.6 shard_map.92
  66.3 0.7 reshape.33
  67.0 0.0 collective-permute-done.21
  67.0 1.7 %collective-permute-done.20 = f32[16,128]{1,0:T(8,128)S(1)} collective-permute-done((f32[16,128]{1,0:T(8,128)S(1)}, f32[16,128]{1,0:T(8,128)S(1)}, u32[]{:S(2)}, u32[]{:S(2)}) %collective-permute-start.20) | collective-permute-done | bytes 8224 | tf_op jit(solution)/shard_map/ppermute | solution.py:260
  68.7 0.0 collective-permute-done.19
  68.7 0.6 add_bitcast_fusion
  (24 shorter events, 0.3 us)
Async XLA Ops:
  1.7 32.7 %copy-start = (bf16[4,256,256]{2,1,0:T(8,128)(2,1)S(1)}, bf16[4,256,256]{2,1,0:T(8,128)(2,1)}, u32[]{:S(2)}) copy-start(bf16[4,256,256]{2,1,0:T(8,128)(2,1)} %constant.61.clone.right) | copy-start | bytes 1572868
  1.8 4.4 %collective-permute-start = (f32[4,5,16,128]{3,2,1,0:T(8,128)S(1)}, f32[4,5,16,128]{3,2,1,0:T(8,128)S(1)}, u32[]{:S(2)}, u32[]{:S(2)}) collective-permute-start(f32[4,5,16,128]{3,2,1,0:T(8,128)S(1)} %pad_maximum_fusion.2), channel_id=1, source_target_pairs={{0,1},{1,0},{2,3},{3,2},{4,5},{5,4},{6,7},{7,6},{8,9},{9,8},{10,11... | collective-permute-start | bytes 491528 | tf_op jit(solution)/shard_map/ppermute | solution.py:256
  6.2 7.3 %collective-permute-start.4 = (f32[2,5,16,128]{3,2,1,0:T(8,128)S(1)}, f32[2,5,16,128]{3,2,1,0:T(8,128)S(1)}, u32[]{:S(2)}, u32[]{:S(2)}) collective-permute-start(f32[2,5,16,128]{3,2,1,0:T(8,128)S(1)} %pad_maximum_fusion.7), channel_id=1, source_target_pairs={{0,56},{8,0},{16,8},{24,16},{32,24},{40,32},{48,40},{56,48},{1,57}... | collective-permute-start | bytes 245768 | tf_op jit(solution)/shard_map/ppermute | solution.py:252
  10.1 8.5 %collective-permute-start.1 = (f32[2,5,16,128]{3,2,1,0:T(8,128)S(1)}, f32[2,5,16,128]{3,2,1,0:T(8,128)S(1)}, u32[]{:S(2)}, u32[]{:S(2)}) collective-permute-start(f32[2,5,16,128]{3,2,1,0:T(8,128)S(1)} %pad_maximum_fusion.4), channel_id=1, source_target_pairs={{0,24},{8,32},{16,40},{24,48},{32,56},{40,0},{48,8},{56,16},{1,33}... | collective-permute-start | bytes 245768 | tf_op jit(solution)/shard_map/ppermute | solution.py:252
  11.5 8.0 %collective-permute-start.2 = (f32[2,5,16,128]{3,2,1,0:T(8,128)S(1)}, f32[2,5,16,128]{3,2,1,0:T(8,128)S(1)}, u32[]{:S(2)}, u32[]{:S(2)}) collective-permute-start(f32[2,5,16,128]{3,2,1,0:T(8,128)S(1)} %pad_maximum_fusion.5), channel_id=1, source_target_pairs={{0,48},{8,56},{16,0},{24,8},{32,16},{40,24},{48,32},{56,40},{1,41}... | collective-permute-start | bytes 245768 | tf_op jit(solution)/shard_map/ppermute | solution.py:252
  11.9 7.6 %collective-permute-start.3 = (f32[2,5,16,128]{3,2,1,0:T(8,128)S(1)}, f32[2,5,16,128]{3,2,1,0:T(8,128)S(1)}, u32[]{:S(2)}, u32[]{:S(2)}) collective-permute-start(f32[2,5,16,128]{3,2,1,0:T(8,128)S(1)} %pad_maximum_fusion.6), channel_id=1, source_target_pairs={{0,8},{8,16},{16,24},{24,32},{32,40},{40,48},{48,56},{56,0},{1,17}... | collective-permute-start | bytes 245768 | tf_op jit(solution)/shard_map/ppermute | solution.py:252
  19.8 6.8 %collective-permute-start.7 = (f32[3,2,5,2,16,128]{5,4,3,2,1,0:T(8,128)S(1)}, f32[3,2,5,2,16,128]{5,4,3,2,1,0:T(8,128)S(1)}, u32[]{:S(2)}, u32[]{:S(2)}) collective-permute-start(f32[3,2,5,2,16,128]{5,4,3,2,1,0:T(8,128)S(1)} %slice.139), channel_id=1, source_target_pairs={{0,1},{1,0},{2,3},{3,2},{4,5},{5,4},{6,7},{7,6},{8,9},{9,8},{10,11... | collective-permute-start | bytes 1474568 | tf_op jit(solution)/shard_map/ppermute | solution.py:256
  22.0 1.7 %collective-permute-start.5 = (f32[2,5,2,16,128]{4,3,2,1,0:T(8,128)S(1)}, f32[2,5,2,16,128]{4,3,2,1,0:T(8,128)S(1)}, u32[]{:S(2)}, u32[]{:S(2)}) collective-permute-start(f32[2,5,2,16,128]{4,3,2,1,0:T(8,128)S(1)} %slice_bitcast_fusion), channel_id=1, source_target_pairs={{0,1},{1,0},{2,3},{3,2},{4,5},{5,4},{6,7},{7,6},{8,9},{9,8},{10,11... | collective-permute-start | bytes 491528 | tf_op jit(solution)/shard_map/ppermute | solution.py:256
  23.7 42.0 %copy-start.1 = (f32[16]{0:T(128)S(1)}, f32[16]{0:T(128)}, u32[]{:S(2)}) copy-start(f32[16]{0:T(128)} %skip_ref.1) | copy-start | bytes 196
  23.7 7.0 %collective-permute-start.6 = (f32[2,5,2,16,128]{4,3,2,1,0:T(8,128)S(1)}, f32[2,5,2,16,128]{4,3,2,1,0:T(8,128)S(1)}, u32[]{:S(2)}, u32[]{:S(2)}) collective-permute-start(f32[2,5,2,16,128]{4,3,2,1,0:T(8,128)S(1)} %fusion.3), channel_id=1, source_target_pairs={{0,4},{2,6},{4,0},{6,2},{1,5},{3,7},{5,1},{7,3},{8,12},{10,14},{12... | collective-permute-start | bytes 491528 | tf_op jit(solution)/shard_map/ppermute | solution.py:247
  26.6 7.7 %collective-permute-start.9 = (f32[2,5,2,16,128]{4,3,2,1,0:T(8,128)S(1)}, f32[2,5,2,16,128]{4,3,2,1,0:T(8,128)S(1)}, u32[]{:S(2)}, u32[]{:S(2)}) collective-permute-start(f32[2,5,2,16,128]{4,3,2,1,0:T(8,128)S(1)} %get-tuple-element.8), channel_id=1, source_target_pairs={{0,6},{2,0},{4,2},{6,4},{1,7},{3,1},{5,3},{7,5},{8,14},{10,8},{12,... | collective-permute-start | bytes 491528 | tf_op jit(solution)/shard_map/ppermute | solution.py:247
  27.6 6.8 %collective-permute-start.8 = (f32[2,5,2,16,128]{4,3,2,1,0:T(8,128)S(1)}, f32[2,5,2,16,128]{4,3,2,1,0:T(8,128)S(1)}, u32[]{:S(2)}, u32[]{:S(2)}) collective-permute-start(f32[2,5,2,16,128]{4,3,2,1,0:T(8,128)S(1)} %get-tuple-element.15), channel_id=1, source_target_pairs={{0,2},{2,4},{4,6},{6,0},{1,3},{3,5},{5,7},{7,1},{8,10},{10,12},{12... | collective-permute-start | bytes 491528 | tf_op jit(solution)/shard_map/ppermute | solution.py:247
  36.2 5.4 %collective-permute-start.10 = (f32[2,3,2,16,128]{4,3,2,1,0:T(8,128)S(1)}, f32[2,3,2,16,128]{4,3,2,1,0:T(8,128)S(1)}, u32[]{:S(2)}, u32[]{:S(2)}) collective-permute-start(f32[2,3,2,16,128]{4,3,2,1,0:T(8,128)S(1)} %get-tuple-element.11), channel_id=1, source_target_pairs={{0,4},{2,6},{4,0},{6,2},{1,5},{3,7},{5,1},{7,3},{8,12},{10,14},{12... | collective-permute-start | bytes 294920 | tf_op jit(solution)/shard_map/ppermute | solution.py:247
  39.6 4.9 %collective-permute-start.11 = (f32[2,3,2,16,128]{4,3,2,1,0:T(8,128)S(1)}, f32[2,3,2,16,128]{4,3,2,1,0:T(8,128)S(1)}, u32[]{:S(2)}, u32[]{:S(2)}) collective-permute-start(f32[2,3,2,16,128]{4,3,2,1,0:T(8,128)S(1)} %get-tuple-element.12), channel_id=1, source_target_pairs={{0,6},{2,0},{4,2},{6,4},{1,7},{3,1},{5,3},{7,5},{8,14},{10,8},{12,... | collective-permute-start | bytes 294920 | tf_op jit(solution)/shard_map/ppermute | solution.py:247
  40.5 4.7 %collective-permute-start.12 = (f32[2,3,2,16,128]{4,3,2,1,0:T(8,128)S(1)}, f32[2,3,2,16,128]{4,3,2,1,0:T(8,128)S(1)}, u32[]{:S(2)}, u32[]{:S(2)}) collective-permute-start(f32[2,3,2,16,128]{4,3,2,1,0:T(8,128)S(1)} %get-tuple-element.13), channel_id=1, source_target_pairs={{0,2},{2,4},{4,6},{6,0},{1,3},{3,5},{5,7},{7,1},{8,10},{10,12},{12... | collective-permute-start | bytes 294920 | tf_op jit(solution)/shard_map/ppermute | solution.py:247
  45.4 3.6 %collective-permute-start.13 = (f32[4,2,3,16,128]{4,3,2,1,0:T(8,128)S(1)}, f32[4,2,3,16,128]{4,3,2,1,0:T(8,128)S(1)}, u32[]{:S(2)}, u32[]{:S(2)}) collective-permute-start(f32[4,2,3,16,128]{4,3,2,1,0:T(8,128)S(1)} %shard_map.91), channel_id=1, source_target_pairs={{0,1},{1,0},{2,3},{3,2},{4,5},{5,4},{6,7},{7,6},{8,9},{9,8},{10,11... | collective-permute-start | bytes 589832 | tf_op jit(solution)/shard_map/ppermute | solution.py:256
  49.0 6.8 %collective-permute-start.17 = (f32[2,3,16,128]{3,2,1,0:T(8,128)S(1)}, f32[2,3,16,128]{3,2,1,0:T(8,128)S(1)}, u32[]{:S(2)}, u32[]{:S(2)}) collective-permute-start(f32[2,3,16,128]{3,2,1,0:T(8,128)S(1)} %get-tuple-element.17), channel_id=1, source_target_pairs={{0,56},{8,0},{16,8},{24,16},{32,24},{40,32},{48,40},{56,48},{1,57}... | collective-permute-start | bytes 147464 | tf_op jit(solution)/shard_map/ppermute | solution.py:252
  50.3 7.4 %collective-permute-start.16 = (f32[2,3,16,128]{3,2,1,0:T(8,128)S(1)}, f32[2,3,16,128]{3,2,1,0:T(8,128)S(1)}, u32[]{:S(2)}, u32[]{:S(2)}) collective-permute-start(f32[2,3,16,128]{3,2,1,0:T(8,128)S(1)} %get-tuple-element.18), channel_id=1, source_target_pairs={{0,24},{8,32},{16,40},{24,48},{32,56},{40,0},{48,8},{56,16},{1,33}... | collective-permute-start | bytes 147464 | tf_op jit(solution)/shard_map/ppermute | solution.py:252
  53.7 4.9 %collective-permute-start.15 = (f32[2,3,16,128]{3,2,1,0:T(8,128)S(1)}, f32[2,3,16,128]{3,2,1,0:T(8,128)S(1)}, u32[]{:S(2)}, u32[]{:S(2)}) collective-permute-start(f32[2,3,16,128]{3,2,1,0:T(8,128)S(1)} %get-tuple-element.19), channel_id=1, source_target_pairs={{0,48},{8,56},{16,0},{24,8},{32,16},{40,24},{48,32},{56,40},{1,41}... | collective-permute-start | bytes 147464 | tf_op jit(solution)/shard_map/ppermute | solution.py:252
  54.8 5.4 %collective-permute-start.14 = (f32[2,3,16,128]{3,2,1,0:T(8,128)S(1)}, f32[2,3,16,128]{3,2,1,0:T(8,128)S(1)}, u32[]{:S(2)}, u32[]{:S(2)}) collective-permute-start(f32[2,3,16,128]{3,2,1,0:T(8,128)S(1)} %get-tuple-element.20), channel_id=1, source_target_pairs={{0,8},{8,16},{16,24},{24,32},{32,40},{40,48},{48,56},{56,0},{1,17}... | collective-permute-start | bytes 147464 | tf_op jit(solution)/shard_map/ppermute | solution.py:252
  60.2 1.9 %collective-permute-start.18 = (f32[4,3,16,128]{3,2,1,0:T(8,128)S(1)}, f32[4,3,16,128]{3,2,1,0:T(8,128)S(1)}, u32[]{:S(2)}, u32[]{:S(2)}) collective-permute-start(f32[4,3,16,128]{3,2,1,0:T(8,128)S(1)} %pad_maximum_fusion.3), channel_id=1, source_target_pairs={{0,1},{1,0},{2,3},{3,2},{4,5},{5,4},{6,7},{7,6},{8,9},{9,8},{10,11... | collective-permute-start | bytes 294920 | tf_op jit(solution)/shard_map/ppermute | solution.py:256
  62.1 5.0 %collective-permute-start.21 = (f32[16,128]{1,0:T(8,128)S(1)}, f32[16,128]{1,0:T(8,128)S(1)}, u32[]{:S(2)}, u32[]{:S(2)}) collective-permute-start(f32[16,128]{1,0:T(8,128)S(1)} %shard_map.93), channel_id=1, source_target_pairs={{0,128},{64,192},{128,0},{192,64},{1,129},{65,193},{129,1},{193,65... | collective-permute-start | bytes 24584 | tf_op jit(solution)/shard_map/ppermute | solution.py:260
  65.0 3.7 %collective-permute-start.20 = (f32[16,128]{1,0:T(8,128)S(1)}, f32[16,128]{1,0:T(8,128)S(1)}, u32[]{:S(2)}, u32[]{:S(2)}) collective-permute-start(f32[16,128]{1,0:T(8,128)S(1)} %shard_map.93), channel_id=1, source_target_pairs={{0,192},{64,128},{128,64},{192,0},{1,193},{65,129},{129,65},{193,1... | collective-permute-start | bytes 24584 | tf_op jit(solution)/shard_map/ppermute | solution.py:260
  65.8 2.9 %collective-permute-start.19 = (f32[16,128]{1,0:T(8,128)S(1)}, f32[16,128]{1,0:T(8,128)S(1)}, u32[]{:S(2)}, u32[]{:S(2)}) collective-permute-start(f32[16,128]{1,0:T(8,128)S(1)} %shard_map.93), channel_id=1, source_target_pairs={{0,64},{64,0},{128,192},{192,128},{1,65},{65,1},{129,193},{193,129... | collective-permute-start | bytes 24584 | tf_op jit(solution)/shard_map/ppermute | solution.py:260

commit v4 on v3

--- a/solution.py
+++ b/solution.py
@@ -12,7 +12,7 @@
 
 Y, Z, X, C = 4, 8, 4, 2
 ROWS_IN, ROWS_OUT = 5, 3
-SHIFTS, SHIFTS_BACK = ((3, 6, 1, 0), (4, 5, 2, 7)), ((1, 6, 3, 0), (2, 5, 4, 7))
+SHIFTS, SHIFTS_BACK = ((3, 6, 1, 0), (5, 2, 7, 4)), ((1, 6, 3, 0), (7, 2, 5, 4))
 KEPT, UNUSED = 3, 7
 ORDER_IN, ORDER_OUT = (2, 0, 1, 3), (0, 2, 1, 3)
 SUB, LANES = 16, 128

time: 69.5 us -> 69 us (level)
  waiting for transfers between devices: 24.5 us -> 22 us
  starting transfers between devices: 36.2 us -> 38.2 us
    ppermute x8, waiting for transfers between devices: 10.3 us -> 7.76 us  [shift_z(): return lax.ppermute(value, ('z', 'c'), pairs)]
    ppermute x8, starting transfers between devices: 14.1 us -> 16.1 us  [shift_z(): return lax.ppermute(value, ('z', 'c'), pairs)]
  transfers between devices with their start and end apart: 22 -> 22, of which waited for: 15 -> 18; matrix products, arithmetic and copies ran while one was open for 4% -> 4% of each run, Pallas kernels for 1% -> 1%
where the time goes in v4:
time: 69 us; the launch traced here: 68.8 us
  starting transfers between devices  38.2 us (55%)
  waiting for transfers between devices  22 us (32%)
  Pallas kernels  4.08 us (6%)
  local copies, waits for them, and re-layouts  2.84 us (4%)
  between operations  0.84 us (1%)
  other arithmetic  0.83 us (1%)
    ppermute x8, starting transfers between devices, shift_z(): return lax.ppermute(value, ('z', 'c'), pairs)  16.1 us
    ppermute x6, starting transfers between devices, shift_x(): return lax.ppermute(value, 'x', [(i, (i + shift) % X) for i in range(X)])  9.27 us
    ppermute x5, starting transfers between devices, swap_core(): return lax.ppermute(value, 'c', [(0, 1), (1, 0)])  9.11 us
    ppermute x6, waiting for transfers between devices, shift_x(): return lax.ppermute(value, 'x', [(i, (i + shift) % X) for i in range(X)])  8.28 us
    ppermute x8, waiting for transfers between devices, shift_z(): return lax.ppermute(value, ('z', 'c'), pairs)  7.76 us
    ppermute x5, waiting for transfers between devices, swap_core(): return lax.ppermute(value, 'c', [(0, 1), (1, 0)])  4.28 us
    ppermute x3, starting transfers between devices, pair_y(): return lax.ppermute(value, 'y', [(i, partner(i)) for i in range(Y)])  3.69 us
    squeeze x2, local copies, waits for them, and re-layouts, mine(): lax.dynamic_index_in_dim(jnp.asarray(table), place, 0, keepdims=False)  2 us
  transfers between devices with their start and end apart: 22, of which 18 were waited for; matrix products, arithmetic and copies ran while one was open for 4% of the time, Pallas kernels for 1%

profile of v4, /device:TPU:1, one launch (start us, length us, event | category | flops | bytes accessed | tf_op | source)
XLA Modules:
  0.0 68.8 jit_solution(3016323357353979688)
XLA Ops:
  0.7 1.0 %shard_map.86.packed_ref = f32[8,5,16,128]{3,2,1,0:T(8,128)S(1)} custom-call(s32[1]{0:T(128)} %bitcast.place_ref, f32[1,16,2048]{2,1,0:T(8,128)} %grad_hbm.1, f32[1,16,2048]{2,1,0:T(8,128)} %input_hbm.1, f32[16,128]{1,0:T(8,128)} %bitcast.31), custom_call_target="tpu_custom_call" | custom-call | tf_op jit(solution)/shard_map/pallas_call | solution.py:274
  1.7 0.0 copy-start
  1.8 3.3 %collective-permute-start = (f32[4,5,16,128]{3,2,1,0:T(8,128)S(1)}, f32[4,5,16,128]{3,2,1,0:T(8,128)S(1)}, u32[]{:S(2)}, u32[]{:S(2)}) collective-permute-start(f32[4,5,16,128]{3,2,1,0:T(8,128)S(1)} %pad_maximum_fusion.2), channel_id=1, source_target_pairs={{0,1},{1,0},{2,3},{3,2},{4,5},{5,4},{6,7},{7,6},{8,9},{9,8},{10,11... | collective-permute-start | bytes 491528 | tf_op jit(solution)/shard_map/ppermute | solution.py:256
  5.1 1.0 %collective-permute-done = f32[4,5,16,128]{3,2,1,0:T(8,128)S(1)} collective-permute-done((f32[4,5,16,128]{3,2,1,0:T(8,128)S(1)}, f32[4,5,16,128]{3,2,1,0:T(8,128)S(1)}, u32[]{:S(2)}, u32[]{:S(2)}) %collective-permute-start) | collective-permute-done | bytes 163872 | tf_op jit(solution)/shard_map/ppermute | solution.py:256
  6.2 5.3 %collective-permute-start.4 = (f32[2,5,16,128]{3,2,1,0:T(8,128)S(1)}, f32[2,5,16,128]{3,2,1,0:T(8,128)S(1)}, u32[]{:S(2)}, u32[]{:S(2)}) collective-permute-start(f32[2,5,16,128]{3,2,1,0:T(8,128)S(1)} %pad_maximum_fusion.7), channel_id=1, source_target_pairs={{0,56},{8,0},{16,8},{24,16},{32,24},{40,32},{48,40},{56,48},{1,33}... | collective-permute-start | bytes 245768 | tf_op jit(solution)/shard_map/ppermute | solution.py:252
  11.4 0.0 collective-permute-start.1
  11.5 1.9 %collective-permute-start.2 = (f32[2,5,16,128]{3,2,1,0:T(8,128)S(1)}, f32[2,5,16,128]{3,2,1,0:T(8,128)S(1)}, u32[]{:S(2)}, u32[]{:S(2)}) collective-permute-start(f32[2,5,16,128]{3,2,1,0:T(8,128)S(1)} %pad_maximum_fusion.5), channel_id=1, source_target_pairs={{0,48},{8,56},{16,0},{24,8},{32,16},{40,24},{48,32},{56,40},{1,17}... | collective-permute-start | bytes 245768 | tf_op jit(solution)/shard_map/ppermute | solution.py:252
  13.4 1.3 %collective-permute-start.3 = (f32[2,5,16,128]{3,2,1,0:T(8,128)S(1)}, f32[2,5,16,128]{3,2,1,0:T(8,128)S(1)}, u32[]{:S(2)}, u32[]{:S(2)}) collective-permute-start(f32[2,5,16,128]{3,2,1,0:T(8,128)S(1)} %pad_maximum_fusion.6), channel_id=1, source_target_pairs={{0,8},{8,16},{16,24},{24,32},{32,40},{40,48},{48,56},{56,0},{1,57}... | collective-permute-start | bytes 245768 | tf_op jit(solution)/shard_map/ppermute | solution.py:252
  14.7 1.6 %collective-permute-done.4 = f32[2,5,16,128]{3,2,1,0:T(8,128)S(1)} collective-permute-done((f32[2,5,16,128]{3,2,1,0:T(8,128)S(1)}, f32[2,5,16,128]{3,2,1,0:T(8,128)S(1)}, u32[]{:S(2)}, u32[]{:S(2)}) %collective-permute-start.4) | collective-permute-done | bytes 81952 | tf_op jit(solution)/shard_map/ppermute | solution.py:252
  16.3 1.1 %collective-permute-done.1.m0 = f32[2,5,16,128]{3,2,1,0:T(8,128)S(1)} collective-permute-done((f32[2,5,16,128]{3,2,1,0:T(8,128)S(1)}, f32[2,5,16,128]{3,2,1,0:T(8,128)S(1)}, u32[]{:S(2)}, u32[]{:S(2)}) %collective-permute-start.1) | collective-permute-done | bytes 81952 | tf_op jit(solution)/shard_map/ppermute | solution.py:252
  17.5 0.6 collective-permute-done.2.m1
  18.1 2.4 %collective-permute-done.3.m2 = f32[2,5,16,128]{3,2,1,0:T(8,128)S(1)} collective-permute-done((f32[2,5,16,128]{3,2,1,0:T(8,128)S(1)}, f32[2,5,16,128]{3,2,1,0:T(8,128)S(1)}, u32[]{:S(2)}, u32[]{:S(2)}) %collective-permute-start.3) | collective-permute-done | bytes 81952 | tf_op jit(solution)/shard_map/ppermute | solution.py:252
  20.5 0.2 shard_map.88
  20.7 1.4 %collective-permute-start.7 = (f32[3,2,5,2,16,128]{5,4,3,2,1,0:T(8,128)S(1)}, f32[3,2,5,2,16,128]{5,4,3,2,1,0:T(8,128)S(1)}, u32[]{:S(2)}, u32[]{:S(2)}) collective-permute-start(f32[3,2,5,2,16,128]{5,4,3,2,1,0:T(8,128)S(1)} %slice.139), channel_id=1, source_target_pairs={{0,1},{1,0},{2,3},{3,2},{4,5},{5,4},{6,7},{7,6},{8,9},{9,8},{10,11... | collective-permute-start | bytes 1474568 | tf_op jit(solution)/shard_map/ppermute | solution.py:256
  22.2 0.1 collective-permute-start.5
  22.3 0.2 shard_map.87
  22.5 1.4 %collective-permute-done.5 = f32[2,5,2,16,128]{4,3,2,1,0:T(8,128)S(1)} collective-permute-done((f32[2,5,2,16,128]{4,3,2,1,0:T(8,128)S(1)}, f32[2,5,2,16,128]{4,3,2,1,0:T(8,128)S(1)}, u32[]{:S(2)}, u32[]{:S(2)}) %collective-permute-start.5) | collective-permute-done | bytes 163872 | tf_op jit(solution)/shard_map/ppermute | solution.py:256
  23.9 0.0 copy-start.1
  23.9 2.8 %collective-permute-start.6 = (f32[2,5,2,16,128]{4,3,2,1,0:T(8,128)S(1)}, f32[2,5,2,16,128]{4,3,2,1,0:T(8,128)S(1)}, u32[]{:S(2)}, u32[]{:S(2)}) collective-permute-start(f32[2,5,2,16,128]{4,3,2,1,0:T(8,128)S(1)} %fusion.3), channel_id=1, source_target_pairs={{0,4},{2,6},{4,0},{6,2},{1,5},{3,7},{5,1},{7,3},{8,12},{10,14},{12... | collective-permute-start | bytes 491528 | tf_op jit(solution)/shard_map/ppermute | solution.py:247
  26.7 0.0 collective-permute-done.7
  26.7 0.1 fusion
  26.8 0.9 %collective-permute-start.9 = (f32[2,5,2,16,128]{4,3,2,1,0:T(8,128)S(1)}, f32[2,5,2,16,128]{4,3,2,1,0:T(8,128)S(1)}, u32[]{:S(2)}, u32[]{:S(2)}) collective-permute-start(f32[2,5,2,16,128]{4,3,2,1,0:T(8,128)S(1)} %get-tuple-element.8), channel_id=1, source_target_pairs={{0,6},{2,0},{4,2},{6,4},{1,7},{3,1},{5,3},{7,5},{8,14},{10,8},{12,... | collective-permute-start | bytes 491528 | tf_op jit(solution)/shard_map/ppermute | solution.py:247
  27.7 0.6 collective-permute-start.8
  28.3 0.9 %dynamic-slice_bitcast_fusion.1.tw = f32[2,128,128]{2,1,0:T(8,128)S(1)} fusion(f32[8,2,128,128]{3,2,1,0:T(8,128)} %constant.63.clone, s32[]{:T(128)S(6)} %select_n.90), kind=kLoop, calls=%fused_computation.13 | loop fusion | bytes 262148 | tf_op jit(solution)/shard_map/jit(dynamic_index_in_dim)/squeeze | solution.py:267
  29.3 1.1 %dynamic-slice_bitcast_fusion.left = bf16[4,256,256]{2,1,0:T(8,128)(2,1)S(1)} fusion(bf16[8,4,256,256]{3,2,1,0:T(8,128)(2,1)} %constant.62.clone, s32[]{:T(128)S(6)} %select_n.90), kind=kLoop, calls=%fused_computation | loop fusion | bytes 1048580 | tf_op jit(solution)/shard_map/jit(dynamic_index_in_dim)/squeeze | solution.py:267
  30.3 0.6 collective-permute-done.6.x0
  30.9 3.6 %collective-permute-done.9.x3 = f32[2,5,2,16,128]{4,3,2,1,0:T(8,128)S(1)} collective-permute-done((f32[2,5,2,16,128]{4,3,2,1,0:T(8,128)S(1)}, f32[2,5,2,16,128]{4,3,2,1,0:T(8,128)S(1)}, u32[]{:S(2)}, u32[]{:S(2)}) %collective-permute-start.9) | collective-permute-done | bytes 163872 | tf_op jit(solution)/shard_map/ppermute | solution.py:247
  34.5 0.1 collective-permute-done.8.x2
  34.6 0.0 copy-done
  34.6 1.7 %shard_map.89 = (f32[2,3,2,16,128]{4,3,2,1,0:T(8,128)S(1)}, f32[2,3,2,16,128]{4,3,2,1,0:T(8,128)S(1)}, f32[2,3,2,16,128]{4,3,2,1,0:T(8,128)S(1)}, f32[2,3,2,16,128]{4,3,2,1,0:T(8,128)S(1)}) custom-call(f32[2,5,2,16,128]{4,3,2,1,0:T(8,128)S(1)} %collective-permute-done.6.x0, f32[2,5,2,16,128]{4,3,2,1,0:T(8,128)S(1)} %get-tuple-element.16.x1, ...), custom_call_target="tpu_custom_call" | custom-call | tf_op jit(solution)/shard_map/pallas_call | solution.py:322
  36.3 3.4 %collective-permute-start.10 = (f32[2,3,2,16,128]{4,3,2,1,0:T(8,128)S(1)}, f32[2,3,2,16,128]{4,3,2,1,0:T(8,128)S(1)}, u32[]{:S(2)}, u32[]{:S(2)}) collective-permute-start(f32[2,3,2,16,128]{4,3,2,1,0:T(8,128)S(1)} %get-tuple-element.11), channel_id=1, source_target_pairs={{0,4},{2,6},{4,0},{6,2},{1,5},{3,7},{5,1},{7,3},{8,12},{10,14},{12... | collective-permute-start | bytes 294920 | tf_op jit(solution)/shard_map/ppermute | solution.py:247
  39.7 0.9 %collective-permute-start.11 = (f32[2,3,2,16,128]{4,3,2,1,0:T(8,128)S(1)}, f32[2,3,2,16,128]{4,3,2,1,0:T(8,128)S(1)}, u32[]{:S(2)}, u32[]{:S(2)}) collective-permute-start(f32[2,3,2,16,128]{4,3,2,1,0:T(8,128)S(1)} %get-tuple-element.12), channel_id=1, source_target_pairs={{0,6},{2,0},{4,2},{6,4},{1,7},{3,1},{5,3},{7,5},{8,14},{10,8},{12,... | collective-permute-start | bytes 294920 | tf_op jit(solution)/shard_map/ppermute | solution.py:247
  40.6 0.6 collective-permute-start.12
  41.2 0.5 collective-permute-done.10
  41.7 2.9 %collective-permute-done.11 = f32[2,3,2,16,128]{4,3,2,1,0:T(8,128)S(1)} collective-permute-done((f32[2,3,2,16,128]{4,3,2,1,0:T(8,128)S(1)}, f32[2,3,2,16,128]{4,3,2,1,0:T(8,128)S(1)}, u32[]{:S(2)}, u32[]{:S(2)}) %collective-permute-start.11) | collective-permute-done | bytes 98336 | tf_op jit(solution)/shard_map/ppermute | solution.py:247
  44.6 0.7 %collective-permute-done.12 = f32[2,3,2,16,128]{4,3,2,1,0:T(8,128)S(1)} collective-permute-done((f32[2,3,2,16,128]{4,3,2,1,0:T(8,128)S(1)}, f32[2,3,2,16,128]{4,3,2,1,0:T(8,128)S(1)}, u32[]{:S(2)}, u32[]{:S(2)}) %collective-permute-start.12) | collective-permute-done | bytes 98336 | tf_op jit(solution)/shard_map/ppermute | solution.py:247
  45.4 0.2 shard_map.91
  45.5 2.5 %collective-permute-start.13 = (f32[4,2,3,16,128]{4,3,2,1,0:T(8,128)S(1)}, f32[4,2,3,16,128]{4,3,2,1,0:T(8,128)S(1)}, u32[]{:S(2)}, u32[]{:S(2)}) collective-permute-start(f32[4,2,3,16,128]{4,3,2,1,0:T(8,128)S(1)} %shard_map.91), channel_id=1, source_target_pairs={{0,1},{1,0},{2,3},{3,2},{4,5},{5,4},{6,7},{7,6},{8,9},{9,8},{10,11... | collective-permute-start | bytes 589832 | tf_op jit(solution)/shard_map/ppermute | solution.py:256
  48.1 0.1 shard_map.90
  48.2 0.9 %collective-permute-done.13 = f32[4,2,3,16,128]{4,3,2,1,0:T(8,128)S(1)} collective-permute-done((f32[4,2,3,16,128]{4,3,2,1,0:T(8,128)S(1)}, f32[4,2,3,16,128]{4,3,2,1,0:T(8,128)S(1)}, u32[]{:S(2)}, u32[]{:S(2)}) %collective-permute-start.13) | collective-permute-done | bytes 196640 | tf_op jit(solution)/shard_map/ppermute | solution.py:256
  49.2 3.0 %collective-permute-start.17 = (f32[2,3,16,128]{3,2,1,0:T(8,128)S(1)}, f32[2,3,16,128]{3,2,1,0:T(8,128)S(1)}, u32[]{:S(2)}, u32[]{:S(2)}) collective-permute-start(f32[2,3,16,128]{3,2,1,0:T(8,128)S(1)} %get-tuple-element.17), channel_id=1, source_target_pairs={{0,56},{8,0},{16,8},{24,16},{32,24},{40,32},{48,40},{56,48},{1,33}... | collective-permute-start | bytes 147464 | tf_op jit(solution)/shard_map/ppermute | solution.py:252
  52.2 0.4 collective-permute-start.16
  52.6 2.7 %collective-permute-start.15 = (f32[2,3,16,128]{3,2,1,0:T(8,128)S(1)}, f32[2,3,16,128]{3,2,1,0:T(8,128)S(1)}, u32[]{:S(2)}, u32[]{:S(2)}) collective-permute-start(f32[2,3,16,128]{3,2,1,0:T(8,128)S(1)} %get-tuple-element.19), channel_id=1, source_target_pairs={{0,48},{8,56},{16,0},{24,8},{32,16},{40,24},{48,32},{56,40},{1,17}... | collective-permute-start | bytes 147464 | tf_op jit(solution)/shard_map/ppermute | solution.py:252
  55.3 1.6 %collective-permute-start.14 = (f32[2,3,16,128]{3,2,1,0:T(8,128)S(1)}, f32[2,3,16,128]{3,2,1,0:T(8,128)S(1)}, u32[]{:S(2)}, u32[]{:S(2)}) collective-permute-start(f32[2,3,16,128]{3,2,1,0:T(8,128)S(1)} %get-tuple-element.20), channel_id=1, source_target_pairs={{0,8},{8,16},{16,24},{24,32},{32,40},{40,48},{48,56},{56,0},{1,57}... | collective-permute-start | bytes 147464 | tf_op jit(solution)/shard_map/ppermute | solution.py:252
  56.8 0.0 collective-permute-done.17
  56.9 0.4 collective-permute-done.16.r2
  57.2 1.0 %collective-permute-done.15.r1 = f32[2,3,16,128]{3,2,1,0:T(8,128)S(1)} collective-permute-done((f32[2,3,16,128]{3,2,1,0:T(8,128)S(1)}, f32[2,3,16,128]{3,2,1,0:T(8,128)S(1)}, u32[]{:S(2)}, u32[]{:S(2)}) %collective-permute-start.15) | collective-permute-done | bytes 49184 | tf_op jit(solution)/shard_map/ppermute | solution.py:252
  58.2 0.6 collective-permute-done.14.r0
  58.9 1.8 %collective-permute-start.18 = (f32[4,3,16,128]{3,2,1,0:T(8,128)S(1)}, f32[4,3,16,128]{3,2,1,0:T(8,128)S(1)}, u32[]{:S(2)}, u32[]{:S(2)}) collective-permute-start(f32[4,3,16,128]{3,2,1,0:T(8,128)S(1)} %pad_maximum_fusion.3), channel_id=1, source_target_pairs={{0,1},{1,0},{2,3},{3,2},{4,5},{5,4},{6,7},{7,6},{8,9},{9,8},{10,11... | collective-permute-start | bytes 294920 | tf_op jit(solution)/shard_map/ppermute | solution.py:256
  60.6 0.9 %collective-permute-done.18.other_ref = f32[4,3,16,128]{3,2,1,0:T(8,128)S(1)} collective-permute-done((f32[4,3,16,128]{3,2,1,0:T(8,128)S(1)}, f32[4,3,16,128]{3,2,1,0:T(8,128)S(1)}, u32[]{:S(2)}, u32[]{:S(2)}) %collective-permute-start.18) | collective-permute-done | bytes 98336 | tf_op jit(solution)/shard_map/ppermute | solution.py:256
  61.6 2.9 %collective-permute-start.21 = (f32[16,128]{1,0:T(8,128)S(1)}, f32[16,128]{1,0:T(8,128)S(1)}, u32[]{:S(2)}, u32[]{:S(2)}) collective-permute-start(f32[16,128]{1,0:T(8,128)S(1)} %shard_map.93), channel_id=1, source_target_pairs={{0,128},{64,192},{128,0},{192,64},{1,129},{65,193},{129,1},{193,65... | collective-permute-start | bytes 24584 | tf_op jit(solution)/shard_map/ppermute | solution.py:260
  64.5 0.8 %collective-permute-start.20 = (f32[16,128]{1,0:T(8,128)S(1)}, f32[16,128]{1,0:T(8,128)S(1)}, u32[]{:S(2)}, u32[]{:S(2)}) collective-permute-start(f32[16,128]{1,0:T(8,128)S(1)} %shard_map.93), channel_id=1, source_target_pairs={{0,192},{64,128},{128,64},{192,0},{1,193},{65,129},{129,65},{193,1... | collective-permute-start | bytes 24584 | tf_op jit(solution)/shard_map/ppermute | solution.py:260
  65.3 0.0 collective-permute-start.19
  65.3 0.0 copy-done.1
  65.3 0.6 shard_map.92
  65.8 0.7 reshape.33
  66.5 0.0 collective-permute-done.21
  66.5 1.7 %collective-permute-done.20 = f32[16,128]{1,0:T(8,128)S(1)} collective-permute-done((f32[16,128]{1,0:T(8,128)S(1)}, f32[16,128]{1,0:T(8,128)S(1)}, u32[]{:S(2)}, u32[]{:S(2)}) %collective-permute-start.20) | collective-permute-done | bytes 8224 | tf_op jit(solution)/shard_map/ppermute | solution.py:260
  68.2 0.0 collective-permute-done.19
  68.2 0.6 add_bitcast_fusion
  (24 shorter events, 0.3 us)
Async XLA Ops:
  1.7 32.8 %copy-start = (bf16[4,256,256]{2,1,0:T(8,128)(2,1)S(1)}, bf16[4,256,256]{2,1,0:T(8,128)(2,1)}, u32[]{:S(2)}) copy-start(bf16[4,256,256]{2,1,0:T(8,128)(2,1)} %constant.61.clone.right) | copy-start | bytes 1572868
  1.8 4.4 %collective-permute-start = (f32[4,5,16,128]{3,2,1,0:T(8,128)S(1)}, f32[4,5,16,128]{3,2,1,0:T(8,128)S(1)}, u32[]{:S(2)}, u32[]{:S(2)}) collective-permute-start(f32[4,5,16,128]{3,2,1,0:T(8,128)S(1)} %pad_maximum_fusion.2), channel_id=1, source_target_pairs={{0,1},{1,0},{2,3},{3,2},{4,5},{5,4},{6,7},{7,6},{8,9},{9,8},{10,11... | collective-permute-start | bytes 491528 | tf_op jit(solution)/shard_map/ppermute | solution.py:256
  6.2 10.1 %collective-permute-start.4 = (f32[2,5,16,128]{3,2,1,0:T(8,128)S(1)}, f32[2,5,16,128]{3,2,1,0:T(8,128)S(1)}, u32[]{:S(2)}, u32[]{:S(2)}) collective-permute-start(f32[2,5,16,128]{3,2,1,0:T(8,128)S(1)} %pad_maximum_fusion.7), channel_id=1, source_target_pairs={{0,56},{8,0},{16,8},{24,16},{32,24},{40,32},{48,40},{56,48},{1,33}... | collective-permute-start | bytes 245768 | tf_op jit(solution)/shard_map/ppermute | solution.py:252
  11.4 6.0 %collective-permute-start.1 = (f32[2,5,16,128]{3,2,1,0:T(8,128)S(1)}, f32[2,5,16,128]{3,2,1,0:T(8,128)S(1)}, u32[]{:S(2)}, u32[]{:S(2)}) collective-permute-start(f32[2,5,16,128]{3,2,1,0:T(8,128)S(1)} %pad_maximum_fusion.4), channel_id=1, source_target_pairs={{0,24},{8,32},{16,40},{24,48},{32,56},{40,0},{48,8},{56,16},{1,41}... | collective-permute-start | bytes 245768 | tf_op jit(solution)/shard_map/ppermute | solution.py:252
  11.5 6.6 %collective-permute-start.2 = (f32[2,5,16,128]{3,2,1,0:T(8,128)S(1)}, f32[2,5,16,128]{3,2,1,0:T(8,128)S(1)}, u32[]{:S(2)}, u32[]{:S(2)}) collective-permute-start(f32[2,5,16,128]{3,2,1,0:T(8,128)S(1)} %pad_maximum_fusion.5), channel_id=1, source_target_pairs={{0,48},{8,56},{16,0},{24,8},{32,16},{40,24},{48,32},{56,40},{1,17}... | collective-permute-start | bytes 245768 | tf_op jit(solution)/shard_map/ppermute | solution.py:252
  13.4 7.1 %collective-permute-start.3 = (f32[2,5,16,128]{3,2,1,0:T(8,128)S(1)}, f32[2,5,16,128]{3,2,1,0:T(8,128)S(1)}, u32[]{:S(2)}, u32[]{:S(2)}) collective-permute-start(f32[2,5,16,128]{3,2,1,0:T(8,128)S(1)} %pad_maximum_fusion.6), channel_id=1, source_target_pairs={{0,8},{8,16},{16,24},{24,32},{32,40},{40,48},{48,56},{56,0},{1,57}... | collective-permute-start | bytes 245768 | tf_op jit(solution)/shard_map/ppermute | solution.py:252
  20.7 6.0 %collective-permute-start.7 = (f32[3,2,5,2,16,128]{5,4,3,2,1,0:T(8,128)S(1)}, f32[3,2,5,2,16,128]{5,4,3,2,1,0:T(8,128)S(1)}, u32[]{:S(2)}, u32[]{:S(2)}) collective-permute-start(f32[3,2,5,2,16,128]{5,4,3,2,1,0:T(8,128)S(1)} %slice.139), channel_id=1, source_target_pairs={{0,1},{1,0},{2,3},{3,2},{4,5},{5,4},{6,7},{7,6},{8,9},{9,8},{10,11... | collective-permute-start | bytes 1474568 | tf_op jit(solution)/shard_map/ppermute | solution.py:256
  22.2 1.7 %collective-permute-start.5 = (f32[2,5,2,16,128]{4,3,2,1,0:T(8,128)S(1)}, f32[2,5,2,16,128]{4,3,2,1,0:T(8,128)S(1)}, u32[]{:S(2)}, u32[]{:S(2)}) collective-permute-start(f32[2,5,2,16,128]{4,3,2,1,0:T(8,128)S(1)} %slice_bitcast_fusion), channel_id=1, source_target_pairs={{0,1},{1,0},{2,3},{3,2},{4,5},{5,4},{6,7},{7,6},{8,9},{9,8},{10,11... | collective-permute-start | bytes 491528 | tf_op jit(solution)/shard_map/ppermute | solution.py:256
  23.9 41.4 %copy-start.1 = (f32[16]{0:T(128)S(1)}, f32[16]{0:T(128)}, u32[]{:S(2)}) copy-start(f32[16]{0:T(128)} %skip_ref.1) | copy-start | bytes 196
  23.9 7.0 %collective-permute-start.6 = (f32[2,5,2,16,128]{4,3,2,1,0:T(8,128)S(1)}, f32[2,5,2,16,128]{4,3,2,1,0:T(8,128)S(1)}, u32[]{:S(2)}, u32[]{:S(2)}) collective-permute-start(f32[2,5,2,16,128]{4,3,2,1,0:T(8,128)S(1)} %fusion.3), channel_id=1, source_target_pairs={{0,4},{2,6},{4,0},{6,2},{1,5},{3,7},{5,1},{7,3},{8,12},{10,14},{12... | collective-permute-start | bytes 491528 | tf_op jit(solution)/shard_map/ppermute | solution.py:247
  26.8 7.7 %collective-permute-start.9 = (f32[2,5,2,16,128]{4,3,2,1,0:T(8,128)S(1)}, f32[2,5,2,16,128]{4,3,2,1,0:T(8,128)S(1)}, u32[]{:S(2)}, u32[]{:S(2)}) collective-permute-start(f32[2,5,2,16,128]{4,3,2,1,0:T(8,128)S(1)} %get-tuple-element.8), channel_id=1, source_target_pairs={{0,6},{2,0},{4,2},{6,4},{1,7},{3,1},{5,3},{7,5},{8,14},{10,8},{12,... | collective-permute-start | bytes 491528 | tf_op jit(solution)/shard_map/ppermute | solution.py:247
  27.7 6.8 %collective-permute-start.8 = (f32[2,5,2,16,128]{4,3,2,1,0:T(8,128)S(1)}, f32[2,5,2,16,128]{4,3,2,1,0:T(8,128)S(1)}, u32[]{:S(2)}, u32[]{:S(2)}) collective-permute-start(f32[2,5,2,16,128]{4,3,2,1,0:T(8,128)S(1)} %get-tuple-element.15), channel_id=1, source_target_pairs={{0,2},{2,4},{4,6},{6,0},{1,3},{3,5},{5,7},{7,1},{8,10},{10,12},{12... | collective-permute-start | bytes 491528 | tf_op jit(solution)/shard_map/ppermute | solution.py:247
  36.3 5.4 %collective-permute-start.10 = (f32[2,3,2,16,128]{4,3,2,1,0:T(8,128)S(1)}, f32[2,3,2,16,128]{4,3,2,1,0:T(8,128)S(1)}, u32[]{:S(2)}, u32[]{:S(2)}) collective-permute-start(f32[2,3,2,16,128]{4,3,2,1,0:T(8,128)S(1)} %get-tuple-element.11), channel_id=1, source_target_pairs={{0,4},{2,6},{4,0},{6,2},{1,5},{3,7},{5,1},{7,3},{8,12},{10,14},{12... | collective-permute-start | bytes 294920 | tf_op jit(solution)/shard_map/ppermute | solution.py:247
  39.7 4.9 %collective-permute-start.11 = (f32[2,3,2,16,128]{4,3,2,1,0:T(8,128)S(1)}, f32[2,3,2,16,128]{4,3,2,1,0:T(8,128)S(1)}, u32[]{:S(2)}, u32[]{:S(2)}) collective-permute-start(f32[2,3,2,16,128]{4,3,2,1,0:T(8,128)S(1)} %get-tuple-element.12), channel_id=1, source_target_pairs={{0,6},{2,0},{4,2},{6,4},{1,7},{3,1},{5,3},{7,5},{8,14},{10,8},{12,... | collective-permute-start | bytes 294920 | tf_op jit(solution)/shard_map/ppermute | solution.py:247
  40.6 4.7 %collective-permute-start.12 = (f32[2,3,2,16,128]{4,3,2,1,0:T(8,128)S(1)}, f32[2,3,2,16,128]{4,3,2,1,0:T(8,128)S(1)}, u32[]{:S(2)}, u32[]{:S(2)}) collective-permute-start(f32[2,3,2,16,128]{4,3,2,1,0:T(8,128)S(1)} %get-tuple-element.13), channel_id=1, source_target_pairs={{0,2},{2,4},{4,6},{6,0},{1,3},{3,5},{5,7},{7,1},{8,10},{10,12},{12... | collective-permute-start | bytes 294920 | tf_op jit(solution)/shard_map/ppermute | solution.py:247
  45.5 3.6 %collective-permute-start.13 = (f32[4,2,3,16,128]{4,3,2,1,0:T(8,128)S(1)}, f32[4,2,3,16,128]{4,3,2,1,0:T(8,128)S(1)}, u32[]{:S(2)}, u32[]{:S(2)}) collective-permute-start(f32[4,2,3,16,128]{4,3,2,1,0:T(8,128)S(1)} %shard_map.91), channel_id=1, source_target_pairs={{0,1},{1,0},{2,3},{3,2},{4,5},{5,4},{6,7},{7,6},{8,9},{9,8},{10,11... | collective-permute-start | bytes 589832 | tf_op jit(solution)/shard_map/ppermute | solution.py:256
  49.2 7.7 %collective-permute-start.17 = (f32[2,3,16,128]{3,2,1,0:T(8,128)S(1)}, f32[2,3,16,128]{3,2,1,0:T(8,128)S(1)}, u32[]{:S(2)}, u32[]{:S(2)}) collective-permute-start(f32[2,3,16,128]{3,2,1,0:T(8,128)S(1)} %get-tuple-element.17), channel_id=1, source_target_pairs={{0,56},{8,0},{16,8},{24,16},{32,24},{40,32},{48,40},{56,48},{1,33}... | collective-permute-start | bytes 147464 | tf_op jit(solution)/shard_map/ppermute | solution.py:252
  52.2 5.0 %collective-permute-start.16 = (f32[2,3,16,128]{3,2,1,0:T(8,128)S(1)}, f32[2,3,16,128]{3,2,1,0:T(8,128)S(1)}, u32[]{:S(2)}, u32[]{:S(2)}) collective-permute-start(f32[2,3,16,128]{3,2,1,0:T(8,128)S(1)} %get-tuple-element.18), channel_id=1, source_target_pairs={{0,24},{8,32},{16,40},{24,48},{32,56},{40,0},{48,8},{56,16},{1,41}... | collective-permute-start | bytes 147464 | tf_op jit(solution)/shard_map/ppermute | solution.py:252
  52.6 5.6 %collective-permute-start.15 = (f32[2,3,16,128]{3,2,1,0:T(8,128)S(1)}, f32[2,3,16,128]{3,2,1,0:T(8,128)S(1)}, u32[]{:S(2)}, u32[]{:S(2)}) collective-permute-start(f32[2,3,16,128]{3,2,1,0:T(8,128)S(1)} %get-tuple-element.19), channel_id=1, source_target_pairs={{0,48},{8,56},{16,0},{24,8},{32,16},{40,24},{48,32},{56,40},{1,17}... | collective-permute-start | bytes 147464 | tf_op jit(solution)/shard_map/ppermute | solution.py:252
  55.3 3.6 %collective-permute-start.14 = (f32[2,3,16,128]{3,2,1,0:T(8,128)S(1)}, f32[2,3,16,128]{3,2,1,0:T(8,128)S(1)}, u32[]{:S(2)}, u32[]{:S(2)}) collective-permute-start(f32[2,3,16,128]{3,2,1,0:T(8,128)S(1)} %get-tuple-element.20), channel_id=1, source_target_pairs={{0,8},{8,16},{16,24},{24,32},{32,40},{40,48},{48,56},{56,0},{1,57}... | collective-permute-start | bytes 147464 | tf_op jit(solution)/shard_map/ppermute | solution.py:252
  58.9 2.7 %collective-permute-start.18 = (f32[4,3,16,128]{3,2,1,0:T(8,128)S(1)}, f32[4,3,16,128]{3,2,1,0:T(8,128)S(1)}, u32[]{:S(2)}, u32[]{:S(2)}) collective-permute-start(f32[4,3,16,128]{3,2,1,0:T(8,128)S(1)} %pad_maximum_fusion.3), channel_id=1, source_target_pairs={{0,1},{1,0},{2,3},{3,2},{4,5},{5,4},{6,7},{7,6},{8,9},{9,8},{10,11... | collective-permute-start | bytes 294920 | tf_op jit(solution)/shard_map/ppermute | solution.py:256
  61.6 5.0 %collective-permute-start.21 = (f32[16,128]{1,0:T(8,128)S(1)}, f32[16,128]{1,0:T(8,128)S(1)}, u32[]{:S(2)}, u32[]{:S(2)}) collective-permute-start(f32[16,128]{1,0:T(8,128)S(1)} %shard_map.93), channel_id=1, source_target_pairs={{0,128},{64,192},{128,0},{192,64},{1,129},{65,193},{129,1},{193,65... | collective-permute-start | bytes 24584 | tf_op jit(solution)/shard_map/ppermute | solution.py:260
  64.5 3.7 %collective-permute-start.20 = (f32[16,128]{1,0:T(8,128)S(1)}, f32[16,128]{1,0:T(8,128)S(1)}, u32[]{:S(2)}, u32[]{:S(2)}) collective-permute-start(f32[16,128]{1,0:T(8,128)S(1)} %shard_map.93), channel_id=1, source_target_pairs={{0,192},{64,128},{128,64},{192,0},{1,193},{65,129},{129,65},{193,1... | collective-permute-start | bytes 24584 | tf_op jit(solution)/shard_map/ppermute | solution.py:260
  65.3 2.9 %collective-permute-start.19 = (f32[16,128]{1,0:T(8,128)S(1)}, f32[16,128]{1,0:T(8,128)S(1)}, u32[]{:S(2)}, u32[]{:S(2)}) collective-permute-start(f32[16,128]{1,0:T(8,128)S(1)} %shard_map.93), channel_id=1, source_target_pairs={{0,64},{64,0},{128,192},{192,128},{1,65},{65,1},{129,193},{193,129... | collective-permute-start | bytes 24584 | tf_op jit(solution)/shard_map/ppermute | solution.py:260

commit v5 on v4

--- a/solution.py
+++ b/solution.py
@@ -12,7 +12,7 @@
 
 Y, Z, X, C = 4, 8, 4, 2
 ROWS_IN, ROWS_OUT = 5, 3
-SHIFTS, SHIFTS_BACK = ((3, 6, 1, 0), (5, 2, 7, 4)), ((1, 6, 3, 0), (7, 2, 5, 4))
+SHIFTS, SHIFTS_BACK = ((3, 1, 6, 0), (5, 7, 2, 4)), ((1, 6, 3, 0), (7, 2, 5, 4))
 KEPT, UNUSED = 3, 7
 ORDER_IN, ORDER_OUT = (2, 0, 1, 3), (0, 2, 1, 3)
 SUB, LANES = 16, 128

time: 69 us -> 68.5 us (level)
  starting transfers between devices: 38.2 us -> 36.9 us
  waiting for transfers between devices: 22 us -> 22.8 us
    ppermute x5, starting transfers between devices: 9.11 us -> 7.03 us  [swap_core(): return lax.ppermute(value, 'c', [(0, 1), (1, 0)])]
    ppermute x8, waiting for transfers between devices: 7.76 us -> 8.61 us  [shift_z(): return lax.ppermute(value, ('z', 'c'), pairs)]
    ppermute x8, starting transfers between devices: 16.1 us -> 16.9 us  [shift_z(): return lax.ppermute(value, ('z', 'c'), pairs)]
  transfers between devices with their start and end apart: 22 -> 22, of which waited for: 18 -> 15; matrix products, arithmetic and copies ran while one was open for 4% -> 4% of each run, Pallas kernels for 1% -> 1%
where the time goes in v5:
time: 68.5 us; the launch traced here: 68.3 us
  starting transfers between devices  36.9 us (54%)
  waiting for transfers between devices  22.8 us (33%)
  Pallas kernels  4.06 us (6%)
  local copies, waits for them, and re-layouts  2.84 us (4%)
  between operations  0.86 us (1%)
  other arithmetic  0.83 us (1%)
    ppermute x8, starting transfers between devices, shift_z(): return lax.ppermute(value, ('z', 'c'), pairs)  16.9 us
    ppermute x6, starting transfers between devices, shift_x(): return lax.ppermute(value, 'x', [(i, (i + shift) % X) for i in range(X)])  9.29 us
    ppermute x8, waiting for transfers between devices, shift_z(): return lax.ppermute(value, ('z', 'c'), pairs)  8.61 us
    ppermute x6, waiting for transfers between devices, shift_x(): return lax.ppermute(value, 'x', [(i, (i + shift) % X) for i in range(X)])  8.28 us
    ppermute x5, starting transfers between devices, swap_core(): return lax.ppermute(value, 'c', [(0, 1), (1, 0)])  7.03 us
    ppermute x5, waiting for transfers between devices, swap_core(): return lax.ppermute(value, 'c', [(0, 1), (1, 0)])  4.23 us
    ppermute x3, starting transfers between devices, pair_y(): return lax.ppermute(value, 'y', [(i, partner(i)) for i in range(Y)])  3.7 us
    squeeze x2, local copies, waits for them, and re-layouts, mine(): lax.dynamic_index_in_dim(jnp.asarray(table), place, 0, keepdims=False)  2 us
  transfers between devices with their start and end apart: 22, of which 15 were waited for; matrix products, arithmetic and copies ran while one was open for 4% of the time, Pallas kernels for 1%

profile of v5, /device:TPU:1, one launch (start us, length us, event | category | flops | bytes accessed | tf_op | source)
XLA Modules:
  0.0 68.3 jit_solution(5490025595647566918)
XLA Ops:
  0.7 1.0 %shard_map.86.packed_ref = f32[8,5,16,128]{3,2,1,0:T(8,128)S(1)} custom-call(s32[1]{0:T(128)} %bitcast.place_ref, f32[1,16,2048]{2,1,0:T(8,128)} %grad_hbm.1, f32[1,16,2048]{2,1,0:T(8,128)} %input_hbm.1, f32[16,128]{1,0:T(8,128)} %bitcast.31), custom_call_target="tpu_custom_call" | custom-call | tf_op jit(solution)/shard_map/pallas_call | solution.py:274
  1.7 0.0 copy-start
  1.8 3.3 %collective-permute-start = (f32[4,5,16,128]{3,2,1,0:T(8,128)S(1)}, f32[4,5,16,128]{3,2,1,0:T(8,128)S(1)}, u32[]{:S(2)}, u32[]{:S(2)}) collective-permute-start(f32[4,5,16,128]{3,2,1,0:T(8,128)S(1)} %pad_maximum_fusion.2), channel_id=1, source_target_pairs={{0,1},{1,0},{2,3},{3,2},{4,5},{5,4},{6,7},{7,6},{8,9},{9,8},{10,11... | collective-permute-start | bytes 491528 | tf_op jit(solution)/shard_map/ppermute | solution.py:256
  5.1 1.0 %collective-permute-done = f32[4,5,16,128]{3,2,1,0:T(8,128)S(1)} collective-permute-done((f32[4,5,16,128]{3,2,1,0:T(8,128)S(1)}, f32[4,5,16,128]{3,2,1,0:T(8,128)S(1)}, u32[]{:S(2)}, u32[]{:S(2)}) %collective-permute-start) | collective-permute-done | bytes 163872 | tf_op jit(solution)/shard_map/ppermute | solution.py:256
  6.2 5.3 %collective-permute-start.4 = (f32[2,5,16,128]{3,2,1,0:T(8,128)S(1)}, f32[2,5,16,128]{3,2,1,0:T(8,128)S(1)}, u32[]{:S(2)}, u32[]{:S(2)}) collective-permute-start(f32[2,5,16,128]{3,2,1,0:T(8,128)S(1)} %pad_maximum_fusion.7), channel_id=1, source_target_pairs={{0,56},{8,0},{16,8},{24,16},{32,24},{40,32},{48,40},{56,48},{1,33}... | collective-permute-start | bytes 245768 | tf_op jit(solution)/shard_map/ppermute | solution.py:252
  11.4 0.0 collective-permute-start.1
  11.5 0.5 collective-permute-start.2
  11.9 1.6 %collective-permute-start.3 = (f32[2,5,16,128]{3,2,1,0:T(8,128)S(1)}, f32[2,5,16,128]{3,2,1,0:T(8,128)S(1)}, u32[]{:S(2)}, u32[]{:S(2)}) collective-permute-start(f32[2,5,16,128]{3,2,1,0:T(8,128)S(1)} %pad_maximum_fusion.6), channel_id=1, source_target_pairs={{0,48},{8,56},{16,0},{24,8},{32,16},{40,24},{48,32},{56,40},{1,17}... | collective-permute-start | bytes 245768 | tf_op jit(solution)/shard_map/ppermute | solution.py:252
  13.5 2.0 %collective-permute-done.4 = f32[2,5,16,128]{3,2,1,0:T(8,128)S(1)} collective-permute-done((f32[2,5,16,128]{3,2,1,0:T(8,128)S(1)}, f32[2,5,16,128]{3,2,1,0:T(8,128)S(1)}, u32[]{:S(2)}, u32[]{:S(2)}) %collective-permute-start.4) | collective-permute-done | bytes 81952 | tf_op jit(solution)/shard_map/ppermute | solution.py:252
  15.5 1.2 %collective-permute-done.1.m0 = f32[2,5,16,128]{3,2,1,0:T(8,128)S(1)} collective-permute-done((f32[2,5,16,128]{3,2,1,0:T(8,128)S(1)}, f32[2,5,16,128]{3,2,1,0:T(8,128)S(1)}, u32[]{:S(2)}, u32[]{:S(2)}) %collective-permute-start.1) | collective-permute-done | bytes 81952 | tf_op jit(solution)/shard_map/ppermute | solution.py:252
  16.7 3.8 %collective-permute-done.2.m1 = f32[2,5,16,128]{3,2,1,0:T(8,128)S(1)} collective-permute-done((f32[2,5,16,128]{3,2,1,0:T(8,128)S(1)}, f32[2,5,16,128]{3,2,1,0:T(8,128)S(1)}, u32[]{:S(2)}, u32[]{:S(2)}) %collective-permute-start.2) | collective-permute-done | bytes 81952 | tf_op jit(solution)/shard_map/ppermute | solution.py:252
  20.5 0.0 collective-permute-done.3.m2
  20.5 0.2 shard_map.88
  20.7 0.5 collective-permute-start.7
  21.3 0.2 collective-permute-start.5
  21.4 0.2 shard_map.87
  21.7 1.3 %collective-permute-done.5 = f32[2,5,2,16,128]{4,3,2,1,0:T(8,128)S(1)} collective-permute-done((f32[2,5,2,16,128]{4,3,2,1,0:T(8,128)S(1)}, f32[2,5,2,16,128]{4,3,2,1,0:T(8,128)S(1)}, u32[]{:S(2)}, u32[]{:S(2)}) %collective-permute-start.5) | collective-permute-done | bytes 163872 | tf_op jit(solution)/shard_map/ppermute | solution.py:256
  23.0 0.0 copy-start.1
  23.0 2.8 %collective-permute-start.6 = (f32[2,5,2,16,128]{4,3,2,1,0:T(8,128)S(1)}, f32[2,5,2,16,128]{4,3,2,1,0:T(8,128)S(1)}, u32[]{:S(2)}, u32[]{:S(2)}) collective-permute-start(f32[2,5,2,16,128]{4,3,2,1,0:T(8,128)S(1)} %fusion.3), channel_id=1, source_target_pairs={{0,4},{2,6},{4,0},{6,2},{1,5},{3,7},{5,1},{7,3},{8,12},{10,14},{12... | collective-permute-start | bytes 491528 | tf_op jit(solution)/shard_map/ppermute | solution.py:247
  25.8 0.0 collective-permute-done.7
  25.8 0.1 fusion
  25.9 0.9 %collective-permute-start.9 = (f32[2,5,2,16,128]{4,3,2,1,0:T(8,128)S(1)}, f32[2,5,2,16,128]{4,3,2,1,0:T(8,128)S(1)}, u32[]{:S(2)}, u32[]{:S(2)}) collective-permute-start(f32[2,5,2,16,128]{4,3,2,1,0:T(8,128)S(1)} %get-tuple-element.8), channel_id=1, source_target_pairs={{0,6},{2,0},{4,2},{6,4},{1,7},{3,1},{5,3},{7,5},{8,14},{10,8},{12,... | collective-permute-start | bytes 491528 | tf_op jit(solution)/shard_map/ppermute | solution.py:247
  26.9 0.6 collective-permute-start.8
  27.5 0.9 %dynamic-slice_bitcast_fusion.1.tw = f32[2,128,128]{2,1,0:T(8,128)S(1)} fusion(f32[8,2,128,128]{3,2,1,0:T(8,128)} %constant.63.clone, s32[]{:T(128)S(6)} %select_n.90), kind=kLoop, calls=%fused_computation.13 | loop fusion | bytes 262148 | tf_op jit(solution)/shard_map/jit(dynamic_index_in_dim)/squeeze | solution.py:267
  28.4 1.1 %dynamic-slice_bitcast_fusion.left = bf16[4,256,256]{2,1,0:T(8,128)(2,1)S(1)} fusion(bf16[8,4,256,256]{3,2,1,0:T(8,128)(2,1)} %constant.62.clone, s32[]{:T(128)S(6)} %select_n.90), kind=kLoop, calls=%fused_computation | loop fusion | bytes 1048580 | tf_op jit(solution)/shard_map/jit(dynamic_index_in_dim)/squeeze | solution.py:267
  29.5 0.6 collective-permute-done.6.x0
  30.0 3.6 %collective-permute-done.9.x3 = f32[2,5,2,16,128]{4,3,2,1,0:T(8,128)S(1)} collective-permute-done((f32[2,5,2,16,128]{4,3,2,1,0:T(8,128)S(1)}, f32[2,5,2,16,128]{4,3,2,1,0:T(8,128)S(1)}, u32[]{:S(2)}, u32[]{:S(2)}) %collective-permute-start.9) | collective-permute-done | bytes 163872 | tf_op jit(solution)/shard_map/ppermute | solution.py:247
  33.6 0.0 collective-permute-done.8.x2
  33.7 0.0 copy-done
  33.7 1.7 %shard_map.89 = (f32[2,3,2,16,128]{4,3,2,1,0:T(8,128)S(1)}, f32[2,3,2,16,128]{4,3,2,1,0:T(8,128)S(1)}, f32[2,3,2,16,128]{4,3,2,1,0:T(8,128)S(1)}, f32[2,3,2,16,128]{4,3,2,1,0:T(8,128)S(1)}) custom-call(f32[2,5,2,16,128]{4,3,2,1,0:T(8,128)S(1)} %collective-permute-done.6.x0, f32[2,5,2,16,128]{4,3,2,1,0:T(8,128)S(1)} %get-tuple-element.16.x1, ...), custom_call_target="tpu_custom_call" | custom-call | tf_op jit(solution)/shard_map/pallas_call | solution.py:322
  35.4 3.4 %collective-permute-start.10 = (f32[2,3,2,16,128]{4,3,2,1,0:T(8,128)S(1)}, f32[2,3,2,16,128]{4,3,2,1,0:T(8,128)S(1)}, u32[]{:S(2)}, u32[]{:S(2)}) collective-permute-start(f32[2,3,2,16,128]{4,3,2,1,0:T(8,128)S(1)} %get-tuple-element.11), channel_id=1, source_target_pairs={{0,4},{2,6},{4,0},{6,2},{1,5},{3,7},{5,1},{7,3},{8,12},{10,14},{12... | collective-permute-start | bytes 294920 | tf_op jit(solution)/shard_map/ppermute | solution.py:247
  38.8 0.9 %collective-permute-start.11 = (f32[2,3,2,16,128]{4,3,2,1,0:T(8,128)S(1)}, f32[2,3,2,16,128]{4,3,2,1,0:T(8,128)S(1)}, u32[]{:S(2)}, u32[]{:S(2)}) collective-permute-start(f32[2,3,2,16,128]{4,3,2,1,0:T(8,128)S(1)} %get-tuple-element.12), channel_id=1, source_target_pairs={{0,6},{2,0},{4,2},{6,4},{1,7},{3,1},{5,3},{7,5},{8,14},{10,8},{12,... | collective-permute-start | bytes 294920 | tf_op jit(solution)/shard_map/ppermute | solution.py:247
  39.8 0.6 collective-permute-start.12
  40.4 0.5 collective-permute-done.10
  40.8 2.9 %collective-permute-done.11 = f32[2,3,2,16,128]{4,3,2,1,0:T(8,128)S(1)} collective-permute-done((f32[2,3,2,16,128]{4,3,2,1,0:T(8,128)S(1)}, f32[2,3,2,16,128]{4,3,2,1,0:T(8,128)S(1)}, u32[]{:S(2)}, u32[]{:S(2)}) %collective-permute-start.11) | collective-permute-done | bytes 98336 | tf_op jit(solution)/shard_map/ppermute | solution.py:247
  43.7 0.7 %collective-permute-done.12 = f32[2,3,2,16,128]{4,3,2,1,0:T(8,128)S(1)} collective-permute-done((f32[2,3,2,16,128]{4,3,2,1,0:T(8,128)S(1)}, f32[2,3,2,16,128]{4,3,2,1,0:T(8,128)S(1)}, u32[]{:S(2)}, u32[]{:S(2)}) %collective-permute-start.12) | collective-permute-done | bytes 98336 | tf_op jit(solution)/shard_map/ppermute | solution.py:247
  44.5 0.2 shard_map.91
  44.6 2.5 %collective-permute-start.13 = (f32[4,2,3,16,128]{4,3,2,1,0:T(8,128)S(1)}, f32[4,2,3,16,128]{4,3,2,1,0:T(8,128)S(1)}, u32[]{:S(2)}, u32[]{:S(2)}) collective-permute-start(f32[4,2,3,16,128]{4,3,2,1,0:T(8,128)S(1)} %shard_map.91), channel_id=1, source_target_pairs={{0,1},{1,0},{2,3},{3,2},{4,5},{5,4},{6,7},{7,6},{8,9},{9,8},{10,11... | collective-permute-start | bytes 589832 | tf_op jit(solution)/shard_map/ppermute | solution.py:256
  47.2 0.1 shard_map.90
  47.3 0.9 %collective-permute-done.13 = f32[4,2,3,16,128]{4,3,2,1,0:T(8,128)S(1)} collective-permute-done((f32[4,2,3,16,128]{4,3,2,1,0:T(8,128)S(1)}, f32[4,2,3,16,128]{4,3,2,1,0:T(8,128)S(1)}, u32[]{:S(2)}, u32[]{:S(2)}) %collective-permute-start.13) | collective-permute-done | bytes 196640 | tf_op jit(solution)/shard_map/ppermute | solution.py:256
  48.3 3.8 %collective-permute-start.17 = (f32[2,3,16,128]{3,2,1,0:T(8,128)S(1)}, f32[2,3,16,128]{3,2,1,0:T(8,128)S(1)}, u32[]{:S(2)}, u32[]{:S(2)}) collective-permute-start(f32[2,3,16,128]{3,2,1,0:T(8,128)S(1)} %get-tuple-element.17), channel_id=1, source_target_pairs={{0,56},{8,0},{16,8},{24,16},{32,24},{40,32},{48,40},{56,48},{1,33}... | collective-permute-start | bytes 147464 | tf_op jit(solution)/shard_map/ppermute | solution.py:252
  52.1 0.7 %collective-permute-start.16 = (f32[2,3,16,128]{3,2,1,0:T(8,128)S(1)}, f32[2,3,16,128]{3,2,1,0:T(8,128)S(1)}, u32[]{:S(2)}, u32[]{:S(2)}) collective-permute-start(f32[2,3,16,128]{3,2,1,0:T(8,128)S(1)} %get-tuple-element.18), channel_id=1, source_target_pairs={{0,24},{8,32},{16,40},{24,48},{32,56},{40,0},{48,8},{56,16},{1,41}... | collective-permute-start | bytes 147464 | tf_op jit(solution)/shard_map/ppermute | solution.py:252
  52.8 2.4 %collective-permute-start.15 = (f32[2,3,16,128]{3,2,1,0:T(8,128)S(1)}, f32[2,3,16,128]{3,2,1,0:T(8,128)S(1)}, u32[]{:S(2)}, u32[]{:S(2)}) collective-permute-start(f32[2,3,16,128]{3,2,1,0:T(8,128)S(1)} %get-tuple-element.19), channel_id=1, source_target_pairs={{0,48},{8,56},{16,0},{24,8},{32,16},{40,24},{48,32},{56,40},{1,17}... | collective-permute-start | bytes 147464 | tf_op jit(solution)/shard_map/ppermute | solution.py:252
  55.2 2.7 %collective-permute-start.14 = (f32[2,3,16,128]{3,2,1,0:T(8,128)S(1)}, f32[2,3,16,128]{3,2,1,0:T(8,128)S(1)}, u32[]{:S(2)}, u32[]{:S(2)}) collective-permute-start(f32[2,3,16,128]{3,2,1,0:T(8,128)S(1)} %get-tuple-element.20), channel_id=1, source_target_pairs={{0,8},{8,16},{16,24},{24,32},{32,40},{40,48},{48,56},{56,0},{1,57}... | collective-permute-start | bytes 147464 | tf_op jit(solution)/shard_map/ppermute | solution.py:252
  57.9 0.0 collective-permute-done.17
  57.9 0.0 collective-permute-done.16.r2
  57.9 0.8 %collective-permute-done.15.r1 = f32[2,3,16,128]{3,2,1,0:T(8,128)S(1)} collective-permute-done((f32[2,3,16,128]{3,2,1,0:T(8,128)S(1)}, f32[2,3,16,128]{3,2,1,0:T(8,128)S(1)}, u32[]{:S(2)}, u32[]{:S(2)}) %collective-permute-start.15) | collective-permute-done | bytes 49184 | tf_op jit(solution)/shard_map/ppermute | solution.py:252
  58.7 0.9 %collective-permute-done.14.r0 = f32[2,3,16,128]{3,2,1,0:T(8,128)S(1)} collective-permute-done((f32[2,3,16,128]{3,2,1,0:T(8,128)S(1)}, f32[2,3,16,128]{3,2,1,0:T(8,128)S(1)}, u32[]{:S(2)}, u32[]{:S(2)}) %collective-permute-start.14) | collective-permute-done | bytes 49184 | tf_op jit(solution)/shard_map/ppermute | solution.py:252
  59.6 0.5 collective-permute-start.18
  60.1 0.9 %collective-permute-done.18.other_ref = f32[4,3,16,128]{3,2,1,0:T(8,128)S(1)} collective-permute-done((f32[4,3,16,128]{3,2,1,0:T(8,128)S(1)}, f32[4,3,16,128]{3,2,1,0:T(8,128)S(1)}, u32[]{:S(2)}, u32[]{:S(2)}) %collective-permute-start.18) | collective-permute-done | bytes 98336 | tf_op jit(solution)/shard_map/ppermute | solution.py:256
  61.0 2.9 %collective-permute-start.21 = (f32[16,128]{1,0:T(8,128)S(1)}, f32[16,128]{1,0:T(8,128)S(1)}, u32[]{:S(2)}, u32[]{:S(2)}) collective-permute-start(f32[16,128]{1,0:T(8,128)S(1)} %shard_map.93), channel_id=1, source_target_pairs={{0,128},{64,192},{128,0},{192,64},{1,129},{65,193},{129,1},{193,65... | collective-permute-start | bytes 24584 | tf_op jit(solution)/shard_map/ppermute | solution.py:260
  64.0 0.8 %collective-permute-start.20 = (f32[16,128]{1,0:T(8,128)S(1)}, f32[16,128]{1,0:T(8,128)S(1)}, u32[]{:S(2)}, u32[]{:S(2)}) collective-permute-start(f32[16,128]{1,0:T(8,128)S(1)} %shard_map.93), channel_id=1, source_target_pairs={{0,192},{64,128},{128,64},{192,0},{1,193},{65,129},{129,65},{193,1... | collective-permute-start | bytes 24584 | tf_op jit(solution)/shard_map/ppermute | solution.py:260
  64.7 0.0 collective-permute-start.19
  64.8 0.0 copy-done.1
  64.8 0.6 shard_map.92
  65.3 0.7 reshape.33
  66.0 0.0 collective-permute-done.21
  66.0 1.7 %collective-permute-done.20 = f32[16,128]{1,0:T(8,128)S(1)} collective-permute-done((f32[16,128]{1,0:T(8,128)S(1)}, f32[16,128]{1,0:T(8,128)S(1)}, u32[]{:S(2)}, u32[]{:S(2)}) %collective-permute-start.20) | collective-permute-done | bytes 8224 | tf_op jit(solution)/shard_map/ppermute | solution.py:260
  67.7 0.0 collective-permute-done.19
  67.7 0.6 add_bitcast_fusion
  (24 shorter events, 0.3 us)
Async XLA Ops:
  1.7 31.9 %copy-start = (bf16[4,256,256]{2,1,0:T(8,128)(2,1)S(1)}, bf16[4,256,256]{2,1,0:T(8,128)(2,1)}, u32[]{:S(2)}) copy-start(bf16[4,256,256]{2,1,0:T(8,128)(2,1)} %constant.61.clone.right) | copy-start | bytes 1572868
  1.8 4.4 %collective-permute-start = (f32[4,5,16,128]{3,2,1,0:T(8,128)S(1)}, f32[4,5,16,128]{3,2,1,0:T(8,128)S(1)}, u32[]{:S(2)}, u32[]{:S(2)}) collective-permute-start(f32[4,5,16,128]{3,2,1,0:T(8,128)S(1)} %pad_maximum_fusion.2), channel_id=1, source_target_pairs={{0,1},{1,0},{2,3},{3,2},{4,5},{5,4},{6,7},{7,6},{8,9},{9,8},{10,11... | collective-permute-start | bytes 491528 | tf_op jit(solution)/shard_map/ppermute | solution.py:256
  6.2 9.3 %collective-permute-start.4 = (f32[2,5,16,128]{3,2,1,0:T(8,128)S(1)}, f32[2,5,16,128]{3,2,1,0:T(8,128)S(1)}, u32[]{:S(2)}, u32[]{:S(2)}) collective-permute-start(f32[2,5,16,128]{3,2,1,0:T(8,128)S(1)} %pad_maximum_fusion.7), channel_id=1, source_target_pairs={{0,56},{8,0},{16,8},{24,16},{32,24},{40,32},{48,40},{56,48},{1,33}... | collective-permute-start | bytes 245768 | tf_op jit(solution)/shard_map/ppermute | solution.py:252
  11.4 5.2 %collective-permute-start.1 = (f32[2,5,16,128]{3,2,1,0:T(8,128)S(1)}, f32[2,5,16,128]{3,2,1,0:T(8,128)S(1)}, u32[]{:S(2)}, u32[]{:S(2)}) collective-permute-start(f32[2,5,16,128]{3,2,1,0:T(8,128)S(1)} %pad_maximum_fusion.4), channel_id=1, source_target_pairs={{0,24},{8,32},{16,40},{24,48},{32,56},{40,0},{48,8},{56,16},{1,41}... | collective-permute-start | bytes 245768 | tf_op jit(solution)/shard_map/ppermute | solution.py:252
  11.5 9.0 %collective-permute-start.2 = (f32[2,5,16,128]{3,2,1,0:T(8,128)S(1)}, f32[2,5,16,128]{3,2,1,0:T(8,128)S(1)}, u32[]{:S(2)}, u32[]{:S(2)}) collective-permute-start(f32[2,5,16,128]{3,2,1,0:T(8,128)S(1)} %pad_maximum_fusion.5), channel_id=1, source_target_pairs={{0,8},{8,16},{16,24},{24,32},{32,40},{40,48},{48,56},{56,0},{1,57}... | collective-permute-start | bytes 245768 | tf_op jit(solution)/shard_map/ppermute | solution.py:252
  11.9 8.5 %collective-permute-start.3 = (f32[2,5,16,128]{3,2,1,0:T(8,128)S(1)}, f32[2,5,16,128]{3,2,1,0:T(8,128)S(1)}, u32[]{:S(2)}, u32[]{:S(2)}) collective-permute-start(f32[2,5,16,128]{3,2,1,0:T(8,128)S(1)} %pad_maximum_fusion.6), channel_id=1, source_target_pairs={{0,48},{8,56},{16,0},{24,8},{32,16},{40,24},{48,32},{56,40},{1,17}... | collective-permute-start | bytes 245768 | tf_op jit(solution)/shard_map/ppermute | solution.py:252
  20.7 5.1 %collective-permute-start.7 = (f32[3,2,5,2,16,128]{5,4,3,2,1,0:T(8,128)S(1)}, f32[3,2,5,2,16,128]{5,4,3,2,1,0:T(8,128)S(1)}, u32[]{:S(2)}, u32[]{:S(2)}) collective-permute-start(f32[3,2,5,2,16,128]{5,4,3,2,1,0:T(8,128)S(1)} %slice.139), channel_id=1, source_target_pairs={{0,1},{1,0},{2,3},{3,2},{4,5},{5,4},{6,7},{7,6},{8,9},{9,8},{10,11... | collective-permute-start | bytes 1474568 | tf_op jit(solution)/shard_map/ppermute | solution.py:256
  21.3 1.7 %collective-permute-start.5 = (f32[2,5,2,16,128]{4,3,2,1,0:T(8,128)S(1)}, f32[2,5,2,16,128]{4,3,2,1,0:T(8,128)S(1)}, u32[]{:S(2)}, u32[]{:S(2)}) collective-permute-start(f32[2,5,2,16,128]{4,3,2,1,0:T(8,128)S(1)} %slice_bitcast_fusion), channel_id=1, source_target_pairs={{0,1},{1,0},{2,3},{3,2},{4,5},{5,4},{6,7},{7,6},{8,9},{9,8},{10,11... | collective-permute-start | bytes 491528 | tf_op jit(solution)/shard_map/ppermute | solution.py:256
  23.0 41.8 %copy-start.1 = (f32[16]{0:T(128)S(1)}, f32[16]{0:T(128)}, u32[]{:S(2)}) copy-start(f32[16]{0:T(128)} %skip_ref.1) | copy-start | bytes 196
  23.0 7.0 %collective-permute-start.6 = (f32[2,5,2,16,128]{4,3,2,1,0:T(8,128)S(1)}, f32[2,5,2,16,128]{4,3,2,1,0:T(8,128)S(1)}, u32[]{:S(2)}, u32[]{:S(2)}) collective-permute-start(f32[2,5,2,16,128]{4,3,2,1,0:T(8,128)S(1)} %fusion.3), channel_id=1, source_target_pairs={{0,4},{2,6},{4,0},{6,2},{1,5},{3,7},{5,1},{7,3},{8,12},{10,14},{12... | collective-permute-start | bytes 491528 | tf_op jit(solution)/shard_map/ppermute | solution.py:247
  25.9 7.7 %collective-permute-start.9 = (f32[2,5,2,16,128]{4,3,2,1,0:T(8,128)S(1)}, f32[2,5,2,16,128]{4,3,2,1,0:T(8,128)S(1)}, u32[]{:S(2)}, u32[]{:S(2)}) collective-permute-start(f32[2,5,2,16,128]{4,3,2,1,0:T(8,128)S(1)} %get-tuple-element.8), channel_id=1, source_target_pairs={{0,6},{2,0},{4,2},{6,4},{1,7},{3,1},{5,3},{7,5},{8,14},{10,8},{12,... | collective-permute-start | bytes 491528 | tf_op jit(solution)/shard_map/ppermute | solution.py:247
  26.9 6.8 %collective-permute-start.8 = (f32[2,5,2,16,128]{4,3,2,1,0:T(8,128)S(1)}, f32[2,5,2,16,128]{4,3,2,1,0:T(8,128)S(1)}, u32[]{:S(2)}, u32[]{:S(2)}) collective-permute-start(f32[2,5,2,16,128]{4,3,2,1,0:T(8,128)S(1)} %get-tuple-element.15), channel_id=1, source_target_pairs={{0,2},{2,4},{4,6},{6,0},{1,3},{3,5},{5,7},{7,1},{8,10},{10,12},{12... | collective-permute-start | bytes 491528 | tf_op jit(solution)/shard_map/ppermute | solution.py:247
  35.4 5.4 %collective-permute-start.10 = (f32[2,3,2,16,128]{4,3,2,1,0:T(8,128)S(1)}, f32[2,3,2,16,128]{4,3,2,1,0:T(8,128)S(1)}, u32[]{:S(2)}, u32[]{:S(2)}) collective-permute-start(f32[2,3,2,16,128]{4,3,2,1,0:T(8,128)S(1)} %get-tuple-element.11), channel_id=1, source_target_pairs={{0,4},{2,6},{4,0},{6,2},{1,5},{3,7},{5,1},{7,3},{8,12},{10,14},{12... | collective-permute-start | bytes 294920 | tf_op jit(solution)/shard_map/ppermute | solution.py:247
  38.8 4.9 %collective-permute-start.11 = (f32[2,3,2,16,128]{4,3,2,1,0:T(8,128)S(1)}, f32[2,3,2,16,128]{4,3,2,1,0:T(8,128)S(1)}, u32[]{:S(2)}, u32[]{:S(2)}) collective-permute-start(f32[2,3,2,16,128]{4,3,2,1,0:T(8,128)S(1)} %get-tuple-element.12), channel_id=1, source_target_pairs={{0,6},{2,0},{4,2},{6,4},{1,7},{3,1},{5,3},{7,5},{8,14},{10,8},{12,... | collective-permute-start | bytes 294920 | tf_op jit(solution)/shard_map/ppermute | solution.py:247
  39.8 4.7 %collective-permute-start.12 = (f32[2,3,2,16,128]{4,3,2,1,0:T(8,128)S(1)}, f32[2,3,2,16,128]{4,3,2,1,0:T(8,128)S(1)}, u32[]{:S(2)}, u32[]{:S(2)}) collective-permute-start(f32[2,3,2,16,128]{4,3,2,1,0:T(8,128)S(1)} %get-tuple-element.13), channel_id=1, source_target_pairs={{0,2},{2,4},{4,6},{6,0},{1,3},{3,5},{5,7},{7,1},{8,10},{10,12},{12... | collective-permute-start | bytes 294920 | tf_op jit(solution)/shard_map/ppermute | solution.py:247
  44.6 3.6 %collective-permute-start.13 = (f32[4,2,3,16,128]{4,3,2,1,0:T(8,128)S(1)}, f32[4,2,3,16,128]{4,3,2,1,0:T(8,128)S(1)}, u32[]{:S(2)}, u32[]{:S(2)}) collective-permute-start(f32[4,2,3,16,128]{4,3,2,1,0:T(8,128)S(1)} %shard_map.91), channel_id=1, source_target_pairs={{0,1},{1,0},{2,3},{3,2},{4,5},{5,4},{6,7},{7,6},{8,9},{9,8},{10,11... | collective-permute-start | bytes 589832 | tf_op jit(solution)/shard_map/ppermute | solution.py:256
  48.3 9.6 %collective-permute-start.17 = (f32[2,3,16,128]{3,2,1,0:T(8,128)S(1)}, f32[2,3,16,128]{3,2,1,0:T(8,128)S(1)}, u32[]{:S(2)}, u32[]{:S(2)}) collective-permute-start(f32[2,3,16,128]{3,2,1,0:T(8,128)S(1)} %get-tuple-element.17), channel_id=1, source_target_pairs={{0,56},{8,0},{16,8},{24,16},{32,24},{40,32},{48,40},{56,48},{1,33}... | collective-permute-start | bytes 147464 | tf_op jit(solution)/shard_map/ppermute | solution.py:252
  52.1 5.8 %collective-permute-start.16 = (f32[2,3,16,128]{3,2,1,0:T(8,128)S(1)}, f32[2,3,16,128]{3,2,1,0:T(8,128)S(1)}, u32[]{:S(2)}, u32[]{:S(2)}) collective-permute-start(f32[2,3,16,128]{3,2,1,0:T(8,128)S(1)} %get-tuple-element.18), channel_id=1, source_target_pairs={{0,24},{8,32},{16,40},{24,48},{32,56},{40,0},{48,8},{56,16},{1,41}... | collective-permute-start | bytes 147464 | tf_op jit(solution)/shard_map/ppermute | solution.py:252
  52.8 5.9 %collective-permute-start.15 = (f32[2,3,16,128]{3,2,1,0:T(8,128)S(1)}, f32[2,3,16,128]{3,2,1,0:T(8,128)S(1)}, u32[]{:S(2)}, u32[]{:S(2)}) collective-permute-start(f32[2,3,16,128]{3,2,1,0:T(8,128)S(1)} %get-tuple-element.19), channel_id=1, source_target_pairs={{0,48},{8,56},{16,0},{24,8},{32,16},{40,24},{48,32},{56,40},{1,17}... | collective-permute-start | bytes 147464 | tf_op jit(solution)/shard_map/ppermute | solution.py:252
  55.2 4.4 %collective-permute-start.14 = (f32[2,3,16,128]{3,2,1,0:T(8,128)S(1)}, f32[2,3,16,128]{3,2,1,0:T(8,128)S(1)}, u32[]{:S(2)}, u32[]{:S(2)}) collective-permute-start(f32[2,3,16,128]{3,2,1,0:T(8,128)S(1)} %get-tuple-element.20), channel_id=1, source_target_pairs={{0,8},{8,16},{16,24},{24,32},{32,40},{40,48},{48,56},{56,0},{1,57}... | collective-permute-start | bytes 147464 | tf_op jit(solution)/shard_map/ppermute | solution.py:252
  59.6 1.4 %collective-permute-start.18 = (f32[4,3,16,128]{3,2,1,0:T(8,128)S(1)}, f32[4,3,16,128]{3,2,1,0:T(8,128)S(1)}, u32[]{:S(2)}, u32[]{:S(2)}) collective-permute-start(f32[4,3,16,128]{3,2,1,0:T(8,128)S(1)} %pad_maximum_fusion.3), channel_id=1, source_target_pairs={{0,1},{1,0},{2,3},{3,2},{4,5},{5,4},{6,7},{7,6},{8,9},{9,8},{10,11... | collective-permute-start | bytes 294920 | tf_op jit(solution)/shard_map/ppermute | solution.py:256
  61.0 5.0 %collective-permute-start.21 = (f32[16,128]{1,0:T(8,128)S(1)}, f32[16,128]{1,0:T(8,128)S(1)}, u32[]{:S(2)}, u32[]{:S(2)}) collective-permute-start(f32[16,128]{1,0:T(8,128)S(1)} %shard_map.93), channel_id=1, source_target_pairs={{0,128},{64,192},{128,0},{192,64},{1,129},{65,193},{129,1},{193,65... | collective-permute-start | bytes 24584 | tf_op jit(solution)/shard_map/ppermute | solution.py:260
  64.0 3.7 %collective-permute-start.20 = (f32[16,128]{1,0:T(8,128)S(1)}, f32[16,128]{1,0:T(8,128)S(1)}, u32[]{:S(2)}, u32[]{:S(2)}) collective-permute-start(f32[16,128]{1,0:T(8,128)S(1)} %shard_map.93), channel_id=1, source_target_pairs={{0,192},{64,128},{128,64},{192,0},{1,193},{65,129},{129,65},{193,1... | collective-permute-start | bytes 24584 | tf_op jit(solution)/shard_map/ppermute | solution.py:260
  64.7 2.9 %collective-permute-start.19 = (f32[16,128]{1,0:T(8,128)S(1)}, f32[16,128]{1,0:T(8,128)S(1)}, u32[]{:S(2)}, u32[]{:S(2)}) collective-permute-start(f32[16,128]{1,0:T(8,128)S(1)} %shard_map.93), channel_id=1, source_target_pairs={{0,64},{64,0},{128,192},{192,128},{1,65},{65,1},{129,193},{193,129... | collective-permute-start | bytes 24584 | tf_op jit(solution)/shard_map/ppermute | solution.py:260

commit v6 on v5

--- a/solution.py
+++ b/solution.py
@@ -153,9 +153,9 @@
             out_ref[i, block ^ half] = totals[block]
 
 
-def filter_sum_kernel(r0, r1, r2, r3, other_ref, out_ref):
-    pairs = [ref[0, 2] + other_ref[i, 2] for i, ref in enumerate((r0, r1, r2, r3))]
-    out_ref[...] = (pairs[0] + pairs[1]) + (pairs[2] + pairs[3])
+def filter_sum_kernel(r0, r1, r2, r3, own_ref, other_ref):
+    for block, out_ref in enumerate((own_ref, other_ref)):
+        out_ref[...] = (r0[block, 2] + r1[block, 2]) + (r2[block, 2] + r3[block, 2])
 
 
 def finish_kernel(place_ref, zone_ref, skip_ref, packed_ref, r0, r1, r2, r3, other_ref, out_ref):
@@ -342,14 +342,15 @@
     crossed = swap_core(z_return(1))
     kept = z_return(0)
     steps = exchange_z([kept[i] + crossed[i] for i in range(Z // 2)], SHIFTS_BACK)
-    others = swap_core(jnp.stack([step[1] for step in steps]))
-    filter_grad = pl.pallas_call(
+    filter_own, filter_other = pl.pallas_call(
         filter_sum_kernel,
-        out_shape=f32(*tile),
-        in_specs=[VMEM] * 5,
-        out_specs=VMEM,
+        out_shape=[f32(*tile)] * 2,
+        in_specs=[VMEM] * 4,
+        out_specs=[VMEM] * 2,
         compiler_params=PARAMS,
-    )(*steps, others)
+    )(*steps)
+    filter_grad = filter_own + swap_core(filter_other)
+    others = swap_core(jnp.stack([step[1, :2] for step in steps]))
     input_grad = pl.pallas_call(
         finish_kernel,
         out_shape=f32(Z, 2, *tile),
@@ -360,8 +361,10 @@
     across = pair_y(filter_grad, lambda i: i ^ 2)
     far = pair_y(filter_grad, lambda i: Y - 1 - i)
     near = pair_y(filter_grad, lambda i: i ^ 1)
+    input_grad = input_grad.reshape(out_grad.shape)
+    filter_grad, input_grad = lax.optimization_barrier((filter_grad, input_grad))
     filter_grad = (filter_grad + near) + (far + across)
-    return (input_grad.reshape(out_grad.shape), filter_grad.reshape(filter_taps.shape))
+    return (input_grad, filter_grad.reshape(filter_taps.shape))
 
 
 def solution(mesh):

time: 68.5 us -> 68.7 us (level)
    ppermute x5 -> x6, starting transfers between devices: 7.03 us -> 7.2 us  [swap_core(): return lax.ppermute(value, 'c', [(0, 1), (1, 0)])]
    ppermute x5 -> x6, waiting for transfers between devices: 4.23 us -> 4.3 us  [swap_core(): return lax.ppermute(value, 'c', [(0, 1), (1, 0)])]
  transfers between devices with their start and end apart: 22 -> 23, of which waited for: 15 -> 15; matrix products, arithmetic and copies ran while one was open for 4% -> 4% of each run, Pallas kernels for 1% -> 1%
where the time goes in v6:
time: 68.7 us; the launch traced here: 68.5 us
  starting transfers between devices  37.1 us (54%)
  waiting for transfers between devices  22.8 us (33%)
  Pallas kernels  4.06 us (6%)
  local copies, waits for them, and re-layouts  2.84 us (4%)
  between operations  0.86 us (1%)
  other arithmetic  0.83 us (1%)
    ppermute x8, starting transfers between devices, shift_z(): return lax.ppermute(value, ('z', 'c'), pairs)  16.9 us
    ppermute x6, starting transfers between devices, shift_x(): return lax.ppermute(value, 'x', [(i, (i + shift) % X) for i in range(X)])  9.29 us
    ppermute x8, waiting for transfers between devices, shift_z(): return lax.ppermute(value, ('z', 'c'), pairs)  8.61 us
    ppermute x6, waiting for transfers between devices, shift_x(): return lax.ppermute(value, 'x', [(i, (i + shift) % X) for i in range(X)])  8.28 us
    ppermute x6, starting transfers between devices, swap_core(): return lax.ppermute(value, 'c', [(0, 1), (1, 0)])  7.2 us
    ppermute x6, waiting for transfers between devices, swap_core(): return lax.ppermute(value, 'c', [(0, 1), (1, 0)])  4.3 us
    ppermute x3, starting transfers between devices, pair_y(): return lax.ppermute(value, 'y', [(i, partner(i)) for i in range(Y)])  3.7 us
    squeeze x2, local copies, waits for them, and re-layouts, mine(): lax.dynamic_index_in_dim(jnp.asarray(table), place, 0, keepdims=False)  2 us
  transfers between devices with their start and end apart: 23, of which 15 were waited for; matrix products, arithmetic and copies ran while one was open for 4% of the time, Pallas kernels for 1%

profile of v6, /device:TPU:1, one launch (start us, length us, event | category | flops | bytes accessed | tf_op | source)
XLA Modules:
  0.0 68.5 jit_solution(14420818269754980614)
XLA Ops:
  0.7 1.0 %shard_map.86.packed_ref = f32[8,5,16,128]{3,2,1,0:T(8,128)S(1)} custom-call(s32[1]{0:T(128)} %bitcast.place_ref, f32[1,16,2048]{2,1,0:T(8,128)} %grad_hbm.1, f32[1,16,2048]{2,1,0:T(8,128)} %input_hbm.1, f32[16,128]{1,0:T(8,128)} %bitcast.31), custom_call_target="tpu_custom_call" | custom-call | tf_op jit(solution)/shard_map/pallas_call | solution.py:274
  1.7 0.0 copy-start
  1.8 3.3 %collective-permute-start = (f32[4,5,16,128]{3,2,1,0:T(8,128)S(1)}, f32[4,5,16,128]{3,2,1,0:T(8,128)S(1)}, u32[]{:S(2)}, u32[]{:S(2)}) collective-permute-start(f32[4,5,16,128]{3,2,1,0:T(8,128)S(1)} %pad_maximum_fusion.2), channel_id=1, source_target_pairs={{0,1},{1,0},{2,3},{3,2},{4,5},{5,4},{6,7},{7,6},{8,9},{9,8},{10,11... | collective-permute-start | bytes 491528 | tf_op jit(solution)/shard_map/ppermute | solution.py:256
  5.1 1.0 %collective-permute-done = f32[4,5,16,128]{3,2,1,0:T(8,128)S(1)} collective-permute-done((f32[4,5,16,128]{3,2,1,0:T(8,128)S(1)}, f32[4,5,16,128]{3,2,1,0:T(8,128)S(1)}, u32[]{:S(2)}, u32[]{:S(2)}) %collective-permute-start) | collective-permute-done | bytes 163872 | tf_op jit(solution)/shard_map/ppermute | solution.py:256
  6.2 5.3 %collective-permute-start.4 = (f32[2,5,16,128]{3,2,1,0:T(8,128)S(1)}, f32[2,5,16,128]{3,2,1,0:T(8,128)S(1)}, u32[]{:S(2)}, u32[]{:S(2)}) collective-permute-start(f32[2,5,16,128]{3,2,1,0:T(8,128)S(1)} %pad_maximum_fusion.6), channel_id=1, source_target_pairs={{0,56},{8,0},{16,8},{24,16},{32,24},{40,32},{48,40},{56,48},{1,33}... | collective-permute-start | bytes 245768 | tf_op jit(solution)/shard_map/ppermute | solution.py:252
  11.4 0.0 collective-permute-start.1
  11.5 0.5 collective-permute-start.2
  11.9 1.6 %collective-permute-start.3 = (f32[2,5,16,128]{3,2,1,0:T(8,128)S(1)}, f32[2,5,16,128]{3,2,1,0:T(8,128)S(1)}, u32[]{:S(2)}, u32[]{:S(2)}) collective-permute-start(f32[2,5,16,128]{3,2,1,0:T(8,128)S(1)} %pad_maximum_fusion.5), channel_id=1, source_target_pairs={{0,48},{8,56},{16,0},{24,8},{32,16},{40,24},{48,32},{56,40},{1,17}... | collective-permute-start | bytes 245768 | tf_op jit(solution)/shard_map/ppermute | solution.py:252
  13.5 2.0 %collective-permute-done.4 = f32[2,5,16,128]{3,2,1,0:T(8,128)S(1)} collective-permute-done((f32[2,5,16,128]{3,2,1,0:T(8,128)S(1)}, f32[2,5,16,128]{3,2,1,0:T(8,128)S(1)}, u32[]{:S(2)}, u32[]{:S(2)}) %collective-permute-start.4) | collective-permute-done | bytes 81952 | tf_op jit(solution)/shard_map/ppermute | solution.py:252
  15.5 1.2 %collective-permute-done.1.m0 = f32[2,5,16,128]{3,2,1,0:T(8,128)S(1)} collective-permute-done((f32[2,5,16,128]{3,2,1,0:T(8,128)S(1)}, f32[2,5,16,128]{3,2,1,0:T(8,128)S(1)}, u32[]{:S(2)}, u32[]{:S(2)}) %collective-permute-start.1) | collective-permute-done | bytes 81952 | tf_op jit(solution)/shard_map/ppermute | solution.py:252
  16.7 3.8 %collective-permute-done.2.m1 = f32[2,5,16,128]{3,2,1,0:T(8,128)S(1)} collective-permute-done((f32[2,5,16,128]{3,2,1,0:T(8,128)S(1)}, f32[2,5,16,128]{3,2,1,0:T(8,128)S(1)}, u32[]{:S(2)}, u32[]{:S(2)}) %collective-permute-start.2) | collective-permute-done | bytes 81952 | tf_op jit(solution)/shard_map/ppermute | solution.py:252
  20.5 0.0 collective-permute-done.3.m2
  20.5 0.2 shard_map.88
  20.7 0.5 collective-permute-start.7
  21.3 0.2 collective-permute-start.5
  21.4 0.2 shard_map.87
  21.7 1.3 %collective-permute-done.5 = f32[2,5,2,16,128]{4,3,2,1,0:T(8,128)S(1)} collective-permute-done((f32[2,5,2,16,128]{4,3,2,1,0:T(8,128)S(1)}, f32[2,5,2,16,128]{4,3,2,1,0:T(8,128)S(1)}, u32[]{:S(2)}, u32[]{:S(2)}) %collective-permute-start.5) | collective-permute-done | bytes 163872 | tf_op jit(solution)/shard_map/ppermute | solution.py:256
  23.0 0.0 copy-start.1
  23.0 2.8 %collective-permute-start.6 = (f32[2,5,2,16,128]{4,3,2,1,0:T(8,128)S(1)}, f32[2,5,2,16,128]{4,3,2,1,0:T(8,128)S(1)}, u32[]{:S(2)}, u32[]{:S(2)}) collective-permute-start(f32[2,5,2,16,128]{4,3,2,1,0:T(8,128)S(1)} %fusion.3), channel_id=1, source_target_pairs={{0,4},{2,6},{4,0},{6,2},{1,5},{3,7},{5,1},{7,3},{8,12},{10,14},{12... | collective-permute-start | bytes 491528 | tf_op jit(solution)/shard_map/ppermute | solution.py:247
  25.8 0.0 collective-permute-done.7
  25.8 0.1 fusion
  25.9 0.9 %collective-permute-start.9 = (f32[2,5,2,16,128]{4,3,2,1,0:T(8,128)S(1)}, f32[2,5,2,16,128]{4,3,2,1,0:T(8,128)S(1)}, u32[]{:S(2)}, u32[]{:S(2)}) collective-permute-start(f32[2,5,2,16,128]{4,3,2,1,0:T(8,128)S(1)} %get-tuple-element.12), channel_id=1, source_target_pairs={{0,6},{2,0},{4,2},{6,4},{1,7},{3,1},{5,3},{7,5},{8,14},{10,8},{12,... | collective-permute-start | bytes 491528 | tf_op jit(solution)/shard_map/ppermute | solution.py:247
  26.9 0.6 collective-permute-start.8
  27.5 0.9 %dynamic-slice_bitcast_fusion.1.tw = f32[2,128,128]{2,1,0:T(8,128)S(1)} fusion(f32[8,2,128,128]{3,2,1,0:T(8,128)} %constant.63.clone, s32[]{:T(128)S(6)} %select_n.90), kind=kLoop, calls=%fused_computation.13 | loop fusion | bytes 262148 | tf_op jit(solution)/shard_map/jit(dynamic_index_in_dim)/squeeze | solution.py:267
  28.4 1.1 %dynamic-slice_bitcast_fusion.left = bf16[4,256,256]{2,1,0:T(8,128)(2,1)S(1)} fusion(bf16[8,4,256,256]{3,2,1,0:T(8,128)(2,1)} %constant.62.clone, s32[]{:T(128)S(6)} %select_n.90), kind=kLoop, calls=%fused_computation | loop fusion | bytes 1048580 | tf_op jit(solution)/shard_map/jit(dynamic_index_in_dim)/squeeze | solution.py:267
  29.5 0.6 collective-permute-done.6.x0
  30.0 3.6 %collective-permute-done.9.x3 = f32[2,5,2,16,128]{4,3,2,1,0:T(8,128)S(1)} collective-permute-done((f32[2,5,2,16,128]{4,3,2,1,0:T(8,128)S(1)}, f32[2,5,2,16,128]{4,3,2,1,0:T(8,128)S(1)}, u32[]{:S(2)}, u32[]{:S(2)}) %collective-permute-start.9) | collective-permute-done | bytes 163872 | tf_op jit(solution)/shard_map/ppermute | solution.py:247
  33.6 0.0 collective-permute-done.8.x2
  33.7 0.0 copy-done
  33.7 1.7 %shard_map.89 = (f32[2,3,2,16,128]{4,3,2,1,0:T(8,128)S(1)}, f32[2,3,2,16,128]{4,3,2,1,0:T(8,128)S(1)}, f32[2,3,2,16,128]{4,3,2,1,0:T(8,128)S(1)}, f32[2,3,2,16,128]{4,3,2,1,0:T(8,128)S(1)}) custom-call(f32[2,5,2,16,128]{4,3,2,1,0:T(8,128)S(1)} %collective-permute-done.6.x0, f32[2,5,2,16,128]{4,3,2,1,0:T(8,128)S(1)} %get-tuple-element.24.x1, ...), custom_call_target="tpu_custom_call" | custom-call | tf_op jit(solution)/shard_map/pallas_call | solution.py:322
  35.4 3.4 %collective-permute-start.10 = (f32[2,3,2,16,128]{4,3,2,1,0:T(8,128)S(1)}, f32[2,3,2,16,128]{4,3,2,1,0:T(8,128)S(1)}, u32[]{:S(2)}, u32[]{:S(2)}) collective-permute-start(f32[2,3,2,16,128]{4,3,2,1,0:T(8,128)S(1)} %get-tuple-element.15), channel_id=1, source_target_pairs={{0,4},{2,6},{4,0},{6,2},{1,5},{3,7},{5,1},{7,3},{8,12},{10,14},{12... | collective-permute-start | bytes 294920 | tf_op jit(solution)/shard_map/ppermute | solution.py:247
  38.8 0.9 %collective-permute-start.11 = (f32[2,3,2,16,128]{4,3,2,1,0:T(8,128)S(1)}, f32[2,3,2,16,128]{4,3,2,1,0:T(8,128)S(1)}, u32[]{:S(2)}, u32[]{:S(2)}) collective-permute-start(f32[2,3,2,16,128]{4,3,2,1,0:T(8,128)S(1)} %get-tuple-element.16), channel_id=1, source_target_pairs={{0,6},{2,0},{4,2},{6,4},{1,7},{3,1},{5,3},{7,5},{8,14},{10,8},{12,... | collective-permute-start | bytes 294920 | tf_op jit(solution)/shard_map/ppermute | solution.py:247
  39.8 0.6 collective-permute-start.12
  40.4 0.5 collective-permute-done.10
  40.8 2.9 %collective-permute-done.11 = f32[2,3,2,16,128]{4,3,2,1,0:T(8,128)S(1)} collective-permute-done((f32[2,3,2,16,128]{4,3,2,1,0:T(8,128)S(1)}, f32[2,3,2,16,128]{4,3,2,1,0:T(8,128)S(1)}, u32[]{:S(2)}, u32[]{:S(2)}) %collective-permute-start.11) | collective-permute-done | bytes 98336 | tf_op jit(solution)/shard_map/ppermute | solution.py:247
  43.7 0.7 %collective-permute-done.12 = f32[2,3,2,16,128]{4,3,2,1,0:T(8,128)S(1)} collective-permute-done((f32[2,3,2,16,128]{4,3,2,1,0:T(8,128)S(1)}, f32[2,3,2,16,128]{4,3,2,1,0:T(8,128)S(1)}, u32[]{:S(2)}, u32[]{:S(2)}) %collective-permute-start.12) | collective-permute-done | bytes 98336 | tf_op jit(solution)/shard_map/ppermute | solution.py:247
  44.5 0.2 shard_map.91
  44.6 2.5 %collective-permute-start.13 = (f32[4,2,3,16,128]{4,3,2,1,0:T(8,128)S(1)}, f32[4,2,3,16,128]{4,3,2,1,0:T(8,128)S(1)}, u32[]{:S(2)}, u32[]{:S(2)}) collective-permute-start(f32[4,2,3,16,128]{4,3,2,1,0:T(8,128)S(1)} %shard_map.91), channel_id=1, source_target_pairs={{0,1},{1,0},{2,3},{3,2},{4,5},{5,4},{6,7},{7,6},{8,9},{9,8},{10,11... | collective-permute-start | bytes 589832 | tf_op jit(solution)/shard_map/ppermute | solution.py:256
  47.2 0.1 shard_map.90
  47.3 0.9 %collective-permute-done.13 = f32[4,2,3,16,128]{4,3,2,1,0:T(8,128)S(1)} collective-permute-done((f32[4,2,3,16,128]{4,3,2,1,0:T(8,128)S(1)}, f32[4,2,3,16,128]{4,3,2,1,0:T(8,128)S(1)}, u32[]{:S(2)}, u32[]{:S(2)}) %collective-permute-start.13) | collective-permute-done | bytes 196640 | tf_op jit(solution)/shard_map/ppermute | solution.py:256
  48.3 3.8 %collective-permute-start.17 = (f32[2,3,16,128]{3,2,1,0:T(8,128)S(1)}, f32[2,3,16,128]{3,2,1,0:T(8,128)S(1)}, u32[]{:S(2)}, u32[]{:S(2)}) collective-permute-start(f32[2,3,16,128]{3,2,1,0:T(8,128)S(1)} %get-tuple-element.25), channel_id=1, source_target_pairs={{0,56},{8,0},{16,8},{24,16},{32,24},{40,32},{48,40},{56,48},{1,33}... | collective-permute-start | bytes 147464 | tf_op jit(solution)/shard_map/ppermute | solution.py:252
  52.1 0.7 %collective-permute-start.16 = (f32[2,3,16,128]{3,2,1,0:T(8,128)S(1)}, f32[2,3,16,128]{3,2,1,0:T(8,128)S(1)}, u32[]{:S(2)}, u32[]{:S(2)}) collective-permute-start(f32[2,3,16,128]{3,2,1,0:T(8,128)S(1)} %get-tuple-element.26), channel_id=1, source_target_pairs={{0,24},{8,32},{16,40},{24,48},{32,56},{40,0},{48,8},{56,16},{1,41}... | collective-permute-start | bytes 147464 | tf_op jit(solution)/shard_map/ppermute | solution.py:252
  52.8 2.4 %collective-permute-start.15 = (f32[2,3,16,128]{3,2,1,0:T(8,128)S(1)}, f32[2,3,16,128]{3,2,1,0:T(8,128)S(1)}, u32[]{:S(2)}, u32[]{:S(2)}) collective-permute-start(f32[2,3,16,128]{3,2,1,0:T(8,128)S(1)} %get-tuple-element.27), channel_id=1, source_target_pairs={{0,48},{8,56},{16,0},{24,8},{32,16},{40,24},{48,32},{56,40},{1,17}... | collective-permute-start | bytes 147464 | tf_op jit(solution)/shard_map/ppermute | solution.py:252
  55.2 2.7 %collective-permute-start.14 = (f32[2,3,16,128]{3,2,1,0:T(8,128)S(1)}, f32[2,3,16,128]{3,2,1,0:T(8,128)S(1)}, u32[]{:S(2)}, u32[]{:S(2)}) collective-permute-start(f32[2,3,16,128]{3,2,1,0:T(8,128)S(1)} %get-tuple-element.28), channel_id=1, source_target_pairs={{0,8},{8,16},{16,24},{24,32},{32,40},{40,48},{48,56},{56,0},{1,57}... | collective-permute-start | bytes 147464 | tf_op jit(solution)/shard_map/ppermute | solution.py:252
  57.9 0.0 collective-permute-done.17
  57.9 0.0 collective-permute-done.16.r2
  57.9 0.8 %collective-permute-done.15.r1 = f32[2,3,16,128]{3,2,1,0:T(8,128)S(1)} collective-permute-done((f32[2,3,16,128]{3,2,1,0:T(8,128)S(1)}, f32[2,3,16,128]{3,2,1,0:T(8,128)S(1)}, u32[]{:S(2)}, u32[]{:S(2)}) %collective-permute-start.15) | collective-permute-done | bytes 49184 | tf_op jit(solution)/shard_map/ppermute | solution.py:252
  58.7 0.9 %collective-permute-done.14.r0 = f32[2,3,16,128]{3,2,1,0:T(8,128)S(1)} collective-permute-done((f32[2,3,16,128]{3,2,1,0:T(8,128)S(1)}, f32[2,3,16,128]{3,2,1,0:T(8,128)S(1)}, u32[]{:S(2)}, u32[]{:S(2)}) %collective-permute-start.14) | collective-permute-done | bytes 49184 | tf_op jit(solution)/shard_map/ppermute | solution.py:252
  59.6 0.5 collective-permute-start.19
  60.1 0.2 collective-permute-start.18
  60.3 1.0 %collective-permute-done.18 = f32[16,128]{1,0:T(8,128)S(1)} collective-permute-done((f32[16,128]{1,0:T(8,128)S(1)}, f32[16,128]{1,0:T(8,128)S(1)}, u32[]{:S(2)}, u32[]{:S(2)}) %collective-permute-start.18) | collective-permute-done | bytes 8224 | tf_op jit(solution)/shard_map/ppermute | solution.py:256
  61.3 2.9 %collective-permute-start.22 = (f32[16,128]{1,0:T(8,128)S(1)}, f32[16,128]{1,0:T(8,128)S(1)}, u32[]{:S(2)}, u32[]{:S(2)}) collective-permute-start(f32[16,128]{1,0:T(8,128)S(1)} %add.147), channel_id=1, source_target_pairs={{0,128},{64,192},{128,0},{192,64},{1,129},{65,193},{129,1},{193,65... | collective-permute-start | bytes 24584 | tf_op jit(solution)/shard_map/ppermute | solution.py:260
  64.2 0.8 %collective-permute-start.21 = (f32[16,128]{1,0:T(8,128)S(1)}, f32[16,128]{1,0:T(8,128)S(1)}, u32[]{:S(2)}, u32[]{:S(2)}) collective-permute-start(f32[16,128]{1,0:T(8,128)S(1)} %add.147), channel_id=1, source_target_pairs={{0,192},{64,128},{128,64},{192,0},{1,193},{65,129},{129,65},{193,1... | collective-permute-start | bytes 24584 | tf_op jit(solution)/shard_map/ppermute | solution.py:260
  65.0 0.0 collective-permute-start.20
  65.0 0.0 collective-permute-done.19.other_ref
  65.0 0.0 copy-done.1
  65.0 0.6 shard_map.93
  65.6 0.7 reshape.33
  66.3 0.0 collective-permute-done.22
  66.3 1.7 %collective-permute-done.21 = f32[16,128]{1,0:T(8,128)S(1)} collective-permute-done((f32[16,128]{1,0:T(8,128)S(1)}, f32[16,128]{1,0:T(8,128)S(1)}, u32[]{:S(2)}, u32[]{:S(2)}) %collective-permute-start.21) | collective-permute-done | bytes 8224 | tf_op jit(solution)/shard_map/ppermute | solution.py:260
  67.9 0.0 collective-permute-done.20
  67.9 0.6 add_bitcast_fusion
  (25 shorter events, 0.3 us)
Async XLA Ops:
  1.7 31.9 %copy-start = (bf16[4,256,256]{2,1,0:T(8,128)(2,1)S(1)}, bf16[4,256,256]{2,1,0:T(8,128)(2,1)}, u32[]{:S(2)}) copy-start(bf16[4,256,256]{2,1,0:T(8,128)(2,1)} %constant.61.clone.right) | copy-start | bytes 1572868
  1.8 4.4 %collective-permute-start = (f32[4,5,16,128]{3,2,1,0:T(8,128)S(1)}, f32[4,5,16,128]{3,2,1,0:T(8,128)S(1)}, u32[]{:S(2)}, u32[]{:S(2)}) collective-permute-start(f32[4,5,16,128]{3,2,1,0:T(8,128)S(1)} %pad_maximum_fusion.2), channel_id=1, source_target_pairs={{0,1},{1,0},{2,3},{3,2},{4,5},{5,4},{6,7},{7,6},{8,9},{9,8},{10,11... | collective-permute-start | bytes 491528 | tf_op jit(solution)/shard_map/ppermute | solution.py:256
  6.2 9.3 %collective-permute-start.4 = (f32[2,5,16,128]{3,2,1,0:T(8,128)S(1)}, f32[2,5,16,128]{3,2,1,0:T(8,128)S(1)}, u32[]{:S(2)}, u32[]{:S(2)}) collective-permute-start(f32[2,5,16,128]{3,2,1,0:T(8,128)S(1)} %pad_maximum_fusion.6), channel_id=1, source_target_pairs={{0,56},{8,0},{16,8},{24,16},{32,24},{40,32},{48,40},{56,48},{1,33}... | collective-permute-start | bytes 245768 | tf_op jit(solution)/shard_map/ppermute | solution.py:252
  11.4 5.2 %collective-permute-start.1 = (f32[2,5,16,128]{3,2,1,0:T(8,128)S(1)}, f32[2,5,16,128]{3,2,1,0:T(8,128)S(1)}, u32[]{:S(2)}, u32[]{:S(2)}) collective-permute-start(f32[2,5,16,128]{3,2,1,0:T(8,128)S(1)} %pad_maximum_fusion.3), channel_id=1, source_target_pairs={{0,24},{8,32},{16,40},{24,48},{32,56},{40,0},{48,8},{56,16},{1,41}... | collective-permute-start | bytes 245768 | tf_op jit(solution)/shard_map/ppermute | solution.py:252
  11.5 9.0 %collective-permute-start.2 = (f32[2,5,16,128]{3,2,1,0:T(8,128)S(1)}, f32[2,5,16,128]{3,2,1,0:T(8,128)S(1)}, u32[]{:S(2)}, u32[]{:S(2)}) collective-permute-start(f32[2,5,16,128]{3,2,1,0:T(8,128)S(1)} %pad_maximum_fusion.4), channel_id=1, source_target_pairs={{0,8},{8,16},{16,24},{24,32},{32,40},{40,48},{48,56},{56,0},{1,57}... | collective-permute-start | bytes 245768 | tf_op jit(solution)/shard_map/ppermute | solution.py:252
  11.9 8.5 %collective-permute-start.3 = (f32[2,5,16,128]{3,2,1,0:T(8,128)S(1)}, f32[2,5,16,128]{3,2,1,0:T(8,128)S(1)}, u32[]{:S(2)}, u32[]{:S(2)}) collective-permute-start(f32[2,5,16,128]{3,2,1,0:T(8,128)S(1)} %pad_maximum_fusion.5), channel_id=1, source_target_pairs={{0,48},{8,56},{16,0},{24,8},{32,16},{40,24},{48,32},{56,40},{1,17}... | collective-permute-start | bytes 245768 | tf_op jit(solution)/shard_map/ppermute | solution.py:252
  20.7 5.1 %collective-permute-start.7 = (f32[3,2,5,2,16,128]{5,4,3,2,1,0:T(8,128)S(1)}, f32[3,2,5,2,16,128]{5,4,3,2,1,0:T(8,128)S(1)}, u32[]{:S(2)}, u32[]{:S(2)}) collective-permute-start(f32[3,2,5,2,16,128]{5,4,3,2,1,0:T(8,128)S(1)} %slice.139), channel_id=1, source_target_pairs={{0,1},{1,0},{2,3},{3,2},{4,5},{5,4},{6,7},{7,6},{8,9},{9,8},{10,11... | collective-permute-start | bytes 1474568 | tf_op jit(solution)/shard_map/ppermute | solution.py:256
  21.3 1.7 %collective-permute-start.5 = (f32[2,5,2,16,128]{4,3,2,1,0:T(8,128)S(1)}, f32[2,5,2,16,128]{4,3,2,1,0:T(8,128)S(1)}, u32[]{:S(2)}, u32[]{:S(2)}) collective-permute-start(f32[2,5,2,16,128]{4,3,2,1,0:T(8,128)S(1)} %slice_bitcast_fusion), channel_id=1, source_target_pairs={{0,1},{1,0},{2,3},{3,2},{4,5},{5,4},{6,7},{7,6},{8,9},{9,8},{10,11... | collective-permute-start | bytes 491528 | tf_op jit(solution)/shard_map/ppermute | solution.py:256
  23.0 42.0 %copy-start.1 = (f32[16]{0:T(128)S(1)}, f32[16]{0:T(128)}, u32[]{:S(2)}) copy-start(f32[16]{0:T(128)} %skip_ref.1) | copy-start | bytes 196
  23.0 7.0 %collective-permute-start.6 = (f32[2,5,2,16,128]{4,3,2,1,0:T(8,128)S(1)}, f32[2,5,2,16,128]{4,3,2,1,0:T(8,128)S(1)}, u32[]{:S(2)}, u32[]{:S(2)}) collective-permute-start(f32[2,5,2,16,128]{4,3,2,1,0:T(8,128)S(1)} %fusion.3), channel_id=1, source_target_pairs={{0,4},{2,6},{4,0},{6,2},{1,5},{3,7},{5,1},{7,3},{8,12},{10,14},{12... | collective-permute-start | bytes 491528 | tf_op jit(solution)/shard_map/ppermute | solution.py:247
  25.9 7.7 %collective-permute-start.9 = (f32[2,5,2,16,128]{4,3,2,1,0:T(8,128)S(1)}, f32[2,5,2,16,128]{4,3,2,1,0:T(8,128)S(1)}, u32[]{:S(2)}, u32[]{:S(2)}) collective-permute-start(f32[2,5,2,16,128]{4,3,2,1,0:T(8,128)S(1)} %get-tuple-element.12), channel_id=1, source_target_pairs={{0,6},{2,0},{4,2},{6,4},{1,7},{3,1},{5,3},{7,5},{8,14},{10,8},{12,... | collective-permute-start | bytes 491528 | tf_op jit(solution)/shard_map/ppermute | solution.py:247
  26.9 6.8 %collective-permute-start.8 = (f32[2,5,2,16,128]{4,3,2,1,0:T(8,128)S(1)}, f32[2,5,2,16,128]{4,3,2,1,0:T(8,128)S(1)}, u32[]{:S(2)}, u32[]{:S(2)}) collective-permute-start(f32[2,5,2,16,128]{4,3,2,1,0:T(8,128)S(1)} %get-tuple-element.23), channel_id=1, source_target_pairs={{0,2},{2,4},{4,6},{6,0},{1,3},{3,5},{5,7},{7,1},{8,10},{10,12},{12... | collective-permute-start | bytes 491528 | tf_op jit(solution)/shard_map/ppermute | solution.py:247
  35.4 5.4 %collective-permute-start.10 = (f32[2,3,2,16,128]{4,3,2,1,0:T(8,128)S(1)}, f32[2,3,2,16,128]{4,3,2,1,0:T(8,128)S(1)}, u32[]{:S(2)}, u32[]{:S(2)}) collective-permute-start(f32[2,3,2,16,128]{4,3,2,1,0:T(8,128)S(1)} %get-tuple-element.15), channel_id=1, source_target_pairs={{0,4},{2,6},{4,0},{6,2},{1,5},{3,7},{5,1},{7,3},{8,12},{10,14},{12... | collective-permute-start | bytes 294920 | tf_op jit(solution)/shard_map/ppermute | solution.py:247
  38.8 4.9 %collective-permute-start.11 = (f32[2,3,2,16,128]{4,3,2,1,0:T(8,128)S(1)}, f32[2,3,2,16,128]{4,3,2,1,0:T(8,128)S(1)}, u32[]{:S(2)}, u32[]{:S(2)}) collective-permute-start(f32[2,3,2,16,128]{4,3,2,1,0:T(8,128)S(1)} %get-tuple-element.16), channel_id=1, source_target_pairs={{0,6},{2,0},{4,2},{6,4},{1,7},{3,1},{5,3},{7,5},{8,14},{10,8},{12,... | collective-permute-start | bytes 294920 | tf_op jit(solution)/shard_map/ppermute | solution.py:247
  39.8 4.7 %collective-permute-start.12 = (f32[2,3,2,16,128]{4,3,2,1,0:T(8,128)S(1)}, f32[2,3,2,16,128]{4,3,2,1,0:T(8,128)S(1)}, u32[]{:S(2)}, u32[]{:S(2)}) collective-permute-start(f32[2,3,2,16,128]{4,3,2,1,0:T(8,128)S(1)} %get-tuple-element.17), channel_id=1, source_target_pairs={{0,2},{2,4},{4,6},{6,0},{1,3},{3,5},{5,7},{7,1},{8,10},{10,12},{12... | collective-permute-start | bytes 294920 | tf_op jit(solution)/shard_map/ppermute | solution.py:247
  44.6 3.6 %collective-permute-start.13 = (f32[4,2,3,16,128]{4,3,2,1,0:T(8,128)S(1)}, f32[4,2,3,16,128]{4,3,2,1,0:T(8,128)S(1)}, u32[]{:S(2)}, u32[]{:S(2)}) collective-permute-start(f32[4,2,3,16,128]{4,3,2,1,0:T(8,128)S(1)} %shard_map.91), channel_id=1, source_target_pairs={{0,1},{1,0},{2,3},{3,2},{4,5},{5,4},{6,7},{7,6},{8,9},{9,8},{10,11... | collective-permute-start | bytes 589832 | tf_op jit(solution)/shard_map/ppermute | solution.py:256
  48.3 9.6 %collective-permute-start.17 = (f32[2,3,16,128]{3,2,1,0:T(8,128)S(1)}, f32[2,3,16,128]{3,2,1,0:T(8,128)S(1)}, u32[]{:S(2)}, u32[]{:S(2)}) collective-permute-start(f32[2,3,16,128]{3,2,1,0:T(8,128)S(1)} %get-tuple-element.25), channel_id=1, source_target_pairs={{0,56},{8,0},{16,8},{24,16},{32,24},{40,32},{48,40},{56,48},{1,33}... | collective-permute-start | bytes 147464 | tf_op jit(solution)/shard_map/ppermute | solution.py:252
  52.1 5.8 %collective-permute-start.16 = (f32[2,3,16,128]{3,2,1,0:T(8,128)S(1)}, f32[2,3,16,128]{3,2,1,0:T(8,128)S(1)}, u32[]{:S(2)}, u32[]{:S(2)}) collective-permute-start(f32[2,3,16,128]{3,2,1,0:T(8,128)S(1)} %get-tuple-element.26), channel_id=1, source_target_pairs={{0,24},{8,32},{16,40},{24,48},{32,56},{40,0},{48,8},{56,16},{1,41}... | collective-permute-start | bytes 147464 | tf_op jit(solution)/shard_map/ppermute | solution.py:252
  52.8 5.9 %collective-permute-start.15 = (f32[2,3,16,128]{3,2,1,0:T(8,128)S(1)}, f32[2,3,16,128]{3,2,1,0:T(8,128)S(1)}, u32[]{:S(2)}, u32[]{:S(2)}) collective-permute-start(f32[2,3,16,128]{3,2,1,0:T(8,128)S(1)} %get-tuple-element.27), channel_id=1, source_target_pairs={{0,48},{8,56},{16,0},{24,8},{32,16},{40,24},{48,32},{56,40},{1,17}... | collective-permute-start | bytes 147464 | tf_op jit(solution)/shard_map/ppermute | solution.py:252
  55.2 4.4 %collective-permute-start.14 = (f32[2,3,16,128]{3,2,1,0:T(8,128)S(1)}, f32[2,3,16,128]{3,2,1,0:T(8,128)S(1)}, u32[]{:S(2)}, u32[]{:S(2)}) collective-permute-start(f32[2,3,16,128]{3,2,1,0:T(8,128)S(1)} %get-tuple-element.28), channel_id=1, source_target_pairs={{0,8},{8,16},{16,24},{24,32},{32,40},{40,48},{48,56},{56,0},{1,57}... | collective-permute-start | bytes 147464 | tf_op jit(solution)/shard_map/ppermute | solution.py:252
  59.6 5.4 %collective-permute-start.19 = (f32[4,2,16,128]{3,2,1,0:T(8,128)S(1)}, f32[4,2,16,128]{3,2,1,0:T(8,128)S(1)}, u32[]{:S(2)}, u32[]{:S(2)}) collective-permute-start(f32[4,2,16,128]{3,2,1,0:T(8,128)S(1)} %pad_maximum_fusion.7), channel_id=1, source_target_pairs={{0,1},{1,0},{2,3},{3,2},{4,5},{5,4},{6,7},{7,6},{8,9},{9,8},{10,11... | collective-permute-start | bytes 196616 | tf_op jit(solution)/shard_map/ppermute | solution.py:256
  60.1 1.2 %collective-permute-start.18 = (f32[16,128]{1,0:T(8,128)S(1)}, f32[16,128]{1,0:T(8,128)S(1)}, u32[]{:S(2)}, u32[]{:S(2)}) collective-permute-start(f32[16,128]{1,0:T(8,128)S(1)} %get-tuple-element.19), channel_id=1, source_target_pairs={{0,1},{1,0},{2,3},{3,2},{4,5},{5,4},{6,7},{7,6},{8,9},{9,8},{10,11... | collective-permute-start | bytes 24584 | tf_op jit(solution)/shard_map/ppermute | solution.py:256
  61.3 5.0 %collective-permute-start.22 = (f32[16,128]{1,0:T(8,128)S(1)}, f32[16,128]{1,0:T(8,128)S(1)}, u32[]{:S(2)}, u32[]{:S(2)}) collective-permute-start(f32[16,128]{1,0:T(8,128)S(1)} %add.147), channel_id=1, source_target_pairs={{0,128},{64,192},{128,0},{192,64},{1,129},{65,193},{129,1},{193,65... | collective-permute-start | bytes 24584 | tf_op jit(solution)/shard_map/ppermute | solution.py:260
  64.2 3.7 %collective-permute-start.21 = (f32[16,128]{1,0:T(8,128)S(1)}, f32[16,128]{1,0:T(8,128)S(1)}, u32[]{:S(2)}, u32[]{:S(2)}) collective-permute-start(f32[16,128]{1,0:T(8,128)S(1)} %add.147), channel_id=1, source_target_pairs={{0,192},{64,128},{128,64},{192,0},{1,193},{65,129},{129,65},{193,1... | collective-permute-start | bytes 24584 | tf_op jit(solution)/shard_map/ppermute | solution.py:260
  65.0 2.9 %collective-permute-start.20 = (f32[16,128]{1,0:T(8,128)S(1)}, f32[16,128]{1,0:T(8,128)S(1)}, u32[]{:S(2)}, u32[]{:S(2)}) collective-permute-start(f32[16,128]{1,0:T(8,128)S(1)} %add.147), channel_id=1, source_target_pairs={{0,64},{64,0},{128,192},{192,128},{1,65},{65,1},{129,193},{193,129... | collective-permute-start | bytes 24584 | tf_op jit(solution)/shard_map/ppermute | solution.py:260
